TPU v7x, 768 devices: a whole 4x8x12 slice. The times are simulated.
768 devices in a mesh: dp: 48 (over x, z), fsdp: 16 (over y, core).
Axes of the slice: x: 4, y: 8, z: 12, core: 2. Of those that a mesh axis runs over, the one named last changes fastest.
Arguments:
- train_x: bfloat16 [12288, 4096], P('dp', 'fsdp'), may hold values from -0.75 to 0.75
- train_attn: bfloat16 [12288, 4096], P('dp', 'fsdp'), may hold values from -0.75 to 0.75
- train_gqkv: bfloat16 [12288, 6144], P('dp', 'fsdp'), may hold values from -0.65625 to 0.65625
- train_go: bfloat16 [12288, 4096], P('dp', 'fsdp'), may hold values from -0.65625 to 0.65625
- train_lengths: int32 [48, 4], P('dp'), may hold values from 1 to 128, 256 in all within a row
- val_x: bfloat16 [48, 32, 4096], P('dp', None, 'fsdp'), may hold values from -0.75 to 0.75
- val_attn: bfloat16 [48, 32, 4096], P('dp', None, 'fsdp'), may hold values from -0.75 to 0.75
- val_gqkv: bfloat16 [48, 32, 6144], P('dp', None, 'fsdp'), may hold values from -0.65625 to 0.65625
- val_go: bfloat16 [48, 32, 4096], P('dp', None, 'fsdp'), may hold values from -0.65625 to 0.65625
- val_lengths: int32 [48], replicated, may hold values from 1 to 32, 1152 in all
Outputs:
- scores: float32 [192, 48], P('dp', 'fsdp')
Inputs may be any that keep to these rules, and one draw needn't show every extreme that they name: `train_lengths`: each row sums to 256; its sequences fill that index's token rows in order; the longest of all is 128. `val_lengths`: the valid positions of a sequence are its first ones; all sum to 1152; the longest is 32.
All inputs are finite; a program needn't handle non-finite values.
Results may differ from a plain program's by a relative error of at most 0.0003.
Values may be sent and summed in bfloat16 or wider, within the bound.
No kernel may reach another device: no remote copies, remote signals or barrier semaphores. Data moves between devices by JAX's collectives and lax.ppermute only.
A program may use at most 32 MiB of HBM per device.

v0:
```python
import jax
import jax.numpy as jnp
from jax import lax
from jax.sharding import PartitionSpec as P

score_scale = 0.015625


def memberships(train_lengths, token_count):
    lengths_row = train_lengths[0]
    seq_ends = jnp.cumsum(lengths_row)
    seq_starts = seq_ends - lengths_row
    places = jnp.arange(token_count, dtype=jnp.int32)[:, None]
    return ((places >= seq_starts[None, :]) & (places < seq_ends[None, :])).astype(jnp.float32)


def reduce_terms(gram_x, gram_attn, gram_q, gram_o, lengths_part, first_place, members):
    extent = gram_x.shape[1]
    places = first_place + jnp.arange(extent, dtype=jnp.int32)
    val_mask = (places[None, :] < lengths_part[:, None]).astype(jnp.float32)
    contrib = gram_x * gram_q + gram_attn * gram_o
    per_token = jnp.einsum("mnt,mn->mt", contrib, val_mask, precision=lax.Precision.HIGHEST)
    return jnp.dot(per_token, members, precision=lax.Precision.HIGHEST)


def local(
    train_x,
    train_attn,
    train_gqkv,
    train_go,
    train_lengths,
    val_x,
    val_attn,
    val_gqkv,
    val_go,
    val_lengths,
):
    members = memberships(train_lengths, train_x.shape[0])
    col_x, col_attn, col_q, col_o = (
        lax.all_to_all(val_x, "fsdp", split_axis=1, concat_axis=2, tiled=True),
        lax.all_to_all(val_attn, "fsdp", split_axis=1, concat_axis=2, tiled=True),
        lax.all_to_all(val_gqkv, "fsdp", split_axis=1, concat_axis=2, tiled=True),
        lax.all_to_all(val_go, "fsdp", split_axis=1, concat_axis=2, tiled=True),
    )
    full_x, full_attn, full_q, full_o = (
        lax.all_gather(train_x, "fsdp", axis=1, tiled=True),
        lax.all_gather(train_attn, "fsdp", axis=1, tiled=True),
        lax.all_gather(train_gqkv, "fsdp", axis=1, tiled=True),
        lax.all_gather(train_go, "fsdp", axis=1, tiled=True),
    )
    first_place = lax.axis_index("fsdp") * col_x.shape[1]
    part_x, part_attn, part_q, part_o = lax.all_gather(
        (col_x, col_attn, col_q, col_o), "dp", axis=0, tiled=True
    )
    gram_x = jnp.einsum("td,mnd->mnt", full_x, part_x, preferred_element_type=jnp.float32)
    gram_attn = jnp.einsum("td,mnd->mnt", full_attn, part_attn, preferred_element_type=jnp.float32)
    gram_q = jnp.einsum("tc,mnc->mnt", full_q, part_q, preferred_element_type=jnp.float32)
    gram_o = jnp.einsum("tc,mnc->mnt", full_o, part_o, preferred_element_type=jnp.float32)
    partial_value = reduce_terms(
        gram_x, gram_attn, gram_q, gram_o, val_lengths, first_place, members
    )
    scores = lax.psum_scatter(partial_value, "fsdp", scatter_dimension=0, tiled=True)
    return scores.T * score_scale


def solution(mesh):
    in_specs = (
        P("dp", "fsdp"),
        P("dp", "fsdp"),
        P("dp", "fsdp"),
        P("dp", "fsdp"),
        P("dp", None),
        P("dp", None, "fsdp"),
        P("dp", None, "fsdp"),
        P("dp", None, "fsdp"),
        P("dp", None, "fsdp"),
        P(),
    )
    out_specs = P("dp", "fsdp")
    return jax.shard_map(local, mesh=mesh, in_specs=in_specs, out_specs=out_specs, check_vma=False)
```

profile of v0, /device:TPU:1, one launch (start us, length us, event | category | flops | bytes accessed | tf_op | source)
XLA Modules:
  0.0 377.6 jit_solution(8314549360847282280)
XLA Ops:
  6.5 0.0 all-gather.14.cloned.1.call-start
  6.5 0.7 all-gather.14.cloned.1.call-update
  7.3 0.0 all-gather.12.cloned.1.call-start
  7.3 0.7 all-gather.12.cloned.1.call-update
  8.0 0.0 all-gather.8.cloned.1.call-start
  8.1 0.8 copy.53
  8.8 0.5 broadcast.16
  9.3 0.8 reduce.10
  10.1 20.4 %all_to_all.72 = bf16[16,2,384]{2,1,0:T(2,128)(2,1)S(1)} all-to-all(bf16[16,2,384]{2,1,0:T(2,128)(2,1)S(1)} %reshape.32), channel_id=1, replica_groups=mesh['dp'=48,'fsdp'=16] {'fsdp'}, dimensions={0} | all-to-all | bytes 49152 | tf_op jit(solution)/shard_map/all_to_all | solution.py:42
  30.6 0.1 bitcast_reduce_fusion
  30.7 0.6 all_to_all.57
  31.3 0.0 all-gather.8.cloned.1.call-update
  31.3 0.0 all-gather.10.cloned.1.call-start
  31.4 0.5 all-gather.10.cloned.1.call-update
  31.9 0.0 all-gather.6.cloned.1.call-start
  32.0 0.5 all-gather.6.cloned.1.call-update
  32.5 0.7 copy.54
  33.2 0.7 reduce.8
  34.0 0.6 reshape.28
  34.6 3.6 all-to-all-start.3
  38.2 0.7 compare_bitcast_fusion
  39.0 0.7 copy.55
  39.7 0.7 reduce.9
  40.4 0.6 reshape.30
  41.1 0.8 reduce-window.4
  41.9 3.7 all-to-all-done.3
  45.6 3.6 all-to-all-start.2
  49.2 0.7 fusion.32
  49.9 0.7 copy.56
  50.6 0.7 reduce.11
  51.4 0.6 reshape.34
  52.0 1.3 dynamic-slice
  53.9 2.7 all-to-all-done.2
  56.7 4.6 %all-to-all-start = ((bf16[16,2,256]{2,1,0:T(2,128)(2,1)}), bf16[16,2,256]{2,1,0:T(2,128)(2,1)S(1)}, u32[]{:S(2)}, u32[]{:S(2)}) async-start(bf16[16,2,256]{2,1,0:T(2,128)(2,1)} %reshape.34), calls=%async_computation | async-start | bytes 32768 | tf_op jit(solution)/shard_map/all_to_all | solution.py:40
  61.2 0.1 bitcast_reduce_fusion.3
  61.3 0.1 bitcast_reduce_fusion.2
  61.5 7.1 %all-to-all-done = bf16[16,2,256]{2,1,0:T(2,128)(2,1)S(1)} async-done(((bf16[16,2,256]{2,1,0:T(2,128)(2,1)}), bf16[16,2,256]{2,1,0:T(2,128)(2,1)S(1)}, u32[]{:S(2)}, u32[]{:S(2)}) %all-to-all-start) | async-done | bytes 16416 | tf_op jit(solution)/shard_map/all_to_all | solution.py:40
  68.6 0.1 bitcast_reduce_fusion.1
  68.7 62.4 %all_gather.30 = bf16[48,2,4096]{2,1,0:T(2,128)(2,1)S(1)} all-gather(bf16[1,2,4096]{2,1,0:T(2,128)(2,1)S(1)} %bitcast.71), channel_id=1, replica_groups=mesh['dp'=48,'fsdp'=16] {'dp'}, dimensions={0}, use_global_device_ids=true | all-gather | bytes 802816 | tf_op jit(solution)/shard_map/all_gather | solution.py:52
  131.1 58.1 %all_gather.28 = bf16[48,2,4096]{2,1,0:T(2,128)(2,1)S(1)} all-gather(bf16[1,2,4096]{2,1,0:T(2,128)(2,1)S(1)} %bitcast.72), channel_id=1, replica_groups=mesh['dp'=48,'fsdp'=16] {'dp'}, dimensions={0}, use_global_device_ids=true | all-gather | bytes 802816 | tf_op jit(solution)/shard_map/all_gather | solution.py:52
  189.2 56.7 %all_gather.24 = bf16[48,2,4096]{2,1,0:T(2,128)(2,1)S(1)} all-gather(bf16[1,2,4096]{2,1,0:T(2,128)(2,1)S(1)} %bitcast.73), channel_id=1, replica_groups=mesh['dp'=48,'fsdp'=16] {'dp'}, dimensions={0}, use_global_device_ids=true | all-gather | bytes 802816 | tf_op jit(solution)/shard_map/all_gather | solution.py:52
  245.8 0.0 all-gather.14.cloned.1.call-done
  245.8 2.6 fusion.2
  248.4 0.0 all-gather.12.cloned.1.call-done
  248.4 2.6 fusion.15
  251.0 0.0 all-gather.8.cloned.1.call-done
  251.0 24.4 %all-gather.10.cloned.1.call-done = bf16[256,6144]{1,0:T(8,128)(2,1)} async-done(((bf16[256,384]{1,0:T(8,128)(2,1)}), bf16[256,6144]{1,0:T(8,128)(2,1)}) %all-gather.10.cloned.1.call-update) | async-done | bytes 3145744 | tf_op jit(solution)/shard_map/all_gather | solution.py:48
  275.4 3.4 fusion
  278.8 43.7 %all-gather.6.cloned.1.call-done = bf16[256,4096]{1,0:T(8,128)(2,1)} async-done(((bf16[256,256]{1,0:T(8,128)(2,1)}), bf16[256,4096]{1,0:T(8,128)(2,1)}) %all-gather.6.cloned.1.call-update) | async-done | bytes 2097168 | tf_op jit(solution)/shard_map/all_gather | solution.py:46
  322.5 2.6 fusion.12
  325.1 0.4 fusion.24
  325.5 0.2 fusion.22
  325.7 44.8 %all-reduce = f32[48,4]{1,0:T(8,128)S(1)} all-reduce(f32[48,4]{1,0:T(8,128)S(1)} %fusion.22), channel_id=2, replica_groups=mesh['dp'=48,'fsdp'=16] {'fsdp'}, use_global_device_ids=true, to_apply=%region_1.2.clone | all-reduce | flops 192 | bytes 1536
  370.5 0.7 copy.25
  (10 shorter events, 0.1 us)
Async XLA Ops:
  6.5 239.3 %all-gather.14.cloned.1.call-start = ((), (), s32[]{:S(2)}) async-start(), calls=%async_computation.8 | async-start | bytes 2228224 | tf_op jit(solution)/shard_map/all_gather | solution.py:49
  7.3 241.2 %all-gather.12.cloned.1.call-start = ((), (), s32[]{:S(2)}) async-start(), calls=%async_computation.7 | async-start | bytes 2228224 | tf_op jit(solution)/shard_map/all_gather | solution.py:47
  8.0 243.0 %all-gather.8.cloned.1.call-start = ((), (), s32[]{:S(2)}) async-start(), calls=%async_computation.5 | async-start | bytes 1204224 | tf_op jit(solution)/shard_map/all_gather | solution.py:52
  31.3 244.1 %all-gather.10.cloned.1.call-start = ((), (), s32[]{:S(2)}) async-start(), calls=%async_computation.6 | async-start | bytes 3342336 | tf_op jit(solution)/shard_map/all_gather | solution.py:48
  31.9 290.6 %all-gather.6.cloned.1.call-start = ((), (), s32[]{:S(2)}) async-start(), calls=%async_computation.4 | async-start | bytes 2228224 | tf_op jit(solution)/shard_map/all_gather | solution.py:46
  34.6 11.0 %all-to-all-start.3 = ((bf16[16,2,256]{2,1,0:T(2,128)(2,1)}), bf16[16,2,256]{2,1,0:T(2,128)(2,1)S(1)}, u32[]{:S(2)}, u32[]{:S(2)}) async-start(bf16[16,2,256]{2,1,0:T(2,128)(2,1)} %reshape.28), calls=%async_computation.3 | async-start | bytes 32768 | tf_op jit(solution)/shard_map/all_to_all | solution.py:43
  45.6 11.0 %all-to-all-start.2 = ((bf16[16,2,256]{2,1,0:T(2,128)(2,1)}), bf16[16,2,256]{2,1,0:T(2,128)(2,1)S(1)}, u32[]{:S(2)}, u32[]{:S(2)}) async-start(bf16[16,2,256]{2,1,0:T(2,128)(2,1)} %reshape.30), calls=%async_computation.2 | async-start | bytes 32768 | tf_op jit(solution)/shard_map/all_to_all | solution.py:41
  56.7 11.9 %all-to-all-start = ((bf16[16,2,256]{2,1,0:T(2,128)(2,1)}), bf16[16,2,256]{2,1,0:T(2,128)(2,1)S(1)}, u32[]{:S(2)}, u32[]{:S(2)}) async-start(bf16[16,2,256]{2,1,0:T(2,128)(2,1)} %reshape.34), calls=%async_computation | async-start | bytes 32768 | tf_op jit(solution)/shard_map/all_to_all | solution.py:40
Sparse Core Ops, SparseCore 0:
  9.7 54.4 all-gather.13
  66.5 45.2 all-gather.11
  115.5 107.7 all-gather.7
  225.5 49.9 all-gather.9
  277.6 44.8 all-gather.5
where the time goes:
time: 381 us; the launch traced here: 378 us
  blocking collectives  242 us (64%)
  waiting for transfers between devices  84.2 us (22%)
  between operations  13.9 us (4%)
  starting transfers between devices  11.9 us (3%)
  matrix products  11.6 us (3%)
  local copies, waits for them, and re-layouts  8.49 us (2%)
  other arithmetic  5.21 us (1%)
    all_gather x3, blocking collectives, local(): lax.all_gather((col_x, col_attn, col_q, col_o), 'dp', axis=0, tiled=True)  177 us
    unnamed x1, blocking collectives  44.8 us
    all_gather x1, waiting for transfers between devices, local(): lax.all_gather(train_x, 'fsdp', axis=1, tiled=True)  43.7 us
    all_gather x1, waiting for transfers between devices, local(): lax.all_gather(train_gqkv, 'fsdp', axis=1, tiled=True)  24.4 us
    all_to_all x1, blocking collectives, local(): lax.all_to_all(val_gqkv, 'fsdp', split_axis=1, concat_axis=2, tiled=True)  20.4 us
  transfers between devices with their start and end apart: 8, of which 5 were waited for; matrix products, arithmetic and copies ran while one was open for 6% of the time, Pallas kernels for 0%

commit v1 on v0

v1 whole, which is shorter than its diff:
```python
import numpy as np
import jax
import jax.numpy as jnp
from jax import lax
from jax.experimental import pallas as pl
from jax.experimental.pallas import tpu as pltpu
from jax.sharding import Mesh, PartitionSpec as P

score_scale = 0.015625

NX, NZ, NY, NC = 4, 12, 8, 2
TOK, VLEN = 256, 32
SEQS = 6
ROWS = SEQS * VLEN
HALF = ROWS // 2
COLS = ((0, 256), (256, 512), (512, 896), (896, 1152))
WIDTH = 1152

SWAP = [
    ((6 * a + r) * NY + b, (6 * b + r) * NY + a)
    for a in range(NY)
    for b in range(NY)
    for r in range(SEQS)
]


def around(size, shift):
    return [(i, (i + shift) % size) for i in range(size)]


def gram_kernel(train, own, right, left, far, out, tbuf, vbuf, sems):
    x = lax.axis_index("x")
    copies = [pltpu.make_async_copy(train, tbuf, sems.at[0])]
    for k, (ref, shift) in enumerate(((own, 0), (right, 1), (left, 3), (far, 2))):
        at = lax.rem(x + shift, NX)
        copies.append(pltpu.make_async_copy(ref, vbuf.at[at], sems.at[k + 1]))
    for c in copies:
        c.start()
    for c in copies:
        c.wait()
    for g, (lo, hi) in enumerate(COLS):
        acc = jnp.zeros((ROWS, TOK), jnp.float32)
        for b in range(NY):
            v = vbuf[b // 2, (b % 2) * ROWS : (b % 2 + 1) * ROWS, lo:hi]
            t = tbuf[b, :, lo:hi]
            acc += lax.dot_general(
                v, t, (((1,), (1,)), ((), ())), preferred_element_type=jnp.float32
            )
        out[0, g] = acc[:HALF]
        out[1, g] = acc[HALF:]


def grams(train, own, right, left, far):
    any_spec = pl.BlockSpec(memory_space=pl.ANY)
    return pl.pallas_call(
        gram_kernel,
        out_shape=jax.ShapeDtypeStruct((2, 4, HALF, TOK), jnp.float32),
        in_specs=[any_spec] * 5,
        out_specs=pl.BlockSpec(memory_space=pltpu.VMEM),
        scratch_shapes=[
            pltpu.VMEM((NY, TOK, WIDTH), jnp.bfloat16),
            pltpu.VMEM((NX, 2 * ROWS, WIDTH), jnp.bfloat16),
            pltpu.SemaphoreType.DMA((5,)),
        ],
        compiler_params=pltpu.CompilerParams(vmem_limit_bytes=32 * 1024 * 1024),
    )(train, own, right, left, far)


def score_kernel(tl, vl, mine, other, out):
    first = 3 * (2 * lax.axis_index("y") + lax.axis_index("core"))
    g = mine[...] + other[...]
    contrib = g[0] * g[2] + g[1] * g[3]
    places = lax.broadcasted_iota(jnp.int32, (VLEN, TOK), 0)
    tokens = lax.broadcasted_iota(jnp.int32, (1, TOK), 1)
    rows = lax.broadcasted_iota(jnp.int32, (4, 3), 0)
    cols = lax.broadcasted_iota(jnp.int32, (4, 3), 1)
    result = jnp.zeros((4, 3), jnp.float32)
    for s in range(3):
        block = contrib[s * VLEN : (s + 1) * VLEN]
        per_token = jnp.sum(
            jnp.where(places < vl[first + s], block, 0.0), axis=0, keepdims=True
        )
        start = jnp.int32(0)
        for k in range(4):
            end = start + tl[0, k]
            inside = (tokens >= start) & (tokens < end)
            total = jnp.sum(
                jnp.where(inside, per_token, 0.0), axis=1, keepdims=True
            )
            result = jnp.where((rows == k) & (cols == s), total, result)
            start = end
    out[...] = result * score_scale


def scores_of(tl, vl, mine, other):
    smem = pl.BlockSpec(memory_space=pltpu.SMEM)
    vmem = pl.BlockSpec(memory_space=pltpu.VMEM)
    return pl.pallas_call(
        score_kernel,
        out_shape=jax.ShapeDtypeStruct((4, 3), jnp.float32),
        in_specs=[smem, smem, vmem, vmem],
        out_specs=vmem,
    )(tl, vl, mine, other)


def local(tx, ta, tq, to, tl, vx, va, vq, vo, vl):
    val = jnp.concatenate((vx[0], va[0], vq[0], vo[0]), axis=1)
    train = jnp.concatenate((tx, ta, tq, to), axis=1)
    val = lax.ppermute(val, ("x", "z", "y"), SWAP)
    full = lax.all_gather(train, "y", axis=0, tiled=False)
    own = lax.all_gather(val, "z", axis=0, tiled=True)
    left = lax.ppermute(own, "x", around(NX, 1))
    right = lax.ppermute(own, "x", around(NX, -1))
    far = jnp.concatenate(
        (
            lax.ppermute(left[:ROWS], "x", around(NX, 1)),
            lax.ppermute(right[ROWS:], "x", around(NX, -1)),
        )
    )
    both = grams(full, own, right, left, far)
    c = lax.axis_index("core")
    mine = lax.dynamic_index_in_dim(both, c, 0, keepdims=False)
    send = lax.dynamic_index_in_dim(both, 1 - c, 0, keepdims=False)
    other = lax.ppermute(send, "core", [(0, 1), (1, 0)])
    return scores_of(tl, vl, mine, other)


def solution(mesh):
    fine = Mesh(mesh.devices.reshape(NX, NZ, NY, NC), ("x", "z", "y", "core"))
    dp, fsdp = ("x", "z"), ("y", "core")
    in_specs = (
        (P(dp, fsdp),) * 4 + (P(dp, None),) + (P(dp, None, fsdp),) * 4 + (P(),)
    )
    return jax.shard_map(
        local, mesh=fine, in_specs=in_specs, out_specs=P(dp, fsdp), check_vma=False
    )
```

time: 381 us -> 124 us (0.33)
  blocking collectives: 242 us -> 49.4 us
  waiting for transfers between devices: 84.2 us -> 23.2 us
  matrix products: 11.6 us -> 0 us
  starting transfers between devices: 11.9 us -> 23.1 us
  Pallas kernels: 0 us -> 4.52 us
    all_gather x3 -> x1, blocking collectives: 177 us -> 49.4 us  [local(): own = lax.all_gather(val, 'z', axis=0, tiled=True)]
    all_gather x5 -> x1, waiting for transfers between devices: 68.2 us -> 0.02 us  [local(): full = lax.all_gather(train, 'y', axis=0, tiled=False)]
    unnamed x1 -> x0, blocking collectives: 44.8 us -> none
    ppermute x0 -> x6, waiting for transfers between devices: none -> 23.2 us  [the longest x1 14.9 us: local(): left = lax.ppermute(own, 'x', around(NX, 1))]
    ppermute x0 -> x6, starting transfers between devices: none -> 23 us  [the longest x1 6.85 us: local(): other = lax.ppermute(send, 'core', [(0, 1), (1, 0)])]
    all_to_all x1 -> x0, blocking collectives: 20.4 us -> none  [local(): lax.all_to_all(val_gqkv, 'fsdp', split_axis=1, concat_axis=2, tiled=True)]
    all_to_all x3 -> x0, waiting for transfers between devices: 13.6 us -> none  [the longest x1 7.09 us: local(): lax.all_to_all(val_x, 'fsdp', split_axis=1, concat_axis=2, tiled=True)]
    all_to_all x3 -> x0, starting transfers between devices: 11.8 us -> none  [the longest x1 4.56 us: local(): lax.all_to_all(val_x, 'fsdp', split_axis=1, concat_axis=2, tiled=True)]
  transfers between devices with their start and end apart: 8 -> 7, of which waited for: 5 -> 5; matrix products, arithmetic and copies ran while one was open for 6% -> 2% of each run, Pallas kernels for 0% -> 0%
where the time goes in v1:
time: 124 us; the launch traced here: 122 us
  blocking collectives  49.4 us (40%)
  waiting for transfers between devices  23.2 us (19%)
  starting transfers between devices  23.1 us (19%)
  between operations  13.5 us (11%)
  local copies, waits for them, and re-layouts  5.55 us (4%)
  Pallas kernels  4.52 us (4%)
  other arithmetic  3.23 us (3%)
    all_gather x1, blocking collectives, local(): own = lax.all_gather(val, 'z', axis=0, tiled=True)  49.4 us
    ppermute x1, waiting for transfers between devices, local(): left = lax.ppermute(own, 'x', around(NX, 1))  14.9 us
    ppermute x1, starting transfers between devices, local(): other = lax.ppermute(send, 'core', [(0, 1), (1, 0)])  6.85 us
    ppermute x1, starting transfers between devices, local(): left = lax.ppermute(own, 'x', around(NX, 1))  5.93 us
    unnamed x14, local copies, waits for them, and re-layouts  3.88 us
    ppermute x1, starting transfers between devices, local(): right = lax.ppermute(own, 'x', around(NX, -1))  3.8 us
    ppermute x1, waiting for transfers between devices, local(): lax.ppermute(left[:ROWS], 'x', around(NX, 1))  3.71 us
    ppermute x1, starting transfers between devices, local(): lax.ppermute(left[:ROWS], 'x', around(NX, 1))  2.91 us
  transfers between devices with their start and end apart: 7, of which 5 were waited for; matrix products, arithmetic and copies ran while one was open for 2% of the time, Pallas kernels for 0%

profile of v1, /device:TPU:1, one launch (start us, length us, event | category | flops | bytes accessed | tf_op | source)
XLA Modules:
  0.0 122.5 jit_solution(1811216167303559210)
XLA Ops:
  6.5 0.0 copy-start.6
  6.5 0.0 copy-start.5
  6.5 0.0 copy-start.3
  6.5 0.0 copy-start.4
  6.5 0.0 all-gather.3.cloned.1.call-start
  6.6 2.0 %pad_maximum_fusion.1 = bf16[256,1152]{1,0:T(8,128)(2,1)} fusion(bf16[256,256]{1,0:T(8,128)(2,1)} %param.13, bf16[256,384]{1,0:T(8,128)(2,1)} %param.12, bf16[256,256]{1,0:T(8,128)(2,1)} %param.11, bf16[256,256]{1,0:T(8,128)(2,1)} %param.10), kind=kLoop, calls=%fused_computation.1 | loop fusion | flops 2359296 | bytes 1179648 | tf_op jit(solution)/shard_map/concatenate | solution.py:108
  8.6 0.0 all-gather.3.cloned.1.call-update
  8.6 0.0 copy-done.6
  8.6 0.0 copy-done.5
  8.6 0.0 copy-done.3
  8.6 0.0 copy-done.4
  8.7 0.7 collective-permute-start
  9.3 0.0 collective-permute-done
  9.4 49.4 %all_gather.11.own = bf16[384,1152]{1,0:T(8,128)(2,1)S(1)} all-gather(bf16[32,1152]{1,0:T(8,128)(2,1)S(1)} %collective-permute-done), channel_id=1, replica_groups=mesh['x'=4,'z'=12,'y'=8,'core'=2] {'z'}, dimensions={0}, use_global_device_ids=true | all-gather | bytes 958464 | tf_op jit(solution)/shard_map/all_gather | solution.py:111
  58.7 5.9 %collective-permute-start.2 = (bf16[384,1152]{1,0:T(8,128)(2,1)S(1)}, bf16[384,1152]{1,0:T(8,128)(2,1)S(1)}, u32[]{:S(2)}, u32[]{:S(2)}) collective-permute-start(bf16[384,1152]{1,0:T(8,128)(2,1)S(1)} %all_gather.11.own), channel_id=1, source_target_pairs={{0,192},{192,384},{384,576},{576,0},{1,193},{193,385},{385,577},{5... | collective-permute-start | bytes 2654216 | tf_op jit(solution)/shard_map/ppermute | solution.py:112
  64.7 3.8 %collective-permute-start.1 = (bf16[384,1152]{1,0:T(8,128)(2,1)S(1)}, bf16[384,1152]{1,0:T(8,128)(2,1)S(1)}, u32[]{:S(2)}, u32[]{:S(2)}) collective-permute-start(bf16[384,1152]{1,0:T(8,128)(2,1)S(1)} %all_gather.11.own), channel_id=1, source_target_pairs={{0,576},{192,0},{384,192},{576,384},{1,577},{193,1},{385,193},{577... | collective-permute-start | bytes 2654216 | tf_op jit(solution)/shard_map/ppermute | solution.py:113
  68.5 14.9 %collective-permute-done.2.left = bf16[384,1152]{1,0:T(8,128)(2,1)S(1)} collective-permute-done((bf16[384,1152]{1,0:T(8,128)(2,1)S(1)}, bf16[384,1152]{1,0:T(8,128)(2,1)S(1)}, u32[]{:S(2)}, u32[]{:S(2)}) %collective-permute-start.2) | collective-permute-done | bytes 884768 | tf_op jit(solution)/shard_map/ppermute | solution.py:112
  83.4 2.9 %collective-permute-start.3 = (bf16[192,1152]{1,0:T(8,128)(2,1)S(1)}, bf16[192,1152]{1,0:T(8,128)(2,1)S(1)}, u32[]{:S(2)}, u32[]{:S(2)}) collective-permute-start(bf16[192,1152]{1,0:T(8,128)(2,1)S(1)} %slice.8), channel_id=1, source_target_pairs={{0,192},{192,384},{384,576},{576,0},{1,193},{193,385},{385,577},{5... | collective-permute-start | bytes 1327112 | tf_op jit(solution)/shard_map/ppermute | solution.py:116
  86.4 0.7 collective-permute-done.1.right
  87.1 0.8 slice.9
  87.9 2.9 %collective-permute-start.4 = (bf16[192,1152]{1,0:T(8,128)(2,1)}, bf16[192,1152]{1,0:T(8,128)(2,1)}, u32[]{:S(2)}, u32[]{:S(2)}) collective-permute-start(bf16[192,1152]{1,0:T(8,128)(2,1)} %slice.9), channel_id=1, source_target_pairs={{0,576},{192,0},{384,192},{576,384},{1,577},{193,1},{385,193},{577... | collective-permute-start | bytes 1327112 | tf_op jit(solution)/shard_map/ppermute | solution.py:117
  90.8 3.7 %collective-permute-done.3 = bf16[192,1152]{1,0:T(8,128)(2,1)S(1)} collective-permute-done((bf16[192,1152]{1,0:T(8,128)(2,1)S(1)}, bf16[192,1152]{1,0:T(8,128)(2,1)S(1)}, u32[]{:S(2)}, u32[]{:S(2)}) %collective-permute-start.3) | collective-permute-done | bytes 442400 | tf_op jit(solution)/shard_map/ppermute | solution.py:116
  94.5 0.0 copy-start.1
  94.5 0.8 copy-done.1
  95.3 2.5 %collective-permute-done.4 = bf16[192,1152]{1,0:T(8,128)(2,1)} collective-permute-done((bf16[192,1152]{1,0:T(8,128)(2,1)}, bf16[192,1152]{1,0:T(8,128)(2,1)}, u32[]{:S(2)}, u32[]{:S(2)}) %collective-permute-start.4) | collective-permute-done | bytes 442400 | tf_op jit(solution)/shard_map/ppermute | solution.py:117
  97.8 1.2 pad_maximum_fusion.far
  99.0 0.0 all-gather.3.cloned.1.call-done
  99.0 0.0 copy-start
  99.0 2.3 %copy-done = bf16[2048,1152]{1,0:T(8,128)(2,1)S(1)} copy-done((bf16[2048,1152]{1,0:T(8,128)(2,1)S(1)}, bf16[2048,1152]{1,0:T(8,128)(2,1)}, u32[]{:S(2)}) %copy-start) | copy-done | bytes 4718616
  101.4 2.7 %shard_map.100 = f32[2,4,96,256]{3,2,1,0:T(8,128)S(1)} custom-call(bf16[8,256,1152]{2,1,0:T(8,128)(2,1)S(1)} %bitcast.9, bf16[384,1152]{1,0:T(8,128)(2,1)S(1)} %all_gather.11.own, bf16[384,1152]{1,0:T(8,128)(2,1)S(1)} %collective-permute-done.1.right, bf16[384,1152]{1,0:T(8,128)(2,1)S(1)} %collective-permute-done.2.left, ...), custom_call_target="tpu_custom_call" | custom-call | tf_op jit(solution)/shard_map/pallas_call | solution.py:55
  104.0 0.8 dynamic-slice_bitcast_fusion
  104.9 6.8 %collective-permute-start.5 = (f32[4,96,256]{2,1,0:T(8,128)S(1)}, f32[4,96,256]{2,1,0:T(8,128)S(1)}, u32[]{:S(2)}, u32[]{:S(2)}) collective-permute-start(f32[4,96,256]{2,1,0:T(8,128)S(1)} %get-tuple-element.5), channel_id=1, source_target_pairs={{0,1},{1,0},{2,3},{3,2},{4,5},{5,4},{6,7},{7,6},{8,9},{9,8},{10,11... | collective-permute-start | bytes 1179656 | tf_op jit(solution)/shard_map/ppermute | solution.py:124
  111.7 1.3 %collective-permute-done.5.other = f32[4,96,256]{2,1,0:T(8,128)S(1)} collective-permute-done((f32[4,96,256]{2,1,0:T(8,128)S(1)}, f32[4,96,256]{2,1,0:T(8,128)S(1)}, u32[]{:S(2)}, u32[]{:S(2)}) %collective-permute-start.5) | collective-permute-done | bytes 393248 | tf_op jit(solution)/shard_map/ppermute | solution.py:124
  113.1 0.0 copy-start.2
  113.1 0.7 copy-done.2
  113.8 1.8 %shard_map.101 = f32[4,3]{1,0:T(4,128)} custom-call(s32[1,4]{1,0:T(1,128)} %tl.1, s32[48]{0:T(128)} %vl.1, f32[4,96,256]{2,1,0:T(8,128)} %get-tuple-element.6.mine, f32[4,96,256]{2,1,0:T(8,128)} %copy-done.2), custom_call_target="tpu_custom_call" | custom-call | tf_op jit(solution)/shard_map/pallas_call | solution.py:98
  (2 shorter events, 0.0 us)
Async XLA Ops:
  6.5 2.1 %copy-start.6 = (bf16[1,32,256]{2,1,0:T(8,128)(2,1)S(1)}, bf16[1,32,256]{2,1,0:T(8,128)(2,1)}, u32[]{:S(2)}) copy-start(bf16[1,32,256]{2,1,0:T(8,128)(2,1)} %param.15) | copy-start | bytes 49156
  6.5 2.1 %copy-start.5 = (bf16[1,32,256]{2,1,0:T(8,128)(2,1)S(1)}, bf16[1,32,256]{2,1,0:T(8,128)(2,1)}, u32[]{:S(2)}) copy-start(bf16[1,32,256]{2,1,0:T(8,128)(2,1)} %param.16) | copy-start | bytes 49156
  6.5 2.1 %copy-start.3 = (bf16[1,32,384]{2,1,0:T(8,128)(2,1)S(1)}, bf16[1,32,384]{2,1,0:T(8,128)(2,1)}, u32[]{:S(2)}) copy-start(bf16[1,32,384]{2,1,0:T(8,128)(2,1)} %param.17) | copy-start | bytes 73732
  6.5 2.1 %copy-start.4 = (bf16[1,32,256]{2,1,0:T(8,128)(2,1)S(1)}, bf16[1,32,256]{2,1,0:T(8,128)(2,1)}, u32[]{:S(2)}) copy-start(bf16[1,32,256]{2,1,0:T(8,128)(2,1)} %param.18) | copy-start | bytes 49156
  6.5 92.5 %all-gather.3.cloned.1.call-start = ((), (), s32[]{:S(2)}) async-start(), calls=%async_computation | async-start | bytes 5308416 | tf_op jit(solution)/shard_map/all_gather | solution.py:110
  8.7 0.7 collective-permute-start
  58.7 24.7 %collective-permute-start.2 = (bf16[384,1152]{1,0:T(8,128)(2,1)S(1)}, bf16[384,1152]{1,0:T(8,128)(2,1)S(1)}, u32[]{:S(2)}, u32[]{:S(2)}) collective-permute-start(bf16[384,1152]{1,0:T(8,128)(2,1)S(1)} %all_gather.11.own), channel_id=1, source_target_pairs={{0,192},{192,384},{384,576},{576,0},{1,193},{193,385},{385,577},{5... | collective-permute-start | bytes 2654216 | tf_op jit(solution)/shard_map/ppermute | solution.py:112
  64.7 22.4 %collective-permute-start.1 = (bf16[384,1152]{1,0:T(8,128)(2,1)S(1)}, bf16[384,1152]{1,0:T(8,128)(2,1)S(1)}, u32[]{:S(2)}, u32[]{:S(2)}) collective-permute-start(bf16[384,1152]{1,0:T(8,128)(2,1)S(1)} %all_gather.11.own), channel_id=1, source_target_pairs={{0,576},{192,0},{384,192},{576,384},{1,577},{193,1},{385,193},{577... | collective-permute-start | bytes 2654216 | tf_op jit(solution)/shard_map/ppermute | solution.py:113
  83.4 11.0 %collective-permute-start.3 = (bf16[192,1152]{1,0:T(8,128)(2,1)S(1)}, bf16[192,1152]{1,0:T(8,128)(2,1)S(1)}, u32[]{:S(2)}, u32[]{:S(2)}) collective-permute-start(bf16[192,1152]{1,0:T(8,128)(2,1)S(1)} %slice.8), channel_id=1, source_target_pairs={{0,192},{192,384},{384,576},{576,0},{1,193},{193,385},{385,577},{5... | collective-permute-start | bytes 1327112 | tf_op jit(solution)/shard_map/ppermute | solution.py:116
  87.9 9.9 %collective-permute-start.4 = (bf16[192,1152]{1,0:T(8,128)(2,1)}, bf16[192,1152]{1,0:T(8,128)(2,1)}, u32[]{:S(2)}, u32[]{:S(2)}) collective-permute-start(bf16[192,1152]{1,0:T(8,128)(2,1)} %slice.9), channel_id=1, source_target_pairs={{0,576},{192,0},{384,192},{576,384},{1,577},{193,1},{385,193},{577... | collective-permute-start | bytes 1327112 | tf_op jit(solution)/shard_map/ppermute | solution.py:117
  94.5 0.8 copy-start.1
  99.0 2.3 %copy-start = (bf16[2048,1152]{1,0:T(8,128)(2,1)S(1)}, bf16[2048,1152]{1,0:T(8,128)(2,1)}, u32[]{:S(2)}) copy-start(bf16[2048,1152]{1,0:T(8,128)(2,1)} %all-gather.3.cloned.1.call-done) | copy-start | bytes 14155780
  104.9 8.2 %collective-permute-start.5 = (f32[4,96,256]{2,1,0:T(8,128)S(1)}, f32[4,96,256]{2,1,0:T(8,128)S(1)}, u32[]{:S(2)}, u32[]{:S(2)}) collective-permute-start(f32[4,96,256]{2,1,0:T(8,128)S(1)} %get-tuple-element.5), channel_id=1, source_target_pairs={{0,1},{1,0},{2,3},{3,2},{4,5},{5,4},{6,7},{7,6},{8,9},{9,8},{10,11... | collective-permute-start | bytes 1179656 | tf_op jit(solution)/shard_map/ppermute | solution.py:124
  113.1 0.8 copy-start.2
Sparse Core Ops, SparseCore 0:
  9.7 72.3 all-gather.2

commit v2 on v1

v2 whole, which is shorter than its diff:
```python
import numpy as np
import jax
import jax.numpy as jnp
from jax import lax
from jax.experimental import pallas as pl
from jax.experimental.pallas import tpu as pltpu
from jax.sharding import Mesh, PartitionSpec as P

score_scale = 0.015625

NX, NZ, NY, NC = 4, 12, 8, 2
TOK, VLEN = 256, 32
SEQS = 6
ROWS = SEQS * VLEN
HALF = ROWS // 2
COLS = ((0, 256), (256, 512), (512, 896), (896, 1152))
WIDTH = 1152

def deal(shift):
    pairs = []
    for a in range(NY):
        for s in range(NX * NZ):
            x, z = divmod(s, NZ)
            to = x * NZ + (z - shift) % NZ
            pairs.append(((SEQS * a + s % SEQS) * NY + s // SEQS, to * NY + a))
    return pairs


def around(size, shift):
    return [(i, (i + shift) % size) for i in range(size)]


def gram_kernel(*refs):
    trains, vals = refs[:NY], refs[NY : NY + 3]
    mine, send, tbuf, vbuf, tsem, vsem = refs[NY + 3 :]
    x, z = lax.axis_index("x"), lax.axis_index("z")
    y, core = lax.axis_index("y"), lax.axis_index("core")
    vcopy = [pltpu.make_async_copy(r, vbuf.at[i], vsem.at[i]) for i, r in enumerate(vals)]
    tcopy = [pltpu.make_async_copy(r, tbuf.at[i], tsem.at[i]) for i, r in enumerate(trains)]
    for c in vcopy + tcopy:
        c.start()
    for c in vcopy:
        c.wait()
    for k in range(NY):
        tcopy[k].wait()
        b = lax.rem(y + k, NY)
        for half, out in ((1 - core, send), (core, mine)):
            blocks = []
            for r in range(3):
                s = SEQS * b + 3 * half + r
                dx = lax.rem(s // NZ - x + NX, NX)
                dz = lax.rem(lax.rem(s, NZ) - z + NZ, NZ)
                kind = lax.rem(dz, 3)
                step = jnp.where(kind == 2, lax.rem((dz + 1) // 3, 4), dz // 3)
                blocks.append((kind, dx * 4 + step))
            for g, (lo, hi) in enumerate(COLS):
                v = jnp.concatenate([vbuf[p, q, :, lo:hi] for p, q in blocks])
                d = lax.dot_general(
                    v,
                    tbuf[k, :, lo:hi],
                    (((1,), (1,)), ((), ())),
                    preferred_element_type=jnp.float32,
                )
                if k == 0:
                    out[g] = d
                else:
                    out[g] += d


def grams(trains, vals):
    half = jax.ShapeDtypeStruct((4, HALF, TOK), jnp.float32)
    vmem = pl.BlockSpec(memory_space=pltpu.VMEM)
    return pl.pallas_call(
        gram_kernel,
        out_shape=(half, half),
        in_specs=[pl.BlockSpec(memory_space=pl.ANY)] * (NY + 3),
        out_specs=(vmem, vmem),
        scratch_shapes=[
            pltpu.VMEM((NY, TOK, WIDTH), jnp.bfloat16),
            pltpu.VMEM((3, 16, VLEN, WIDTH), jnp.bfloat16),
            pltpu.SemaphoreType.DMA((NY,)),
            pltpu.SemaphoreType.DMA((3,)),
        ],
        compiler_params=pltpu.CompilerParams(vmem_limit_bytes=32 * 1024 * 1024),
    )(*trains, *vals)


def score_kernel(tl, vl, mine_any, other_any, out, mine, other, sems):
    copies = (
        pltpu.make_async_copy(mine_any, mine, sems.at[0]),
        pltpu.make_async_copy(other_any, other, sems.at[1]),
    )
    for c in copies:
        c.start()
    for c in copies:
        c.wait()
    first = 3 * (2 * lax.axis_index("y") + lax.axis_index("core"))
    g = mine[...] + other[...]
    contrib = g[0] * g[2] + g[1] * g[3]
    places = lax.broadcasted_iota(jnp.int32, (VLEN, TOK), 0)
    tokens = lax.broadcasted_iota(jnp.int32, (1, TOK), 1)
    rows = lax.broadcasted_iota(jnp.int32, (4, 3), 0)
    cols = lax.broadcasted_iota(jnp.int32, (4, 3), 1)
    result = jnp.zeros((4, 3), jnp.float32)
    for s in range(3):
        block = contrib[s * VLEN : (s + 1) * VLEN]
        per_token = jnp.sum(
            jnp.where(places < vl[first + s], block, 0.0), axis=0, keepdims=True
        )
        start = jnp.int32(0)
        for k in range(4):
            end = start + tl[0, k]
            inside = (tokens >= start) & (tokens < end)
            total = jnp.sum(
                jnp.where(inside, per_token, 0.0), axis=1, keepdims=True
            )
            result = jnp.where((rows == k) & (cols == s), total, result)
            start = end
    out[...] = result * score_scale


def scores_of(tl, vl, mine, other):
    smem = pl.BlockSpec(memory_space=pltpu.SMEM)
    any_spec = pl.BlockSpec(memory_space=pl.ANY)
    half = pltpu.VMEM((4, HALF, TOK), jnp.float32)
    return pl.pallas_call(
        score_kernel,
        out_shape=jax.ShapeDtypeStruct((4, 3), jnp.float32),
        in_specs=[smem, smem, any_spec, any_spec],
        out_specs=pl.BlockSpec(memory_space=pltpu.VMEM),
        scratch_shapes=[half, half, pltpu.SemaphoreType.DMA((2,))],
    )(tl, vl, mine, other)


def local(tx, ta, tq, to, tl, vx, va, vq, vo, vl):
    val = jnp.concatenate((vx[0], va[0], vq[0], vo[0]), axis=1)
    train = jnp.concatenate((tx, ta, tq, to), axis=1)
    dealt = jnp.stack([lax.ppermute(val, ("x", "z", "y"), deal(3 * k)) for k in range(4)])

    above, below = [train], [train]
    for _ in range(3):
        above.append(lax.ppermute(above[-1], "y", around(NY, -1)))
        below.append(lax.ppermute(below[-1], "y", around(NY, 1)))
    below.append(lax.ppermute(below[-1], "y", around(NY, 1)))
    trains = above + below[:0:-1]

    plane = jnp.concatenate(
        [dealt] + [lax.ppermute(dealt, "x", around(NX, -d)) for d in (1, 2, 3)]
    )
    up = lax.ppermute(plane, "z", around(NZ, -1))
    down = lax.ppermute(plane, "z", around(NZ, 1))
    mine, send = grams(trains, (plane, up, down))
    other = lax.ppermute(send, "core", [(0, 1), (1, 0)])
    return scores_of(tl, vl, mine, other)


def solution(mesh):
    fine = Mesh(mesh.devices.reshape(NX, NZ, NY, NC), ("x", "z", "y", "core"))
    dp, fsdp = ("x", "z"), ("y", "core")
    in_specs = (
        (P(dp, fsdp),) * 4 + (P(dp, None),) + (P(dp, None, fsdp),) * 4 + (P(),)
    )
    return jax.shard_map(
        local, mesh=fine, in_specs=in_specs, out_specs=P(dp, fsdp), check_vma=False
    )
```

time: 124 us -> 134 us (1.081)
  the two profiles are of different devices: /device:TPU:1 before, /device:TPU:3 now
where the time goes in v2:
time: 134 us; the launch traced here: 133 us
  starting transfers between devices  88 us (66%)
  waiting for transfers between devices  31.7 us (24%)
  Pallas kernels  7.26 us (5%)
  local copies, waits for them, and re-layouts  5.33 us (4%)
    ppermute x4, starting transfers between devices, local(): lax.ppermute(val, ('x', 'z', 'y'), deal(3 * k))  26.9 us
    ppermute x3, starting transfers between devices, local(): above.append(lax.ppermute(above[-1], 'y', around(NY, -1)))  20.7 us
    ppermute x3, waiting for transfers between devices, local(): above.append(lax.ppermute(above[-1], 'y', around(NY, -1)))  19.8 us
    ppermute x4, starting transfers between devices, local(): below.append(lax.ppermute(below[-1], 'y', around(NY, 1)))  17 us
    ppermute x4, waiting for transfers between devices, local(): below.append(lax.ppermute(below[-1], 'y', around(NY, 1)))  7.7 us
    ppermute x3, starting transfers between devices, local(): lax.ppermute(dealt, 'x', around(NX, -d))  7.34 us
    ppermute x1, starting transfers between devices, local(): up = lax.ppermute(plane, 'z', around(NZ, -1))  7.06 us
    ppermute x1, starting transfers between devices, local(): other = lax.ppermute(send, 'core', [(0, 1), (1, 0)])  4.77 us
  transfers between devices with their start and end apart: 17, of which 6 were waited for; matrix products, arithmetic and copies ran while one was open for 3% of the time, Pallas kernels for 0%

profile of v2, /device:TPU:3, one launch (start us, length us, event | category | flops | bytes accessed | tf_op | source)
XLA Modules:
  0.0 133.3 jit_solution(10221861582985333924)
XLA Ops:
  0.0 0.8 pad_maximum_fusion.1
  0.8 9.6 %collective-permute-start.10 = (bf16[32,1152]{1,0:T(8,128)(2,1)S(1)}, bf16[32,1152]{1,0:T(8,128)(2,1)S(1)}, u32[]{:S(2)}, u32[]{:S(2)}) collective-permute-start(bf16[32,1152]{1,0:T(8,128)(2,1)S(1)} %pad_maximum_fusion.1), channel_id=1, source_target_pairs={{0,48},{16,64},{32,80},{48,96},{64,112},{80,128},{2,144},{18,160},... | collective-permute-start | bytes 221192 | tf_op jit(solution)/shard_map/ppermute | solution.py:138
  10.4 9.2 %collective-permute-start.9 = (bf16[32,1152]{1,0:T(8,128)(2,1)S(1)}, bf16[32,1152]{1,0:T(8,128)(2,1)S(1)}, u32[]{:S(2)}, u32[]{:S(2)}) collective-permute-start(bf16[32,1152]{1,0:T(8,128)(2,1)S(1)} %pad_maximum_fusion.1), channel_id=1, source_target_pairs={{0,96},{16,112},{32,128},{48,144},{64,160},{80,176},{2,0},{18,16},... | collective-permute-start | bytes 221192 | tf_op jit(solution)/shard_map/ppermute | solution.py:138
  19.6 3.0 %collective-permute-start.8 = (bf16[32,1152]{1,0:T(8,128)(2,1)S(1)}, bf16[32,1152]{1,0:T(8,128)(2,1)S(1)}, u32[]{:S(2)}, u32[]{:S(2)}) collective-permute-start(bf16[32,1152]{1,0:T(8,128)(2,1)S(1)} %pad_maximum_fusion.1), channel_id=1, source_target_pairs={{0,144},{16,160},{32,176},{48,0},{64,16},{80,32},{2,48},{18,64},{3... | collective-permute-start | bytes 221192 | tf_op jit(solution)/shard_map/ppermute | solution.py:138
  22.6 5.1 %collective-permute-start.7 = (bf16[32,1152]{1,0:T(8,128)(2,1)S(1)}, bf16[32,1152]{1,0:T(8,128)(2,1)S(1)}, u32[]{:S(2)}, u32[]{:S(2)}) collective-permute-start(bf16[32,1152]{1,0:T(8,128)(2,1)S(1)} %pad_maximum_fusion.1), channel_id=1, source_target_pairs={{0,0},{16,16},{32,32},{48,48},{64,64},{80,80},{2,96},{18,112},{34,... | collective-permute-start | bytes 221192 | tf_op jit(solution)/shard_map/ppermute | solution.py:138
  27.7 0.9 constant_dynamic-update-slice_fusion.3
  28.6 0.9 constant_dynamic-update-slice_fusion.2
  29.5 1.0 constant_dynamic-update-slice_fusion.1
  30.5 0.9 constant_dynamic-update-slice_fusion.refs_0_
  31.4 5.5 %collective-permute-start.3 = (bf16[256,1152]{1,0:T(8,128)(2,1)S(1)}, bf16[256,1152]{1,0:T(8,128)(2,1)S(1)}, u32[]{:S(2)}, u32[]{:S(2)}) collective-permute-start(bf16[256,1152]{1,0:T(8,128)(2,1)S(1)} %constant_dynamic-update-slice_fusion.refs_0_), channel_id=1, source_target_pairs={{0,2},{2,4},{4,6},{6,8},{8,10},{10,12},{12,14},{14,0},{1,3},{3,5},... | collective-permute-start | bytes 1769480 | tf_op jit(solution)/shard_map/ppermute | solution.py:143
  36.9 0.0 collective-permute-done.10
  36.9 9.3 %collective-permute-start = (bf16[256,1152]{1,0:T(8,128)(2,1)S(1)}, bf16[256,1152]{1,0:T(8,128)(2,1)S(1)}, u32[]{:S(2)}, u32[]{:S(2)}) collective-permute-start(bf16[256,1152]{1,0:T(8,128)(2,1)S(1)} %constant_dynamic-update-slice_fusion.refs_0_), channel_id=1, source_target_pairs={{0,14},{2,0},{4,2},{6,4},{8,6},{10,8},{12,10},{14,12},{1,15},{3,1}... | collective-permute-start | bytes 1769480 | tf_op jit(solution)/shard_map/ppermute | solution.py:142
  46.2 0.0 collective-permute-done.9
  46.2 0.0 collective-permute-done.8
  46.2 0.0 collective-permute-done.7
  46.3 1.9 %collective-permute-start.13 = (bf16[4,32,1152]{2,1,0:T(8,128)(2,1)S(1)}, bf16[4,32,1152]{2,1,0:T(8,128)(2,1)S(1)}, u32[]{:S(2)}, u32[]{:S(2)}) collective-permute-start(bf16[4,32,1152]{2,1,0:T(8,128)(2,1)S(1)} %pad_maximum_fusion), channel_id=1, source_target_pairs={{0,192},{192,384},{384,576},{576,0},{1,193},{193,385},{385,577},{5... | collective-permute-start | bytes 884744 | tf_op jit(solution)/shard_map/ppermute | solution.py:148
  48.2 1.9 %collective-permute-start.12 = (bf16[4,32,1152]{2,1,0:T(8,128)(2,1)S(1)}, bf16[4,32,1152]{2,1,0:T(8,128)(2,1)S(1)}, u32[]{:S(2)}, u32[]{:S(2)}) collective-permute-start(bf16[4,32,1152]{2,1,0:T(8,128)(2,1)S(1)} %pad_maximum_fusion), channel_id=1, source_target_pairs={{0,384},{192,576},{384,0},{576,192},{1,385},{193,577},{385,1},{577... | collective-permute-start | bytes 884744 | tf_op jit(solution)/shard_map/ppermute | solution.py:148
  50.1 3.5 %collective-permute-start.11 = (bf16[4,32,1152]{2,1,0:T(8,128)(2,1)S(1)}, bf16[4,32,1152]{2,1,0:T(8,128)(2,1)S(1)}, u32[]{:S(2)}, u32[]{:S(2)}) collective-permute-start(bf16[4,32,1152]{2,1,0:T(8,128)(2,1)S(1)} %pad_maximum_fusion), channel_id=1, source_target_pairs={{0,576},{192,0},{384,192},{576,384},{1,577},{193,1},{385,193},{577... | collective-permute-start | bytes 884744 | tf_op jit(solution)/shard_map/ppermute | solution.py:148
  53.7 2.6 %collective-permute-done.3.refs_7_ = bf16[256,1152]{1,0:T(8,128)(2,1)S(1)} collective-permute-done((bf16[256,1152]{1,0:T(8,128)(2,1)S(1)}, bf16[256,1152]{1,0:T(8,128)(2,1)S(1)}, u32[]{:S(2)}, u32[]{:S(2)}) %collective-permute-start.3) | collective-permute-done | bytes 589856 | tf_op jit(solution)/shard_map/ppermute | solution.py:143
  56.3 7.6 %collective-permute-start.4 = (bf16[256,1152]{1,0:T(8,128)(2,1)S(1)}, bf16[256,1152]{1,0:T(8,128)(2,1)S(1)}, u32[]{:S(2)}, u32[]{:S(2)}) collective-permute-start(bf16[256,1152]{1,0:T(8,128)(2,1)S(1)} %collective-permute-done.3.refs_7_), channel_id=1, source_target_pairs={{0,2},{2,4},{4,6},{6,8},{8,10},{10,12},{12,14},{14,0},{1,3},{3,5},... | collective-permute-start | bytes 1769480 | tf_op jit(solution)/shard_map/ppermute | solution.py:143
  64.0 2.8 %collective-permute-done.11 = bf16[4,32,1152]{2,1,0:T(8,128)(2,1)S(1)} collective-permute-done((bf16[4,32,1152]{2,1,0:T(8,128)(2,1)S(1)}, bf16[4,32,1152]{2,1,0:T(8,128)(2,1)S(1)}, u32[]{:S(2)}, u32[]{:S(2)}) %collective-permute-start.11) | collective-permute-done | bytes 294944 | tf_op jit(solution)/shard_map/ppermute | solution.py:148
  66.8 0.0 collective-permute-done.12
  66.9 0.0 collective-permute-done.13
  66.9 4.3 %collective-permute-start.15 = (bf16[16,32,1152]{2,1,0:T(8,128)(2,1)S(1)}, bf16[16,32,1152]{2,1,0:T(8,128)(2,1)S(1)}, u32[]{:S(2)}, u32[]{:S(2)}) collective-permute-start(bf16[16,32,1152]{2,1,0:T(8,128)(2,1)S(1)} %constant_dynamic-update-slice_fusion.4.refs_8_), channel_id=1, source_target_pairs={{0,16},{16,32},{32,48},{48,64},{64,80},{80,96},{96,112},{112,128},... | collective-permute-start | bytes 3538952 | tf_op jit(solution)/shard_map/ppermute | solution.py:151
  71.2 7.1 %collective-permute-start.14 = (bf16[16,32,1152]{2,1,0:T(8,128)(2,1)S(1)}, bf16[16,32,1152]{2,1,0:T(8,128)(2,1)S(1)}, u32[]{:S(2)}, u32[]{:S(2)}) collective-permute-start(bf16[16,32,1152]{2,1,0:T(8,128)(2,1)S(1)} %constant_dynamic-update-slice_fusion.4.refs_8_), channel_id=1, source_target_pairs={{0,176},{16,0},{32,16},{48,32},{64,48},{80,64},{96,80},{112,96},{1... | collective-permute-start | bytes 3538952 | tf_op jit(solution)/shard_map/ppermute | solution.py:150
  78.3 0.0 collective-permute-done.refs_1_
  78.3 7.0 %collective-permute-start.1 = (bf16[256,1152]{1,0:T(8,128)(2,1)S(1)}, bf16[256,1152]{1,0:T(8,128)(2,1)S(1)}, u32[]{:S(2)}, u32[]{:S(2)}) collective-permute-start(bf16[256,1152]{1,0:T(8,128)(2,1)S(1)} %collective-permute-done.refs_1_), channel_id=1, source_target_pairs={{0,14},{2,0},{4,2},{6,4},{8,6},{10,8},{12,10},{14,12},{1,15},{3,1}... | collective-permute-start | bytes 1769480 | tf_op jit(solution)/shard_map/ppermute | solution.py:142
  85.3 0.0 collective-permute-done.4.refs_6_
  85.3 1.9 %collective-permute-start.5 = (bf16[256,1152]{1,0:T(8,128)(2,1)S(1)}, bf16[256,1152]{1,0:T(8,128)(2,1)S(1)}, u32[]{:S(2)}, u32[]{:S(2)}) collective-permute-start(bf16[256,1152]{1,0:T(8,128)(2,1)S(1)} %collective-permute-done.4.refs_6_), channel_id=1, source_target_pairs={{0,2},{2,4},{4,6},{6,8},{8,10},{10,12},{12,14},{14,0},{1,3},{3,5},... | collective-permute-start | bytes 1769480 | tf_op jit(solution)/shard_map/ppermute | solution.py:143
  87.3 10.8 %collective-permute-done.1.refs_2_ = bf16[256,1152]{1,0:T(8,128)(2,1)S(1)} collective-permute-done((bf16[256,1152]{1,0:T(8,128)(2,1)S(1)}, bf16[256,1152]{1,0:T(8,128)(2,1)S(1)}, u32[]{:S(2)}, u32[]{:S(2)}) %collective-permute-start.1) | collective-permute-done | bytes 589856 | tf_op jit(solution)/shard_map/ppermute | solution.py:142
  98.1 4.4 %collective-permute-start.2 = (bf16[256,1152]{1,0:T(8,128)(2,1)S(1)}, bf16[256,1152]{1,0:T(8,128)(2,1)S(1)}, u32[]{:S(2)}, u32[]{:S(2)}) collective-permute-start(bf16[256,1152]{1,0:T(8,128)(2,1)S(1)} %collective-permute-done.1.refs_2_), channel_id=1, source_target_pairs={{0,14},{2,0},{4,2},{6,4},{8,6},{10,8},{12,10},{14,12},{1,15},{3,1}... | collective-permute-start | bytes 1769480 | tf_op jit(solution)/shard_map/ppermute | solution.py:142
  102.5 0.0 collective-permute-done.5.refs_5_
  102.5 1.9 %collective-permute-start.6 = (bf16[256,1152]{1,0:T(8,128)(2,1)S(1)}, bf16[256,1152]{1,0:T(8,128)(2,1)S(1)}, u32[]{:S(2)}, u32[]{:S(2)}) collective-permute-start(bf16[256,1152]{1,0:T(8,128)(2,1)S(1)} %collective-permute-done.5.refs_5_), channel_id=1, source_target_pairs={{0,2},{2,4},{4,6},{6,8},{8,10},{10,12},{12,14},{14,0},{1,3},{3,5},... | collective-permute-start | bytes 1769480 | tf_op jit(solution)/shard_map/ppermute | solution.py:144
  104.4 0.0 collective-permute-done.15.refs_10_
  104.5 0.0 collective-permute-done.14.refs_9_
  104.5 9.0 %collective-permute-done.2.refs_3_ = bf16[256,1152]{1,0:T(8,128)(2,1)S(1)} collective-permute-done((bf16[256,1152]{1,0:T(8,128)(2,1)S(1)}, bf16[256,1152]{1,0:T(8,128)(2,1)S(1)}, u32[]{:S(2)}, u32[]{:S(2)}) %collective-permute-start.2) | collective-permute-done | bytes 589856 | tf_op jit(solution)/shard_map/ppermute | solution.py:142
  113.4 5.1 %collective-permute-done.6.refs_4_ = bf16[256,1152]{1,0:T(8,128)(2,1)S(1)} collective-permute-done((bf16[256,1152]{1,0:T(8,128)(2,1)S(1)}, bf16[256,1152]{1,0:T(8,128)(2,1)S(1)}, u32[]{:S(2)}, u32[]{:S(2)}) %collective-permute-start.6) | collective-permute-done | bytes 589856 | tf_op jit(solution)/shard_map/ppermute | solution.py:144
  118.5 4.7 %shard_map.100 = (f32[4,96,256]{2,1,0:T(8,128)S(1)}, f32[4,96,256]{2,1,0:T(8,128)S(1)}) custom-call(bf16[256,1152]{1,0:T(8,128)(2,1)S(1)} %constant_dynamic-update-slice_fusion.refs_0_, bf16[256,1152]{1,0:T(8,128)(2,1)S(1)} %collective-permute-done.refs_1_, bf16[256,1152]{1,0:T(8,128)(2,1)S(1)} %collective-permute-done.1.refs_2_, ...), custom_call_target="tpu_custom_call" | custom-call | tf_op jit(solution)/shard_map/pallas_call | solution.py:73
  123.2 0.0 copy-start
  123.3 0.7 copy-done
  124.0 4.8 %collective-permute-start.16 = (f32[4,96,256]{2,1,0:T(8,128)S(1)}, f32[4,96,256]{2,1,0:T(8,128)S(1)}, u32[]{:S(2)}, u32[]{:S(2)}) collective-permute-start(f32[4,96,256]{2,1,0:T(8,128)S(1)} %get-tuple-element.8), channel_id=1, source_target_pairs={{0,1},{1,0},{2,3},{3,2},{4,5},{5,4},{6,7},{7,6},{8,9},{9,8},{10,11... | collective-permute-start | bytes 1179656 | tf_op jit(solution)/shard_map/ppermute | solution.py:153
  128.8 1.3 collective-permute-done.16.other_any
  130.1 0.0 copy-start.1
  130.1 0.7 copy-done.1
  130.8 2.5 %shard_map.101 = f32[4,3]{1,0:T(4,128)} custom-call(s32[1,4]{1,0:T(1,128)} %tl.1, s32[48]{0:T(128)} %vl.1, f32[4,96,256]{2,1,0:T(8,128)} %copy-done, f32[4,96,256]{2,1,0:T(8,128)} %copy-done.1), custom_call_target="tpu_custom_call" | custom-call | tf_op jit(solution)/shard_map/pallas_call | solution.py:126
  (8 shorter events, 0.2 us)
Async XLA Ops:
  0.8 36.1 %collective-permute-start.10 = (bf16[32,1152]{1,0:T(8,128)(2,1)S(1)}, bf16[32,1152]{1,0:T(8,128)(2,1)S(1)}, u32[]{:S(2)}, u32[]{:S(2)}) collective-permute-start(bf16[32,1152]{1,0:T(8,128)(2,1)S(1)} %pad_maximum_fusion.1), channel_id=1, source_target_pairs={{0,48},{16,64},{32,80},{48,96},{64,112},{80,128},{2,144},{18,160},... | collective-permute-start | bytes 221192 | tf_op jit(solution)/shard_map/ppermute | solution.py:138
  10.4 35.8 %collective-permute-start.9 = (bf16[32,1152]{1,0:T(8,128)(2,1)S(1)}, bf16[32,1152]{1,0:T(8,128)(2,1)S(1)}, u32[]{:S(2)}, u32[]{:S(2)}) collective-permute-start(bf16[32,1152]{1,0:T(8,128)(2,1)S(1)} %pad_maximum_fusion.1), channel_id=1, source_target_pairs={{0,96},{16,112},{32,128},{48,144},{64,160},{80,176},{2,0},{18,16},... | collective-permute-start | bytes 221192 | tf_op jit(solution)/shard_map/ppermute | solution.py:138
  19.6 26.6 %collective-permute-start.8 = (bf16[32,1152]{1,0:T(8,128)(2,1)S(1)}, bf16[32,1152]{1,0:T(8,128)(2,1)S(1)}, u32[]{:S(2)}, u32[]{:S(2)}) collective-permute-start(bf16[32,1152]{1,0:T(8,128)(2,1)S(1)} %pad_maximum_fusion.1), channel_id=1, source_target_pairs={{0,144},{16,160},{32,176},{48,0},{64,16},{80,32},{2,48},{18,64},{3... | collective-permute-start | bytes 221192 | tf_op jit(solution)/shard_map/ppermute | solution.py:138
  22.6 23.6 %collective-permute-start.7 = (bf16[32,1152]{1,0:T(8,128)(2,1)S(1)}, bf16[32,1152]{1,0:T(8,128)(2,1)S(1)}, u32[]{:S(2)}, u32[]{:S(2)}) collective-permute-start(bf16[32,1152]{1,0:T(8,128)(2,1)S(1)} %pad_maximum_fusion.1), channel_id=1, source_target_pairs={{0,0},{16,16},{32,32},{48,48},{64,64},{80,80},{2,96},{18,112},{34,... | collective-permute-start | bytes 221192 | tf_op jit(solution)/shard_map/ppermute | solution.py:138
  31.4 25.0 %collective-permute-start.3 = (bf16[256,1152]{1,0:T(8,128)(2,1)S(1)}, bf16[256,1152]{1,0:T(8,128)(2,1)S(1)}, u32[]{:S(2)}, u32[]{:S(2)}) collective-permute-start(bf16[256,1152]{1,0:T(8,128)(2,1)S(1)} %constant_dynamic-update-slice_fusion.refs_0_), channel_id=1, source_target_pairs={{0,2},{2,4},{4,6},{6,8},{8,10},{10,12},{12,14},{14,0},{1,3},{3,5},... | collective-permute-start | bytes 1769480 | tf_op jit(solution)/shard_map/ppermute | solution.py:143
  36.9 41.4 %collective-permute-start = (bf16[256,1152]{1,0:T(8,128)(2,1)S(1)}, bf16[256,1152]{1,0:T(8,128)(2,1)S(1)}, u32[]{:S(2)}, u32[]{:S(2)}) collective-permute-start(bf16[256,1152]{1,0:T(8,128)(2,1)S(1)} %constant_dynamic-update-slice_fusion.refs_0_), channel_id=1, source_target_pairs={{0,14},{2,0},{4,2},{6,4},{8,6},{10,8},{12,10},{14,12},{1,15},{3,1}... | collective-permute-start | bytes 1769480 | tf_op jit(solution)/shard_map/ppermute | solution.py:142
  46.3 20.6 %collective-permute-start.13 = (bf16[4,32,1152]{2,1,0:T(8,128)(2,1)S(1)}, bf16[4,32,1152]{2,1,0:T(8,128)(2,1)S(1)}, u32[]{:S(2)}, u32[]{:S(2)}) collective-permute-start(bf16[4,32,1152]{2,1,0:T(8,128)(2,1)S(1)} %pad_maximum_fusion), channel_id=1, source_target_pairs={{0,192},{192,384},{384,576},{576,0},{1,193},{193,385},{385,577},{5... | collective-permute-start | bytes 884744 | tf_op jit(solution)/shard_map/ppermute | solution.py:148
  48.2 18.7 %collective-permute-start.12 = (bf16[4,32,1152]{2,1,0:T(8,128)(2,1)S(1)}, bf16[4,32,1152]{2,1,0:T(8,128)(2,1)S(1)}, u32[]{:S(2)}, u32[]{:S(2)}) collective-permute-start(bf16[4,32,1152]{2,1,0:T(8,128)(2,1)S(1)} %pad_maximum_fusion), channel_id=1, source_target_pairs={{0,384},{192,576},{384,0},{576,192},{1,385},{193,577},{385,1},{577... | collective-permute-start | bytes 884744 | tf_op jit(solution)/shard_map/ppermute | solution.py:148
  50.1 16.7 %collective-permute-start.11 = (bf16[4,32,1152]{2,1,0:T(8,128)(2,1)S(1)}, bf16[4,32,1152]{2,1,0:T(8,128)(2,1)S(1)}, u32[]{:S(2)}, u32[]{:S(2)}) collective-permute-start(bf16[4,32,1152]{2,1,0:T(8,128)(2,1)S(1)} %pad_maximum_fusion), channel_id=1, source_target_pairs={{0,576},{192,0},{384,192},{576,384},{1,577},{193,1},{385,193},{577... | collective-permute-start | bytes 884744 | tf_op jit(solution)/shard_map/ppermute | solution.py:148
  56.3 29.0 %collective-permute-start.4 = (bf16[256,1152]{1,0:T(8,128)(2,1)S(1)}, bf16[256,1152]{1,0:T(8,128)(2,1)S(1)}, u32[]{:S(2)}, u32[]{:S(2)}) collective-permute-start(bf16[256,1152]{1,0:T(8,128)(2,1)S(1)} %collective-permute-done.3.refs_7_), channel_id=1, source_target_pairs={{0,2},{2,4},{4,6},{6,8},{8,10},{10,12},{12,14},{14,0},{1,3},{3,5},... | collective-permute-start | bytes 1769480 | tf_op jit(solution)/shard_map/ppermute | solution.py:143
  66.9 37.5 %collective-permute-start.15 = (bf16[16,32,1152]{2,1,0:T(8,128)(2,1)S(1)}, bf16[16,32,1152]{2,1,0:T(8,128)(2,1)S(1)}, u32[]{:S(2)}, u32[]{:S(2)}) collective-permute-start(bf16[16,32,1152]{2,1,0:T(8,128)(2,1)S(1)} %constant_dynamic-update-slice_fusion.4.refs_8_), channel_id=1, source_target_pairs={{0,16},{16,32},{32,48},{48,64},{64,80},{80,96},{96,112},{112,128},... | collective-permute-start | bytes 3538952 | tf_op jit(solution)/shard_map/ppermute | solution.py:151
  71.2 33.2 %collective-permute-start.14 = (bf16[16,32,1152]{2,1,0:T(8,128)(2,1)S(1)}, bf16[16,32,1152]{2,1,0:T(8,128)(2,1)S(1)}, u32[]{:S(2)}, u32[]{:S(2)}) collective-permute-start(bf16[16,32,1152]{2,1,0:T(8,128)(2,1)S(1)} %constant_dynamic-update-slice_fusion.4.refs_8_), channel_id=1, source_target_pairs={{0,176},{16,0},{32,16},{48,32},{64,48},{80,64},{96,80},{112,96},{1... | collective-permute-start | bytes 3538952 | tf_op jit(solution)/shard_map/ppermute | solution.py:150
  78.3 19.8 %collective-permute-start.1 = (bf16[256,1152]{1,0:T(8,128)(2,1)S(1)}, bf16[256,1152]{1,0:T(8,128)(2,1)S(1)}, u32[]{:S(2)}, u32[]{:S(2)}) collective-permute-start(bf16[256,1152]{1,0:T(8,128)(2,1)S(1)} %collective-permute-done.refs_1_), channel_id=1, source_target_pairs={{0,14},{2,0},{4,2},{6,4},{8,6},{10,8},{12,10},{14,12},{1,15},{3,1}... | collective-permute-start | bytes 1769480 | tf_op jit(solution)/shard_map/ppermute | solution.py:142
  85.3 17.2 %collective-permute-start.5 = (bf16[256,1152]{1,0:T(8,128)(2,1)S(1)}, bf16[256,1152]{1,0:T(8,128)(2,1)S(1)}, u32[]{:S(2)}, u32[]{:S(2)}) collective-permute-start(bf16[256,1152]{1,0:T(8,128)(2,1)S(1)} %collective-permute-done.4.refs_6_), channel_id=1, source_target_pairs={{0,2},{2,4},{4,6},{6,8},{8,10},{10,12},{12,14},{14,0},{1,3},{3,5},... | collective-permute-start | bytes 1769480 | tf_op jit(solution)/shard_map/ppermute | solution.py:143
  98.1 15.4 %collective-permute-start.2 = (bf16[256,1152]{1,0:T(8,128)(2,1)S(1)}, bf16[256,1152]{1,0:T(8,128)(2,1)S(1)}, u32[]{:S(2)}, u32[]{:S(2)}) collective-permute-start(bf16[256,1152]{1,0:T(8,128)(2,1)S(1)} %collective-permute-done.1.refs_2_), channel_id=1, source_target_pairs={{0,14},{2,0},{4,2},{6,4},{8,6},{10,8},{12,10},{14,12},{1,15},{3,1}... | collective-permute-start | bytes 1769480 | tf_op jit(solution)/shard_map/ppermute | solution.py:142
  102.5 16.0 %collective-permute-start.6 = (bf16[256,1152]{1,0:T(8,128)(2,1)S(1)}, bf16[256,1152]{1,0:T(8,128)(2,1)S(1)}, u32[]{:S(2)}, u32[]{:S(2)}) collective-permute-start(bf16[256,1152]{1,0:T(8,128)(2,1)S(1)} %collective-permute-done.5.refs_5_), channel_id=1, source_target_pairs={{0,2},{2,4},{4,6},{6,8},{8,10},{10,12},{12,14},{14,0},{1,3},{3,5},... | collective-permute-start | bytes 1769480 | tf_op jit(solution)/shard_map/ppermute | solution.py:144
  123.2 0.7 copy-start
  124.0 6.1 %collective-permute-start.16 = (f32[4,96,256]{2,1,0:T(8,128)S(1)}, f32[4,96,256]{2,1,0:T(8,128)S(1)}, u32[]{:S(2)}, u32[]{:S(2)}) collective-permute-start(f32[4,96,256]{2,1,0:T(8,128)S(1)} %get-tuple-element.8), channel_id=1, source_target_pairs={{0,1},{1,0},{2,3},{3,2},{4,5},{5,4},{6,7},{7,6},{8,9},{9,8},{10,11... | collective-permute-start | bytes 1179656 | tf_op jit(solution)/shard_map/ppermute | solution.py:153
  130.1 0.7 copy-start.1

commit v3 on v1

v3 whole, which is shorter than its diff:
```python
import jax
import jax.numpy as jnp
from jax import lax
from jax.experimental import pallas as pl
from jax.experimental.pallas import tpu as pltpu
from jax.sharding import Mesh, PartitionSpec as P

score_scale = 0.015625

NX, NZ, NY, NC = 4, 12, 8, 2
TOK, VLEN = 256, 32
SEQS = 6
ROWS = SEQS * VLEN
HALF = ROWS // 2
COLS = ((0, 256), (256, 512), (512, 896), (896, 1152))
WIDTH = 1152
MIB = 1024 * 1024

ANY = pl.BlockSpec(memory_space=pl.ANY)
VMEM = pl.BlockSpec(memory_space=pltpu.VMEM)
SMEM = pl.BlockSpec(memory_space=pltpu.SMEM)


def deal(shift):
    pairs = []
    for a in range(NY):
        for s in range(NX * NZ):
            x, z = divmod(s, NZ)
            to = x * NZ + (z - shift) % NZ
            pairs.append(((SEQS * a + s % SEQS) * NY + s // SEQS, to * NY + a))
    return pairs


def around(size, shift):
    return [(i, (i + shift) % size) for i in range(size)]


def join_kernel(tx, ta, tq, to, vx, va, vq, vo, train, val, sems):
    copies = []
    for i, (t, v, (lo, hi)) in enumerate(zip((tx, ta, tq, to), (vx, va, vq, vo), COLS)):
        copies.append(pltpu.make_async_copy(t, train.at[:, lo:hi], sems.at[2 * i]))
        copies.append(pltpu.make_async_copy(v.at[0], val.at[:, lo:hi], sems.at[2 * i + 1]))
    for c in copies:
        c.start()
    for c in copies:
        c.wait()


def join(*arrays):
    return pl.pallas_call(
        join_kernel,
        out_shape=(
            jax.ShapeDtypeStruct((TOK, WIDTH), jnp.bfloat16),
            jax.ShapeDtypeStruct((VLEN, WIDTH), jnp.bfloat16),
        ),
        in_specs=[ANY] * 8,
        out_specs=(ANY, ANY),
        scratch_shapes=[pltpu.SemaphoreType.DMA((8,))],
        compiler_params=pltpu.CompilerParams(vmem_limit_bytes=60 * MIB),
    )(*arrays)


def gram_kernel(train, c0, c1, u0, u1, d0, d1, mine, send, tbuf, vbuf, tsem, vsem):
    x, z = lax.axis_index("x"), lax.axis_index("z")
    core = lax.axis_index("core")
    vcopy = []
    for i, (near, rest) in enumerate(((c0, c1), (u0, u1), (d0, d1))):
        vcopy.append(pltpu.make_async_copy(near, vbuf.at[i, 0:4], vsem.at[2 * i]))
        vcopy.append(pltpu.make_async_copy(rest, vbuf.at[i, 4:16], vsem.at[2 * i + 1]))
    tcopy = [
        pltpu.make_async_copy(train.at[b], tbuf.at[b], tsem.at[b]) for b in range(NY)
    ]
    for c in vcopy + tcopy:
        c.start()
    for c in vcopy:
        c.wait()

    def place(b, i):
        r = i % 3 + 3 * (core if i >= 3 else 1 - core)
        s = SEQS * b + r
        dx = lax.rem(s // NZ - x + NX, NX)
        dz = lax.rem(lax.rem(s, NZ) - z + NZ, NZ)
        kind = lax.rem(dz, 3)
        step = jnp.where(kind == 2, lax.rem((dz + 1) // 3, 4), dz // 3)
        return kind, dx * 4 + step

    places = [[place(b, i) for i in range(SEQS)] for b in range(NY)]
    for g, (lo, hi) in enumerate(COLS):
        acc = None
        for b in range(NY):
            if g == 0:
                tcopy[b].wait()
            v = jnp.concatenate([vbuf[p, q, :, lo:hi] for p, q in places[b]])
            d = lax.dot_general(
                v,
                tbuf[b, :, lo:hi],
                (((1,), (1,)), ((), ())),
                preferred_element_type=jnp.float32,
            )
            acc = d if acc is None else acc + d
        send[g] = acc[:HALF]
        mine[g] = acc[HALF:]


def grams(*arrays):
    half = jax.ShapeDtypeStruct((4, HALF, TOK), jnp.float32)
    return pl.pallas_call(
        gram_kernel,
        out_shape=(half, half),
        in_specs=[ANY] * 7,
        out_specs=(VMEM, VMEM),
        scratch_shapes=[
            pltpu.VMEM((NY, TOK, WIDTH), jnp.bfloat16),
            pltpu.VMEM((3, 16, VLEN, WIDTH), jnp.bfloat16),
            pltpu.SemaphoreType.DMA((NY,)),
            pltpu.SemaphoreType.DMA((6,)),
        ],
        compiler_params=pltpu.CompilerParams(vmem_limit_bytes=GRAM_MIB * MIB),
    )(*arrays)


GRAM_MIB = 56


def score_kernel(tl, vl, mine, other, out):
    first = 3 * (2 * lax.axis_index("y") + lax.axis_index("core"))
    g = mine[...] + other[...]
    contrib = g[0] * g[2] + g[1] * g[3]
    places = lax.broadcasted_iota(jnp.int32, (VLEN, TOK), 0)
    tokens = lax.broadcasted_iota(jnp.int32, (1, TOK), 1)
    rows = lax.broadcasted_iota(jnp.int32, (4, 3), 0)
    cols = lax.broadcasted_iota(jnp.int32, (4, 3), 1)
    result = jnp.zeros((4, 3), jnp.float32)
    for s in range(3):
        block = contrib[s * VLEN : (s + 1) * VLEN]
        per_token = jnp.sum(
            jnp.where(places < vl[first + s], block, 0.0), axis=0, keepdims=True
        )
        start = jnp.int32(0)
        for k in range(4):
            end = start + tl[0, k]
            inside = (tokens >= start) & (tokens < end)
            total = jnp.sum(
                jnp.where(inside, per_token, 0.0), axis=1, keepdims=True
            )
            result = jnp.where((rows == k) & (cols == s), total, result)
            start = end
    out[...] = result * score_scale


def scores_of(tl, vl, mine, other):
    return pl.pallas_call(
        score_kernel,
        out_shape=jax.ShapeDtypeStruct((4, 3), jnp.float32),
        in_specs=[SMEM, SMEM, VMEM, VMEM],
        out_specs=VMEM,
        compiler_params=pltpu.CompilerParams(vmem_limit_bytes=16 * MIB),
    )(tl, vl, mine, other)


def local(tx, ta, tq, to, tl, vx, va, vq, vo, vl):
    train, val = join(tx, ta, tq, to, vx, va, vq, vo)
    full = lax.all_gather(train, "y", axis=0, tiled=False)
    c0 = jnp.stack([lax.ppermute(val, ("x", "z", "y"), deal(3 * k)) for k in range(4)])
    aside = [lax.ppermute(c0, "x", around(NX, -d)) for d in (1, 2, 3)]
    u0 = lax.ppermute(c0, "z", around(NZ, -1))
    d0 = lax.ppermute(c0, "z", around(NZ, 1))
    *aside, u0, d0 = lax.optimization_barrier((*aside, u0, d0))
    c1 = jnp.concatenate(aside)
    u1 = lax.ppermute(c1, "z", around(NZ, -1))
    d1 = lax.ppermute(c1, "z", around(NZ, 1))
    mine, send = grams(full, c0, c1, u0, u1, d0, d1)
    other = lax.ppermute(send, "core", [(0, 1), (1, 0)])
    return scores_of(tl, vl, mine, other)


def solution(mesh):
    fine = Mesh(mesh.devices.reshape(NX, NZ, NY, NC), ("x", "z", "y", "core"))
    dp, fsdp = ("x", "z"), ("y", "core")
    in_specs = (
        (P(dp, fsdp),) * 4 + (P(dp, None),) + (P(dp, None, fsdp),) * 4 + (P(),)
    )
    return jax.shard_map(
        local, mesh=fine, in_specs=in_specs, out_specs=P(dp, fsdp), check_vma=False
    )
```

time: 124 us -> 157 us (1.27)
  the two profiles are of different devices: /device:TPU:1 before, /device:TPU:11 now
where the time goes in v3:
time: 157 us
  starting transfers between devices  66.5 us (42%)
  waiting for transfers between devices  45.3 us (29%)
  Pallas kernels  29 us (18%)
  between operations  13.6 us (9%)
  local copies, waits for them, and re-layouts  2.01 us (1%)
    ppermute x4, starting transfers between devices, local(): lax.ppermute(val, ('x', 'z', 'y'), deal(3 * k))  29.2 us
    pallas_call x1, Pallas kernels, join(): pl.pallas_call(join_kernel, out_shape=(jax.ShapeDtypeStruct((TOK, WIDTH),...  21.3 us
    ppermute x3, starting transfers between devices, local(): aside = [lax.ppermute(c0, 'x', around(NX, -d)) for d in (1, 2, 3)]  20.3 us
    ppermute x1, waiting for transfers between devices, local(): d1 = lax.ppermute(c1, 'z', around(NZ, 1))  17.3 us
    ppermute x3, waiting for transfers between devices, local(): aside = [lax.ppermute(c0, 'x', around(NX, -d)) for d in (1, 2, 3)]  13 us
    ppermute x4, waiting for transfers between devices, local(): lax.ppermute(val, ('x', 'z', 'y'), deal(3 * k))  11.6 us
    pallas_call x1, Pallas kernels, grams(): pl.pallas_call(gram_kernel, out_shape=(half, half), in_specs=[ANY] * 7, o...  6.49 us
    ppermute x1, starting transfers between devices, local(): d0 = lax.ppermute(c0, 'z', around(NZ, 1))  5.05 us
  transfers between devices with their start and end apart: 13, of which 7 were waited for; matrix products, arithmetic and copies ran while one was open for 0% of the time, Pallas kernels for 0%

profile of v3, /device:TPU:11, one launch (start us, length us, event | category | flops | bytes accessed | tf_op | source)
XLA Modules:
  0.0 156.5 jit_solution(5307950915516951399)
XLA Ops:
  6.5 0.0 all-gather.3.cloned.1.call-start
  6.5 21.3 %shard_map.100 = (bf16[256,1152]{1,0:T(8,128)(2,1)}, bf16[32,1152]{1,0:T(8,128)(2,1)}) custom-call(bf16[256,256]{1,0:T(8,128)(2,1)} %tx.1, bf16[256,256]{1,0:T(8,128)(2,1)} %ta.1, bf16[256,384]{1,0:T(8,128)(2,1)} %tq.1, bf16[256,256]{1,0:T(8,128)(2,1)} %to.1, bf16[1,32,256]{2,1,0:T(8,128)(2,1)} %vx.1, bf16[1,32,256]{2,1,0:T(8,128)(2,1)} %va.1, ...), custom_call_target="tpu_custom_call" | custom-call | tf_op jit(solution)/shard_map/pallas_call | solution.py:50
  27.8 0.0 all-gather.3.cloned.1.call-update
  27.8 15.3 %collective-permute-start.3 = (bf16[32,1152]{1,0:T(8,128)(2,1)}, bf16[32,1152]{1,0:T(8,128)(2,1)S(1)}, u32[]{:S(2)}, u32[]{:S(2)}) collective-permute-start(bf16[32,1152]{1,0:T(8,128)(2,1)} %get-tuple-element.15), channel_id=1, source_target_pairs={{0,48},{16,64},{32,80},{48,96},{64,112},{80,128},{2,144},{18,160},... | collective-permute-start | bytes 221192 | tf_op jit(solution)/shard_map/ppermute | solution.py:164
  43.1 1.9 %collective-permute-start.2 = (bf16[32,1152]{1,0:T(8,128)(2,1)}, bf16[32,1152]{1,0:T(8,128)(2,1)S(1)}, u32[]{:S(2)}, u32[]{:S(2)}) collective-permute-start(bf16[32,1152]{1,0:T(8,128)(2,1)} %get-tuple-element.15), channel_id=1, source_target_pairs={{0,96},{16,112},{32,128},{48,144},{64,160},{80,176},{2,0},{18,16},... | collective-permute-start | bytes 221192 | tf_op jit(solution)/shard_map/ppermute | solution.py:164
  45.0 10.0 %collective-permute-start.1 = (bf16[32,1152]{1,0:T(8,128)(2,1)}, bf16[32,1152]{1,0:T(8,128)(2,1)S(1)}, u32[]{:S(2)}, u32[]{:S(2)}) collective-permute-start(bf16[32,1152]{1,0:T(8,128)(2,1)} %get-tuple-element.15), channel_id=1, source_target_pairs={{0,144},{16,160},{32,176},{48,0},{64,16},{80,32},{2,48},{18,64},{3... | collective-permute-start | bytes 221192 | tf_op jit(solution)/shard_map/ppermute | solution.py:164
  55.1 1.9 %collective-permute-start = (bf16[32,1152]{1,0:T(8,128)(2,1)}, bf16[32,1152]{1,0:T(8,128)(2,1)S(1)}, u32[]{:S(2)}, u32[]{:S(2)}) collective-permute-start(bf16[32,1152]{1,0:T(8,128)(2,1)} %get-tuple-element.15), channel_id=1, source_target_pairs={{0,0},{16,16},{32,32},{48,48},{64,64},{80,80},{2,96},{18,112},{34,... | collective-permute-start | bytes 221192 | tf_op jit(solution)/shard_map/ppermute | solution.py:164
  57.0 0.0 collective-permute-done.3
  57.0 1.3 collective-permute-done.2
  58.3 0.0 collective-permute-done.1
  58.3 10.4 %collective-permute-done = bf16[32,1152]{1,0:T(8,128)(2,1)S(1)} collective-permute-done((bf16[32,1152]{1,0:T(8,128)(2,1)}, bf16[32,1152]{1,0:T(8,128)(2,1)S(1)}, u32[]{:S(2)}, u32[]{:S(2)}) %collective-permute-start) | collective-permute-done | bytes 73760 | tf_op jit(solution)/shard_map/ppermute | solution.py:164
  68.7 0.0 copy-start.4
  68.7 5.0 %collective-permute-start.8 = (bf16[4,32,1152]{2,1,0:T(8,128)(2,1)S(1)}, bf16[4,32,1152]{2,1,0:T(8,128)(2,1)S(1)}, u32[]{:S(2)}, u32[]{:S(2)}) collective-permute-start(bf16[4,32,1152]{2,1,0:T(8,128)(2,1)S(1)} %pad_maximum_fusion.c0), channel_id=1, source_target_pairs={{0,16},{16,32},{32,48},{48,64},{64,80},{80,96},{96,112},{112,128},... | collective-permute-start | bytes 884744 | tf_op jit(solution)/shard_map/ppermute | solution.py:167
  73.8 1.9 %collective-permute-start.7 = (bf16[4,32,1152]{2,1,0:T(8,128)(2,1)S(1)}, bf16[4,32,1152]{2,1,0:T(8,128)(2,1)S(1)}, u32[]{:S(2)}, u32[]{:S(2)}) collective-permute-start(bf16[4,32,1152]{2,1,0:T(8,128)(2,1)S(1)} %pad_maximum_fusion.c0), channel_id=1, source_target_pairs={{0,176},{16,0},{32,16},{48,32},{64,48},{80,64},{96,80},{112,96},{1... | collective-permute-start | bytes 884744 | tf_op jit(solution)/shard_map/ppermute | solution.py:166
  75.7 14.7 %collective-permute-start.6 = (bf16[4,32,1152]{2,1,0:T(8,128)(2,1)S(1)}, bf16[4,32,1152]{2,1,0:T(8,128)(2,1)S(1)}, u32[]{:S(2)}, u32[]{:S(2)}) collective-permute-start(bf16[4,32,1152]{2,1,0:T(8,128)(2,1)S(1)} %pad_maximum_fusion.c0), channel_id=1, source_target_pairs={{0,192},{192,384},{384,576},{576,0},{1,193},{193,385},{385,577},{5... | collective-permute-start | bytes 884744 | tf_op jit(solution)/shard_map/ppermute | solution.py:165
  90.4 1.9 %collective-permute-start.5 = (bf16[4,32,1152]{2,1,0:T(8,128)(2,1)S(1)}, bf16[4,32,1152]{2,1,0:T(8,128)(2,1)S(1)}, u32[]{:S(2)}, u32[]{:S(2)}) collective-permute-start(bf16[4,32,1152]{2,1,0:T(8,128)(2,1)S(1)} %pad_maximum_fusion.c0), channel_id=1, source_target_pairs={{0,384},{192,576},{384,0},{576,192},{1,385},{193,577},{385,1},{577... | collective-permute-start | bytes 884744 | tf_op jit(solution)/shard_map/ppermute | solution.py:165
  92.3 3.7 %collective-permute-start.4 = (bf16[4,32,1152]{2,1,0:T(8,128)(2,1)S(1)}, bf16[4,32,1152]{2,1,0:T(8,128)(2,1)S(1)}, u32[]{:S(2)}, u32[]{:S(2)}) collective-permute-start(bf16[4,32,1152]{2,1,0:T(8,128)(2,1)S(1)} %pad_maximum_fusion.c0), channel_id=1, source_target_pairs={{0,576},{192,0},{384,192},{576,384},{1,577},{193,1},{385,193},{577... | collective-permute-start | bytes 884744 | tf_op jit(solution)/shard_map/ppermute | solution.py:165
  96.1 0.0 collective-permute-done.8.d0
  96.1 0.0 copy-start.7
  96.1 0.0 collective-permute-done.7.u0
  96.1 0.0 copy-start.8
  96.1 5.1 %collective-permute-done.6 = bf16[4,32,1152]{2,1,0:T(8,128)(2,1)S(1)} collective-permute-done((bf16[4,32,1152]{2,1,0:T(8,128)(2,1)S(1)}, bf16[4,32,1152]{2,1,0:T(8,128)(2,1)S(1)}, u32[]{:S(2)}, u32[]{:S(2)}) %collective-permute-start.6) | collective-permute-done | bytes 294944 | tf_op jit(solution)/shard_map/ppermute | solution.py:165
  101.2 0.0 collective-permute-done.5
  101.2 7.8 %collective-permute-done.4 = bf16[4,32,1152]{2,1,0:T(8,128)(2,1)S(1)} collective-permute-done((bf16[4,32,1152]{2,1,0:T(8,128)(2,1)S(1)}, bf16[4,32,1152]{2,1,0:T(8,128)(2,1)S(1)}, u32[]{:S(2)}, u32[]{:S(2)}) %collective-permute-start.4) | collective-permute-done | bytes 294944 | tf_op jit(solution)/shard_map/ppermute | solution.py:165
  109.1 0.0 copy-start.1
  109.1 0.0 copy-start.2
  109.2 0.0 copy-start.3
  109.2 3.4 %collective-permute-start.10 = (bf16[12,32,1152]{2,1,0:T(8,128)(2,1)S(1)}, bf16[12,32,1152]{2,1,0:T(8,128)(2,1)S(1)}, u32[]{:S(2)}, u32[]{:S(2)}) collective-permute-start(bf16[12,32,1152]{2,1,0:T(8,128)(2,1)S(1)} %constant_dynamic-update-slice_fusion.c1), channel_id=1, source_target_pairs={{0,16},{16,32},{32,48},{48,64},{64,80},{80,96},{96,112},{112,128},... | collective-permute-start | bytes 2654216 | tf_op jit(solution)/shard_map/ppermute | solution.py:171
  112.6 3.1 %collective-permute-start.9 = (bf16[12,32,1152]{2,1,0:T(8,128)(2,1)S(1)}, bf16[12,32,1152]{2,1,0:T(8,128)(2,1)S(1)}, u32[]{:S(2)}, u32[]{:S(2)}) collective-permute-start(bf16[12,32,1152]{2,1,0:T(8,128)(2,1)S(1)} %constant_dynamic-update-slice_fusion.c1), channel_id=1, source_target_pairs={{0,176},{16,0},{32,16},{48,32},{64,48},{80,64},{96,80},{112,96},{1... | collective-permute-start | bytes 2654216 | tf_op jit(solution)/shard_map/ppermute | solution.py:170
  115.7 17.3 %collective-permute-done.10.d1 = bf16[12,32,1152]{2,1,0:T(8,128)(2,1)S(1)} collective-permute-done((bf16[12,32,1152]{2,1,0:T(8,128)(2,1)S(1)}, bf16[12,32,1152]{2,1,0:T(8,128)(2,1)S(1)}, u32[]{:S(2)}, u32[]{:S(2)}) %collective-permute-start.10) | collective-permute-done | bytes 884768 | tf_op jit(solution)/shard_map/ppermute | solution.py:171
  133.0 0.0 copy-start.5
  133.0 1.8 %collective-permute-done.9.u1 = bf16[12,32,1152]{2,1,0:T(8,128)(2,1)S(1)} collective-permute-done((bf16[12,32,1152]{2,1,0:T(8,128)(2,1)S(1)}, bf16[12,32,1152]{2,1,0:T(8,128)(2,1)S(1)}, u32[]{:S(2)}, u32[]{:S(2)}) %collective-permute-start.9) | collective-permute-done | bytes 884768 | tf_op jit(solution)/shard_map/ppermute | solution.py:170
  134.9 0.0 copy-start.6
  134.9 0.0 all-gather.3.cloned.1.call-done
  134.9 0.0 copy-done.4
  134.9 0.0 copy-done.7
  134.9 0.0 copy-done.8
  134.9 0.0 copy-done.3
  134.9 0.0 copy-done.5
  134.9 0.9 copy-done.6
  135.8 6.5 %shard_map.101 = (f32[4,96,256]{2,1,0:T(8,128)}, f32[4,96,256]{2,1,0:T(8,128)}) custom-call(bf16[8,256,1152]{2,1,0:T(8,128)(2,1)} %bitcast.5, bf16[4,32,1152]{2,1,0:T(8,128)(2,1)} %copy-done.4, bf16[12,32,1152]{2,1,0:T(8,128)(2,1)} %copy-done.3, bf16[4,32,1152]{2,1,0:T(8,128)(2,1)} %copy-done.8, bf16[12,32,1152]{2,1,0:T(8,128)(2,1)} %copy-done.6, ...), custom_call_target="tpu_custom_call" | custom-call | tf_op jit(solution)/shard_map/pallas_call | solution.py:107
  142.3 3.6 %collective-permute-start.11 = (f32[4,96,256]{2,1,0:T(8,128)}, f32[4,96,256]{2,1,0:T(8,128)S(1)}, u32[]{:S(2)}, u32[]{:S(2)}) collective-permute-start(f32[4,96,256]{2,1,0:T(8,128)} %get-tuple-element.22), channel_id=1, source_target_pairs={{0,1},{1,0},{2,3},{3,2},{4,5},{5,4},{6,7},{7,6},{8,9},{9,8},{10,11... | collective-permute-start | bytes 1179656 | tf_op jit(solution)/shard_map/ppermute | solution.py:173
  145.9 1.5 collective-permute-done.11.other
  147.4 0.0 copy-done.1
  147.4 0.0 copy-done.2
  147.4 0.0 copy-start
  147.4 1.0 copy-done
  148.4 1.3 shard_map.102
  (4 shorter events, 0.1 us)
Async XLA Ops:
  6.5 128.3 %all-gather.3.cloned.1.call-start = ((), (), s32[]{:S(2)}) async-start(), calls=%async_computation | async-start | bytes 5308416 | tf_op jit(solution)/shard_map/all_gather | solution.py:163
  27.8 29.2 %collective-permute-start.3 = (bf16[32,1152]{1,0:T(8,128)(2,1)}, bf16[32,1152]{1,0:T(8,128)(2,1)S(1)}, u32[]{:S(2)}, u32[]{:S(2)}) collective-permute-start(bf16[32,1152]{1,0:T(8,128)(2,1)} %get-tuple-element.15), channel_id=1, source_target_pairs={{0,48},{16,64},{32,80},{48,96},{64,112},{80,128},{2,144},{18,160},... | collective-permute-start | bytes 221192 | tf_op jit(solution)/shard_map/ppermute | solution.py:164
  43.1 15.2 %collective-permute-start.2 = (bf16[32,1152]{1,0:T(8,128)(2,1)}, bf16[32,1152]{1,0:T(8,128)(2,1)S(1)}, u32[]{:S(2)}, u32[]{:S(2)}) collective-permute-start(bf16[32,1152]{1,0:T(8,128)(2,1)} %get-tuple-element.15), channel_id=1, source_target_pairs={{0,96},{16,112},{32,128},{48,144},{64,160},{80,176},{2,0},{18,16},... | collective-permute-start | bytes 221192 | tf_op jit(solution)/shard_map/ppermute | solution.py:164
  45.0 13.3 %collective-permute-start.1 = (bf16[32,1152]{1,0:T(8,128)(2,1)}, bf16[32,1152]{1,0:T(8,128)(2,1)S(1)}, u32[]{:S(2)}, u32[]{:S(2)}) collective-permute-start(bf16[32,1152]{1,0:T(8,128)(2,1)} %get-tuple-element.15), channel_id=1, source_target_pairs={{0,144},{16,160},{32,176},{48,0},{64,16},{80,32},{2,48},{18,64},{3... | collective-permute-start | bytes 221192 | tf_op jit(solution)/shard_map/ppermute | solution.py:164
  55.1 13.6 %collective-permute-start = (bf16[32,1152]{1,0:T(8,128)(2,1)}, bf16[32,1152]{1,0:T(8,128)(2,1)S(1)}, u32[]{:S(2)}, u32[]{:S(2)}) collective-permute-start(bf16[32,1152]{1,0:T(8,128)(2,1)} %get-tuple-element.15), channel_id=1, source_target_pairs={{0,0},{16,16},{32,32},{48,48},{64,64},{80,80},{2,96},{18,112},{34,... | collective-permute-start | bytes 221192 | tf_op jit(solution)/shard_map/ppermute | solution.py:164
  68.7 66.1 %copy-start.4 = (bf16[4,32,1152]{2,1,0:T(8,128)(2,1)}, bf16[4,32,1152]{2,1,0:T(8,128)(2,1)S(1)}, u32[]{:S(2)}) copy-start(bf16[4,32,1152]{2,1,0:T(8,128)(2,1)S(1)} %pad_maximum_fusion.c0) | copy-start | bytes 884740
  68.7 27.3 %collective-permute-start.8 = (bf16[4,32,1152]{2,1,0:T(8,128)(2,1)S(1)}, bf16[4,32,1152]{2,1,0:T(8,128)(2,1)S(1)}, u32[]{:S(2)}, u32[]{:S(2)}) collective-permute-start(bf16[4,32,1152]{2,1,0:T(8,128)(2,1)S(1)} %pad_maximum_fusion.c0), channel_id=1, source_target_pairs={{0,16},{16,32},{32,48},{48,64},{64,80},{80,96},{96,112},{112,128},... | collective-permute-start | bytes 884744 | tf_op jit(solution)/shard_map/ppermute | solution.py:167
  73.8 22.3 %collective-permute-start.7 = (bf16[4,32,1152]{2,1,0:T(8,128)(2,1)S(1)}, bf16[4,32,1152]{2,1,0:T(8,128)(2,1)S(1)}, u32[]{:S(2)}, u32[]{:S(2)}) collective-permute-start(bf16[4,32,1152]{2,1,0:T(8,128)(2,1)S(1)} %pad_maximum_fusion.c0), channel_id=1, source_target_pairs={{0,176},{16,0},{32,16},{48,32},{64,48},{80,64},{96,80},{112,96},{1... | collective-permute-start | bytes 884744 | tf_op jit(solution)/shard_map/ppermute | solution.py:166
  75.7 25.5 %collective-permute-start.6 = (bf16[4,32,1152]{2,1,0:T(8,128)(2,1)S(1)}, bf16[4,32,1152]{2,1,0:T(8,128)(2,1)S(1)}, u32[]{:S(2)}, u32[]{:S(2)}) collective-permute-start(bf16[4,32,1152]{2,1,0:T(8,128)(2,1)S(1)} %pad_maximum_fusion.c0), channel_id=1, source_target_pairs={{0,192},{192,384},{384,576},{576,0},{1,193},{193,385},{385,577},{5... | collective-permute-start | bytes 884744 | tf_op jit(solution)/shard_map/ppermute | solution.py:165
  90.4 10.8 %collective-permute-start.5 = (bf16[4,32,1152]{2,1,0:T(8,128)(2,1)S(1)}, bf16[4,32,1152]{2,1,0:T(8,128)(2,1)S(1)}, u32[]{:S(2)}, u32[]{:S(2)}) collective-permute-start(bf16[4,32,1152]{2,1,0:T(8,128)(2,1)S(1)} %pad_maximum_fusion.c0), channel_id=1, source_target_pairs={{0,384},{192,576},{384,0},{576,192},{1,385},{193,577},{385,1},{577... | collective-permute-start | bytes 884744 | tf_op jit(solution)/shard_map/ppermute | solution.py:165
  92.3 16.7 %collective-permute-start.4 = (bf16[4,32,1152]{2,1,0:T(8,128)(2,1)S(1)}, bf16[4,32,1152]{2,1,0:T(8,128)(2,1)S(1)}, u32[]{:S(2)}, u32[]{:S(2)}) collective-permute-start(bf16[4,32,1152]{2,1,0:T(8,128)(2,1)S(1)} %pad_maximum_fusion.c0), channel_id=1, source_target_pairs={{0,576},{192,0},{384,192},{576,384},{1,577},{193,1},{385,193},{577... | collective-permute-start | bytes 884744 | tf_op jit(solution)/shard_map/ppermute | solution.py:165
  96.1 38.8 %copy-start.7 = (bf16[4,32,1152]{2,1,0:T(8,128)(2,1)}, bf16[4,32,1152]{2,1,0:T(8,128)(2,1)S(1)}, u32[]{:S(2)}) copy-start(bf16[4,32,1152]{2,1,0:T(8,128)(2,1)S(1)} %collective-permute-done.8.d0) | copy-start | bytes 884740
  96.1 38.8 %copy-start.8 = (bf16[4,32,1152]{2,1,0:T(8,128)(2,1)}, bf16[4,32,1152]{2,1,0:T(8,128)(2,1)S(1)}, u32[]{:S(2)}) copy-start(bf16[4,32,1152]{2,1,0:T(8,128)(2,1)S(1)} %collective-permute-done.7.u0) | copy-start | bytes 884740
  109.1 38.3 %copy-start.1 = (s32[1,4]{1,0:T(1,128)S(1)}, s32[1,4]{1,0:T(1,128)}, u32[]{:S(2)}) copy-start(s32[1,4]{1,0:T(1,128)} %tl.1) | copy-start | bytes 52
  109.1 38.3 %copy-start.2 = (s32[48]{0:T(128)S(1)}, s32[48]{0:T(128)}, u32[]{:S(2)}) copy-start(s32[48]{0:T(128)} %vl.1) | copy-start | bytes 580
  109.2 25.7 %copy-start.3 = (bf16[12,32,1152]{2,1,0:T(8,128)(2,1)}, bf16[12,32,1152]{2,1,0:T(8,128)(2,1)S(1)}, u32[]{:S(2)}) copy-start(bf16[12,32,1152]{2,1,0:T(8,128)(2,1)S(1)} %constant_dynamic-update-slice_fusion.c1) | copy-start | bytes 2654212
  109.2 23.8 %collective-permute-start.10 = (bf16[12,32,1152]{2,1,0:T(8,128)(2,1)S(1)}, bf16[12,32,1152]{2,1,0:T(8,128)(2,1)S(1)}, u32[]{:S(2)}, u32[]{:S(2)}) collective-permute-start(bf16[12,32,1152]{2,1,0:T(8,128)(2,1)S(1)} %constant_dynamic-update-slice_fusion.c1), channel_id=1, source_target_pairs={{0,16},{16,32},{32,48},{48,64},{64,80},{80,96},{96,112},{112,128},... | collective-permute-start | bytes 2654216 | tf_op jit(solution)/shard_map/ppermute | solution.py:171
  112.6 22.3 %collective-permute-start.9 = (bf16[12,32,1152]{2,1,0:T(8,128)(2,1)S(1)}, bf16[12,32,1152]{2,1,0:T(8,128)(2,1)S(1)}, u32[]{:S(2)}, u32[]{:S(2)}) collective-permute-start(bf16[12,32,1152]{2,1,0:T(8,128)(2,1)S(1)} %constant_dynamic-update-slice_fusion.c1), channel_id=1, source_target_pairs={{0,176},{16,0},{32,16},{48,32},{64,48},{80,64},{96,80},{112,96},{1... | collective-permute-start | bytes 2654216 | tf_op jit(solution)/shard_map/ppermute | solution.py:170
  133.0 1.9 %copy-start.5 = (bf16[12,32,1152]{2,1,0:T(8,128)(2,1)}, bf16[12,32,1152]{2,1,0:T(8,128)(2,1)S(1)}, u32[]{:S(2)}) copy-start(bf16[12,32,1152]{2,1,0:T(8,128)(2,1)S(1)} %collective-permute-done.10.d1) | copy-start | bytes 2654212
  134.9 0.9 copy-start.6
  142.3 5.1 %collective-permute-start.11 = (f32[4,96,256]{2,1,0:T(8,128)}, f32[4,96,256]{2,1,0:T(8,128)S(1)}, u32[]{:S(2)}, u32[]{:S(2)}) collective-permute-start(f32[4,96,256]{2,1,0:T(8,128)} %get-tuple-element.22), channel_id=1, source_target_pairs={{0,1},{1,0},{2,3},{3,2},{4,5},{5,4},{6,7},{7,6},{8,9},{9,8},{10,11... | collective-permute-start | bytes 1179656 | tf_op jit(solution)/shard_map/ppermute | solution.py:173
  147.4 1.0 copy-start
Sparse Core Ops, SparseCore 0:
  28.0 80.9 all-gather.2

commit v4 on v1

v4 whole, which is shorter than its diff:
```python
import jax
import jax.numpy as jnp
from jax import lax
from jax.experimental import pallas as pl
from jax.experimental.pallas import tpu as pltpu
from jax.sharding import Mesh, PartitionSpec as P

score_scale = 0.015625

NX, NZ, NY, NC = 4, 12, 8, 2
TOK, VLEN = 256, 32
SEQS = 6
ROWS = SEQS * VLEN
HALF = ROWS // 2
COLS = ((0, 256), (256, 512), (512, 896), (896, 1152))
WIDTH = 1152
MIB = 1024 * 1024

ANY = pl.BlockSpec(memory_space=pl.ANY)
VMEM = pl.BlockSpec(memory_space=pltpu.VMEM)
SMEM = pl.BlockSpec(memory_space=pltpu.SMEM)


SWAP = [
    ((SEQS * a + r) * NY + b, (SEQS * b + r) * NY + a)
    for a in range(NY)
    for b in range(NY)
    for r in range(SEQS)
]


def around(size, shift):
    return [(i, (i + shift) % size) for i in range(size)]


def join_kernel(tx, ta, tq, to, vx, va, vq, vo, train, val):
    for t, v, (lo, hi) in zip((tx, ta, tq, to), (vx, va, vq, vo), COLS):
        train[:, lo:hi] = t[...]
        val[:, lo:hi] = v[0]


def join(*arrays):
    return pl.pallas_call(
        join_kernel,
        out_shape=(
            jax.ShapeDtypeStruct((TOK, WIDTH), jnp.bfloat16),
            jax.ShapeDtypeStruct((VLEN, WIDTH), jnp.bfloat16),
        ),
        in_specs=[VMEM] * 8,
        out_specs=(VMEM, VMEM),
        compiler_params=pltpu.CompilerParams(vmem_limit_bytes=60 * MIB),
    )(*arrays)


def gram_kernel(train, own, right, left, far0, far1, mine, send, tbuf, vbuf, tsem, vsem):
    x = lax.axis_index("x")
    first = lax.axis_index("core") == 0
    opposite = lax.rem(x + 2, NX)
    vcopy = [
        pltpu.make_async_copy(src, dst, vsem.at[i])
        for i, (src, dst) in enumerate(
            (
                (own, vbuf.at[x]),
                (right, vbuf.at[lax.rem(x + 1, NX)]),
                (left, vbuf.at[lax.rem(x + 3, NX)]),
                (far0, vbuf.at[opposite, 0:ROWS]),
                (far1, vbuf.at[opposite, ROWS : 2 * ROWS]),
            )
        )
    ]
    tcopy = [
        pltpu.make_async_copy(train.at[:, :, lo:hi], tbuf.at[:, :, lo:hi], tsem.at[g])
        for g, (lo, hi) in enumerate(COLS)
    ]
    for c in (*tcopy, *vcopy):
        c.start()
    for c in vcopy:
        c.wait()
    for g, (lo, hi) in enumerate(COLS):
        tcopy[g].wait()
        acc = jnp.zeros((ROWS, TOK), jnp.float32)
        for b in range(NY):
            acc += lax.dot_general(
                vbuf[b // 2, (b % 2) * ROWS : (b % 2 + 1) * ROWS, lo:hi],
                tbuf[b, :, lo:hi],
                (((1,), (1,)), ((), ())),
                preferred_element_type=jnp.float32,
            )
        send[g] = jnp.where(first, acc[HALF:], acc[:HALF])
        mine[g] = jnp.where(first, acc[:HALF], acc[HALF:])


def grams(*arrays):
    half = jax.ShapeDtypeStruct((4, HALF, TOK), jnp.float32)
    return pl.pallas_call(
        gram_kernel,
        out_shape=(half, half),
        in_specs=[ANY] * 6,
        out_specs=(VMEM, VMEM),
        scratch_shapes=[
            pltpu.VMEM((NY, TOK, WIDTH), jnp.bfloat16),
            pltpu.VMEM((NX, 2 * ROWS, WIDTH), jnp.bfloat16),
            pltpu.SemaphoreType.DMA((4,)),
            pltpu.SemaphoreType.DMA((5,)),
        ],
        compiler_params=pltpu.CompilerParams(vmem_limit_bytes=GRAM_MIB * MIB),
    )(*arrays)


GRAM_MIB = 50


def score_kernel(tl, vl, mine, other, out):
    first = 3 * (2 * lax.axis_index("y") + lax.axis_index("core"))
    g = mine[...] + other[...]
    contrib = g[0] * g[2] + g[1] * g[3]
    places = lax.broadcasted_iota(jnp.int32, (VLEN, TOK), 0)
    tokens = lax.broadcasted_iota(jnp.int32, (1, TOK), 1)
    rows = lax.broadcasted_iota(jnp.int32, (4, 3), 0)
    cols = lax.broadcasted_iota(jnp.int32, (4, 3), 1)
    result = jnp.zeros((4, 3), jnp.float32)
    for s in range(3):
        block = contrib[s * VLEN : (s + 1) * VLEN]
        per_token = jnp.sum(
            jnp.where(places < vl[first + s], block, 0.0), axis=0, keepdims=True
        )
        start = jnp.int32(0)
        for k in range(4):
            end = start + tl[0, k]
            inside = (tokens >= start) & (tokens < end)
            total = jnp.sum(
                jnp.where(inside, per_token, 0.0), axis=1, keepdims=True
            )
            result = jnp.where((rows == k) & (cols == s), total, result)
            start = end
    out[...] = result * score_scale


def scores_of(tl, vl, mine, other):
    return pl.pallas_call(
        score_kernel,
        out_shape=jax.ShapeDtypeStruct((4, 3), jnp.float32),
        in_specs=[SMEM, SMEM, VMEM, VMEM],
        out_specs=VMEM,
        compiler_params=pltpu.CompilerParams(vmem_limit_bytes=16 * MIB),
    )(tl, vl, mine, other)


def local(tx, ta, tq, to, tl, vx, va, vq, vo, vl):
    train, val = join(tx, ta, tq, to, vx, va, vq, vo)
    full = lax.all_gather(train, "y", axis=0, tiled=False)
    val = lax.ppermute(val, ("x", "z", "y"), SWAP)
    own = lax.all_gather(val, "z", axis=0, tiled=True)
    right = lax.ppermute(own, "x", around(NX, -1))
    left = lax.ppermute(own, "x", around(NX, 1))
    far0 = lax.ppermute(left[:ROWS], "x", around(NX, 1))
    far1 = lax.ppermute(right[ROWS:], "x", around(NX, -1))
    mine, send = grams(full, own, right, left, far0, far1)
    other = lax.ppermute(send, "core", [(0, 1), (1, 0)])
    return scores_of(tl, vl, mine, other)


def solution(mesh):
    fine = Mesh(mesh.devices.reshape(NX, NZ, NY, NC), ("x", "z", "y", "core"))
    dp, fsdp = ("x", "z"), ("y", "core")
    in_specs = (
        (P(dp, fsdp),) * 4 + (P(dp, None),) + (P(dp, None, fsdp),) * 4 + (P(),)
    )
    return jax.shard_map(
        local, mesh=fine, in_specs=in_specs, out_specs=P(dp, fsdp), check_vma=False
    )
```

time: 124 us -> 121 us (0.976)
  local copies, waits for them, and re-layouts: 5.55 us -> 0.09 us
  Pallas kernels: 4.52 us -> 9.22 us
  other arithmetic: 3.23 us -> 0 us
    pallas_call x1 -> x2, Pallas kernels: 2.68 us -> 7.96 us  [the longest x1 5.93 us: grams(): pl.pallas_call(gram_kernel, out_shape=(half, half), in_specs=[ANY] * 6, o...]
    unnamed x14 -> x6, local copies, waits for them, and re-layouts: 3.88 us -> 0.02 us
    concatenate x3 -> x0, other arithmetic: 3.23 us -> none  [the longest x1 2 us: local(): train = jnp.concatenate((tx, ta, tq, to), axis=1)]
  transfers between devices with their start and end apart: 7 -> 7, of which waited for: 5 -> 5; matrix products, arithmetic and copies ran while one was open for 2% -> 0% of each run, Pallas kernels for 0% -> 0%
where the time goes in v4:
time: 121 us; the launch traced here: 119 us
  blocking collectives  48.7 us (40%)
  starting transfers between devices  24.2 us (20%)
  waiting for transfers between devices  23.5 us (19%)
  between operations  13.5 us (11%)
  Pallas kernels  9.22 us (8%)
    all_gather x1, blocking collectives, local(): own = lax.all_gather(val, 'z', axis=0, tiled=True)  48.7 us
    ppermute x1, waiting for transfers between devices, local(): left = lax.ppermute(own, 'x', around(NX, 1))  14.9 us
    ppermute x1, starting transfers between devices, local(): other = lax.ppermute(send, 'core', [(0, 1), (1, 0)])  6.86 us
    pallas_call x1, Pallas kernels, grams(): pl.pallas_call(gram_kernel, out_shape=(half, half), in_specs=[ANY] * 6, o...  5.93 us
    ppermute x1, starting transfers between devices, local(): left = lax.ppermute(own, 'x', around(NX, 1))  5.82 us
    ppermute x1, waiting for transfers between devices, local(): far0 = lax.ppermute(left[:ROWS], 'x', around(NX, 1))  4.47 us
    ppermute x1, starting transfers between devices, local(): right = lax.ppermute(own, 'x', around(NX, -1))  3.9 us
    ppermute x1, starting transfers between devices, local(): far1 = lax.ppermute(right[ROWS:], 'x', around(NX, -1))  3.05 us
  transfers between devices with their start and end apart: 7, of which 5 were waited for; matrix products, arithmetic and copies ran while one was open for 0% of the time, Pallas kernels for 0%

profile of v4, /device:TPU:1, one launch (start us, length us, event | category | flops | bytes accessed | tf_op | source)
XLA Modules:
  0.0 119.2 jit_solution(4249758091751243918)
XLA Ops:
  6.5 0.0 all-gather.3.cloned.1.call-start
  6.5 2.0 %shard_map.100 = (bf16[256,1152]{1,0:T(8,128)(2,1)}, bf16[32,1152]{1,0:T(8,128)(2,1)}) custom-call(bf16[256,256]{1,0:T(8,128)(2,1)} %tx.1, bf16[256,256]{1,0:T(8,128)(2,1)} %ta.1, bf16[256,384]{1,0:T(8,128)(2,1)} %tq.1, bf16[256,256]{1,0:T(8,128)(2,1)} %to.1, bf16[1,32,256]{2,1,0:T(8,128)(2,1)} %vx.1, bf16[1,32,256]{2,1,0:T(8,128)(2,1)} %va.1, ...), custom_call_target="tpu_custom_call" | custom-call | tf_op jit(solution)/shard_map/pallas_call | solution.py:43
  8.6 0.0 all-gather.3.cloned.1.call-update
  8.6 1.5 %collective-permute-start = (bf16[32,1152]{1,0:T(8,128)(2,1)}, bf16[32,1152]{1,0:T(8,128)(2,1)S(1)}, u32[]{:S(2)}, u32[]{:S(2)}) collective-permute-start(bf16[32,1152]{1,0:T(8,128)(2,1)} %get-tuple-element.10), channel_id=1, source_target_pairs={{0,0},{16,16},{32,32},{48,48},{64,64},{80,80},{2,96},{18,112},{34,... | collective-permute-start | bytes 221192 | tf_op jit(solution)/shard_map/ppermute | solution.py:152
  10.1 0.0 collective-permute-done
  10.1 48.7 %all_gather.11.own = bf16[384,1152]{1,0:T(8,128)(2,1)S(1)} all-gather(bf16[32,1152]{1,0:T(8,128)(2,1)S(1)} %collective-permute-done), channel_id=1, replica_groups=mesh['x'=4,'z'=12,'y'=8,'core'=2] {'z'}, dimensions={0}, use_global_device_ids=true | all-gather | bytes 958464 | tf_op jit(solution)/shard_map/all_gather | solution.py:153
  58.9 5.8 %collective-permute-start.2 = (bf16[384,1152]{1,0:T(8,128)(2,1)S(1)}, bf16[384,1152]{1,0:T(8,128)(2,1)S(1)}, u32[]{:S(2)}, u32[]{:S(2)}) collective-permute-start(bf16[384,1152]{1,0:T(8,128)(2,1)S(1)} %all_gather.11.own), channel_id=1, source_target_pairs={{0,192},{192,384},{384,576},{576,0},{1,193},{193,385},{385,577},{5... | collective-permute-start | bytes 2654216 | tf_op jit(solution)/shard_map/ppermute | solution.py:155
  64.7 3.9 %collective-permute-start.1 = (bf16[384,1152]{1,0:T(8,128)(2,1)S(1)}, bf16[384,1152]{1,0:T(8,128)(2,1)S(1)}, u32[]{:S(2)}, u32[]{:S(2)}) collective-permute-start(bf16[384,1152]{1,0:T(8,128)(2,1)S(1)} %all_gather.11.own), channel_id=1, source_target_pairs={{0,576},{192,0},{384,192},{576,384},{1,577},{193,1},{385,193},{577... | collective-permute-start | bytes 2654216 | tf_op jit(solution)/shard_map/ppermute | solution.py:154
  68.6 14.9 %collective-permute-done.2.left = bf16[384,1152]{1,0:T(8,128)(2,1)S(1)} collective-permute-done((bf16[384,1152]{1,0:T(8,128)(2,1)S(1)}, bf16[384,1152]{1,0:T(8,128)(2,1)S(1)}, u32[]{:S(2)}, u32[]{:S(2)}) %collective-permute-start.2) | collective-permute-done | bytes 884768 | tf_op jit(solution)/shard_map/ppermute | solution.py:155
  83.5 0.0 copy-start.2
  83.6 0.0 copy-start
  83.6 0.0 copy-start.1
  83.6 3.0 %collective-permute-start.3 = (bf16[192,1152]{1,0:T(8,128)(2,1)S(1)}, bf16[192,1152]{1,0:T(8,128)(2,1)S(1)}, u32[]{:S(2)}, u32[]{:S(2)}) collective-permute-start(bf16[192,1152]{1,0:T(8,128)(2,1)S(1)} %slice.8), channel_id=1, source_target_pairs={{0,192},{192,384},{384,576},{576,0},{1,193},{193,385},{385,577},{5... | collective-permute-start | bytes 1327112 | tf_op jit(solution)/shard_map/ppermute | solution.py:156
  86.7 0.6 collective-permute-done.1.right
  87.2 3.0 %collective-permute-start.4 = (bf16[192,1152]{1,0:T(8,128)(2,1)S(1)}, bf16[192,1152]{1,0:T(8,128)(2,1)S(1)}, u32[]{:S(2)}, u32[]{:S(2)}) collective-permute-start(bf16[192,1152]{1,0:T(8,128)(2,1)S(1)} %slice.9), channel_id=1, source_target_pairs={{0,576},{192,0},{384,192},{576,384},{1,577},{193,1},{385,193},{577... | collective-permute-start | bytes 1327112 | tf_op jit(solution)/shard_map/ppermute | solution.py:157
  90.3 4.5 %collective-permute-done.3.far0 = bf16[192,1152]{1,0:T(8,128)(2,1)S(1)} collective-permute-done((bf16[192,1152]{1,0:T(8,128)(2,1)S(1)}, bf16[192,1152]{1,0:T(8,128)(2,1)S(1)}, u32[]{:S(2)}, u32[]{:S(2)}) %collective-permute-start.3) | collective-permute-done | bytes 442400 | tf_op jit(solution)/shard_map/ppermute | solution.py:156
  94.8 2.2 %collective-permute-done.4.far1 = bf16[192,1152]{1,0:T(8,128)(2,1)S(1)} collective-permute-done((bf16[192,1152]{1,0:T(8,128)(2,1)S(1)}, bf16[192,1152]{1,0:T(8,128)(2,1)S(1)}, u32[]{:S(2)}, u32[]{:S(2)}) %collective-permute-start.4) | collective-permute-done | bytes 442400 | tf_op jit(solution)/shard_map/ppermute | solution.py:157
  97.0 0.0 all-gather.3.cloned.1.call-done
  97.0 0.0 copy-done.2
  97.0 5.9 %shard_map.101 = (f32[4,96,256]{2,1,0:T(8,128)S(1)}, f32[4,96,256]{2,1,0:T(8,128)S(1)}) custom-call(bf16[8,256,1152]{2,1,0:T(8,128)(2,1)} %bitcast.1, bf16[384,1152]{1,0:T(8,128)(2,1)S(1)} %all_gather.11.own, bf16[384,1152]{1,0:T(8,128)(2,1)S(1)} %collective-permute-done.1.right, bf16[384,1152]{1,0:T(8,128)(2,1)} %copy-done.2, ...), custom_call_target="tpu_custom_call" | custom-call | tf_op jit(solution)/shard_map/pallas_call | solution.py:95
  102.9 6.9 %collective-permute-start.5 = (f32[4,96,256]{2,1,0:T(8,128)S(1)}, f32[4,96,256]{2,1,0:T(8,128)S(1)}, u32[]{:S(2)}, u32[]{:S(2)}) collective-permute-start(f32[4,96,256]{2,1,0:T(8,128)S(1)} %get-tuple-element.12), channel_id=1, source_target_pairs={{0,1},{1,0},{2,3},{3,2},{4,5},{5,4},{6,7},{7,6},{8,9},{9,8},{10,11... | collective-permute-start | bytes 1179656 | tf_op jit(solution)/shard_map/ppermute | solution.py:159
  109.8 1.3 %collective-permute-done.5.other = f32[4,96,256]{2,1,0:T(8,128)S(1)} collective-permute-done((f32[4,96,256]{2,1,0:T(8,128)S(1)}, f32[4,96,256]{2,1,0:T(8,128)S(1)}, u32[]{:S(2)}, u32[]{:S(2)}) %collective-permute-start.5) | collective-permute-done | bytes 393248 | tf_op jit(solution)/shard_map/ppermute | solution.py:159
  111.1 0.0 copy-done
  111.1 0.0 copy-done.1
  111.1 1.3 %shard_map.102 = f32[4,3]{1,0:T(4,128)} custom-call(s32[1,4]{1,0:T(1,128)S(1)} %copy-done, s32[48]{0:T(128)S(1)} %copy-done.1, f32[4,96,256]{2,1,0:T(8,128)S(1)} %get-tuple-element.11.mine, f32[4,96,256]{2,1,0:T(8,128)S(1)} %collective-permute-done.5.other), custom_call_target="tpu_custom_call" | custom-call | tf_op jit(solution)/shard_map/pallas_call | solution.py:140
  (2 shorter events, 0.1 us)
Async XLA Ops:
  6.5 90.5 %all-gather.3.cloned.1.call-start = ((), (), s32[]{:S(2)}) async-start(), calls=%async_computation | async-start | bytes 5308416 | tf_op jit(solution)/shard_map/all_gather | solution.py:151
  8.6 1.5 %collective-permute-start = (bf16[32,1152]{1,0:T(8,128)(2,1)}, bf16[32,1152]{1,0:T(8,128)(2,1)S(1)}, u32[]{:S(2)}, u32[]{:S(2)}) collective-permute-start(bf16[32,1152]{1,0:T(8,128)(2,1)} %get-tuple-element.10), channel_id=1, source_target_pairs={{0,0},{16,16},{32,32},{48,48},{64,64},{80,80},{2,96},{18,112},{34,... | collective-permute-start | bytes 221192 | tf_op jit(solution)/shard_map/ppermute | solution.py:152
  58.9 24.7 %collective-permute-start.2 = (bf16[384,1152]{1,0:T(8,128)(2,1)S(1)}, bf16[384,1152]{1,0:T(8,128)(2,1)S(1)}, u32[]{:S(2)}, u32[]{:S(2)}) collective-permute-start(bf16[384,1152]{1,0:T(8,128)(2,1)S(1)} %all_gather.11.own), channel_id=1, source_target_pairs={{0,192},{192,384},{384,576},{576,0},{1,193},{193,385},{385,577},{5... | collective-permute-start | bytes 2654216 | tf_op jit(solution)/shard_map/ppermute | solution.py:155
  64.7 22.5 %collective-permute-start.1 = (bf16[384,1152]{1,0:T(8,128)(2,1)S(1)}, bf16[384,1152]{1,0:T(8,128)(2,1)S(1)}, u32[]{:S(2)}, u32[]{:S(2)}) collective-permute-start(bf16[384,1152]{1,0:T(8,128)(2,1)S(1)} %all_gather.11.own), channel_id=1, source_target_pairs={{0,576},{192,0},{384,192},{576,384},{1,577},{193,1},{385,193},{577... | collective-permute-start | bytes 2654216 | tf_op jit(solution)/shard_map/ppermute | solution.py:154
  83.5 13.5 %copy-start.2 = (bf16[384,1152]{1,0:T(8,128)(2,1)}, bf16[384,1152]{1,0:T(8,128)(2,1)S(1)}, u32[]{:S(2)}) copy-start(bf16[384,1152]{1,0:T(8,128)(2,1)S(1)} %collective-permute-done.2.left) | copy-start | bytes 2654212
  83.6 27.5 %copy-start = (s32[1,4]{1,0:T(1,128)S(1)}, s32[1,4]{1,0:T(1,128)}, u32[]{:S(2)}) copy-start(s32[1,4]{1,0:T(1,128)} %tl.1) | copy-start | bytes 52
  83.6 27.5 %copy-start.1 = (s32[48]{0:T(128)S(1)}, s32[48]{0:T(128)}, u32[]{:S(2)}) copy-start(s32[48]{0:T(128)} %vl.1) | copy-start | bytes 580
  83.6 11.2 %collective-permute-start.3 = (bf16[192,1152]{1,0:T(8,128)(2,1)S(1)}, bf16[192,1152]{1,0:T(8,128)(2,1)S(1)}, u32[]{:S(2)}, u32[]{:S(2)}) collective-permute-start(bf16[192,1152]{1,0:T(8,128)(2,1)S(1)} %slice.8), channel_id=1, source_target_pairs={{0,192},{192,384},{384,576},{576,0},{1,193},{193,385},{385,577},{5... | collective-permute-start | bytes 1327112 | tf_op jit(solution)/shard_map/ppermute | solution.py:156
  87.2 9.7 %collective-permute-start.4 = (bf16[192,1152]{1,0:T(8,128)(2,1)S(1)}, bf16[192,1152]{1,0:T(8,128)(2,1)S(1)}, u32[]{:S(2)}, u32[]{:S(2)}) collective-permute-start(bf16[192,1152]{1,0:T(8,128)(2,1)S(1)} %slice.9), channel_id=1, source_target_pairs={{0,576},{192,0},{384,192},{576,384},{1,577},{193,1},{385,193},{577... | collective-permute-start | bytes 1327112 | tf_op jit(solution)/shard_map/ppermute | solution.py:157
  102.9 8.2 %collective-permute-start.5 = (f32[4,96,256]{2,1,0:T(8,128)S(1)}, f32[4,96,256]{2,1,0:T(8,128)S(1)}, u32[]{:S(2)}, u32[]{:S(2)}) collective-permute-start(f32[4,96,256]{2,1,0:T(8,128)S(1)} %get-tuple-element.12), channel_id=1, source_target_pairs={{0,1},{1,0},{2,3},{3,2},{4,5},{5,4},{6,7},{7,6},{8,9},{9,8},{10,11... | collective-permute-start | bytes 1179656 | tf_op jit(solution)/shard_map/ppermute | solution.py:159
Sparse Core Ops, SparseCore 0:
  9.7 72.3 all-gather.2

commit v5 on v4

--- a/solution.py
+++ b/solution.py
@@ -1,3 +1,5 @@
+import functools
+
 import jax
 import jax.numpy as jnp
 from jax import lax
@@ -52,62 +54,75 @@
     )(*arrays)
 
 
-def gram_kernel(train, own, right, left, far0, far1, mine, send, tbuf, vbuf, tsem, vsem):
+NEAR = ((0, 2 * ROWS), (1, 2 * ROWS), (3, 2 * ROWS))
+FAR = ((2, ROWS), (2, ROWS))
+
+
+def gram_kernel(pieces, *refs):
+    n = len(pieces)
+    count = sum(rows for _, rows in pieces) // ROWS
+    train, vals, rest = refs[0], refs[1 : n + 1], refs[n + 1 :]
+    before, (mine, send, tbuf, vbuf, tsem, vsem) = rest[:-6], rest[-6:]
     x = lax.axis_index("x")
     first = lax.axis_index("core") == 0
-    opposite = lax.rem(x + 2, NX)
-    vcopy = [
-        pltpu.make_async_copy(src, dst, vsem.at[i])
-        for i, (src, dst) in enumerate(
-            (
-                (own, vbuf.at[x]),
-                (right, vbuf.at[lax.rem(x + 1, NX)]),
-                (left, vbuf.at[lax.rem(x + 3, NX)]),
-                (far0, vbuf.at[opposite, 0:ROWS]),
-                (far1, vbuf.at[opposite, ROWS : 2 * ROWS]),
-            )
+    tcopy, vcopy, j = [], [], 0
+    for i, (ref, (shift, rows)) in enumerate(zip(vals, pieces)):
+        blocks = rows // ROWS
+        vcopy.append(
+            pltpu.make_async_copy(ref, vbuf.at[pl.ds(j * ROWS, rows)], vsem.at[i])
         )
-    ]
-    tcopy = [
-        pltpu.make_async_copy(train.at[:, :, lo:hi], tbuf.at[:, :, lo:hi], tsem.at[g])
-        for g, (lo, hi) in enumerate(COLS)
-    ]
-    for c in (*tcopy, *vcopy):
+        for h in range(blocks):
+            b = 2 * lax.rem(x + shift, NX) + (h if blocks == 2 else i)
+            tcopy.append(pltpu.make_async_copy(train.at[b], tbuf.at[j], tsem.at[j]))
+            j += 1
+    for c in (*vcopy, *tcopy):
         c.start()
     for c in vcopy:
         c.wait()
     for g, (lo, hi) in enumerate(COLS):
-        tcopy[g].wait()
-        acc = jnp.zeros((ROWS, TOK), jnp.float32)
-        for b in range(NY):
-            acc += lax.dot_general(
-                vbuf[b // 2, (b % 2) * ROWS : (b % 2 + 1) * ROWS, lo:hi],
-                tbuf[b, :, lo:hi],
+        acc = None
+        for j in range(count):
+            if g == 0:
+                tcopy[j].wait()
+            d = lax.dot_general(
+                vbuf[j * ROWS : (j + 1) * ROWS, lo:hi],
+                tbuf[j, :, lo:hi],
                 (((1,), (1,)), ((), ())),
                 preferred_element_type=jnp.float32,
             )
-        send[g] = jnp.where(first, acc[HALF:], acc[:HALF])
-        mine[g] = jnp.where(first, acc[:HALF], acc[HALF:])
+            acc = d if acc is None else acc + d
+        keep = jnp.where(first, acc[:HALF], acc[HALF:])
+        give = jnp.where(first, acc[HALF:], acc[:HALF])
+        if before:
+            keep, give = keep + before[0][g], give + before[1][g]
+        mine[g] = keep
+        send[g] = give
 
 
-def grams(*arrays):
+def grams(pieces, train, vals, before=()):
     half = jax.ShapeDtypeStruct((4, HALF, TOK), jnp.float32)
+    count = sum(rows for _, rows in pieces) // ROWS
     return pl.pallas_call(
-        gram_kernel,
+        functools.partial(gram_kernel, pieces),
         out_shape=(half, half),
-        in_specs=[ANY] * 6,
+        in_specs=[ANY] * (1 + len(pieces)) + [VMEM] * len(before),
         out_specs=(VMEM, VMEM),
         scratch_shapes=[
-            pltpu.VMEM((NY, TOK, WIDTH), jnp.bfloat16),
-            pltpu.VMEM((NX, 2 * ROWS, WIDTH), jnp.bfloat16),
-            pltpu.SemaphoreType.DMA((4,)),
-            pltpu.SemaphoreType.DMA((5,)),
+            pltpu.VMEM((count, TOK, WIDTH), jnp.bfloat16),
+            pltpu.VMEM((count * ROWS, WIDTH), jnp.bfloat16),
+            pltpu.SemaphoreType.DMA((count,)),
+            pltpu.SemaphoreType.DMA((len(pieces),)),
         ],
         compiler_params=pltpu.CompilerParams(vmem_limit_bytes=GRAM_MIB * MIB),
-    )(*arrays)
+        cost_estimate=pl.CostEstimate(
+            flops=2 * count * ROWS * TOK * WIDTH,
+            bytes_accessed=2 * count * (ROWS + TOK) * WIDTH,
+            transcendentals=0,
+        ),
+    )(train, *vals, *before)
 
 
-GRAM_MIB = 50
+GRAM_MIB = 48
 
 
 def score_kernel(tl, vl, mine, other, out):
@@ -155,7 +170,8 @@
     left = lax.ppermute(own, "x", around(NX, 1))
     far0 = lax.ppermute(left[:ROWS], "x", around(NX, 1))
     far1 = lax.ppermute(right[ROWS:], "x", around(NX, -1))
-    mine, send = grams(full, own, right, left, far0, far1)
+    near = grams(NEAR, full, (own, right, left))
+    mine, send = grams(FAR, full, (far0, far1), near)
     other = lax.ppermute(send, "core", [(0, 1), (1, 0)])
     return scores_of(tl, vl, mine, other)
 

time: 121 us -> 119 us (0.983)
  waiting for transfers between devices: 23.5 us -> 19.5 us
  local copies, waits for them, and re-layouts: 0.09 us -> 1.66 us
    ppermute x1, waiting for transfers between devices: 4.47 us -> 0.24 us  [local(): far0 = lax.ppermute(left[:ROWS], 'x', around(NX, 1))]
    pallas_call x1 -> x2, Pallas kernels: 5.93 us -> 5.95 us  [grams(): pl.pallas_call(functools.partial(gram_kernel, pieces), out_shape=(half, h...]
  transfers between devices with their start and end apart: 7 -> 7, of which waited for: 5 -> 4; matrix products, arithmetic and copies ran while one was open for 0% -> 1% of each run, Pallas kernels for 0% -> 3%
where the time goes in v5:
time: 119 us; the launch traced here: 117 us
  blocking collectives  48.7 us (41%)
  starting transfers between devices  24.6 us (21%)
  waiting for transfers between devices  19.5 us (16%)
  between operations  13.5 us (11%)
  Pallas kernels  9.25 us (8%)
  local copies, waits for them, and re-layouts  1.66 us (1%)
    all_gather x1, blocking collectives, local(): own = lax.all_gather(val, 'z', axis=0, tiled=True)  48.7 us
    ppermute x1, waiting for transfers between devices, local(): left = lax.ppermute(own, 'x', around(NX, 1))  14.9 us
    ppermute x1, starting transfers between devices, local(): other = lax.ppermute(send, 'core', [(0, 1), (1, 0)])  6.85 us
    pallas_call x2, Pallas kernels, grams(): pl.pallas_call(functools.partial(gram_kernel, pieces), out_shape=(half, h...  5.95 us
    ppermute x1, starting transfers between devices, local(): left = lax.ppermute(own, 'x', around(NX, 1))  5.93 us
    ppermute x1, starting transfers between devices, local(): right = lax.ppermute(own, 'x', around(NX, -1))  3.8 us
    ppermute x1, starting transfers between devices, local(): far1 = lax.ppermute(right[ROWS:], 'x', around(NX, -1))  3.57 us
    ppermute x1, waiting for transfers between devices, local(): far1 = lax.ppermute(right[ROWS:], 'x', around(NX, -1))  2.96 us
  transfers between devices with their start and end apart: 7, of which 4 were waited for; matrix products, arithmetic and copies ran while one was open for 1% of the time, Pallas kernels for 3%

profile of v5, /device:TPU:1, one launch (start us, length us, event | category | flops | bytes accessed | tf_op | source)
XLA Modules:
  0.0 117.2 jit_solution(7925699866735215410)
XLA Ops:
  6.5 0.0 all-gather.3.cloned.1.call-start
  6.5 2.0 %shard_map.100 = (bf16[256,1152]{1,0:T(8,128)(2,1)}, bf16[32,1152]{1,0:T(8,128)(2,1)}) custom-call(bf16[256,256]{1,0:T(8,128)(2,1)} %tx.1, bf16[256,256]{1,0:T(8,128)(2,1)} %ta.1, bf16[256,384]{1,0:T(8,128)(2,1)} %tq.1, bf16[256,256]{1,0:T(8,128)(2,1)} %to.1, bf16[1,32,256]{2,1,0:T(8,128)(2,1)} %vx.1, bf16[1,32,256]{2,1,0:T(8,128)(2,1)} %va.1, ...), custom_call_target="tpu_custom_call" | custom-call | tf_op jit(solution)/shard_map/pallas_call | solution.py:45
  8.6 0.0 all-gather.3.cloned.1.call-update
  8.6 1.5 %collective-permute-start = (bf16[32,1152]{1,0:T(8,128)(2,1)}, bf16[32,1152]{1,0:T(8,128)(2,1)S(1)}, u32[]{:S(2)}, u32[]{:S(2)}) collective-permute-start(bf16[32,1152]{1,0:T(8,128)(2,1)} %get-tuple-element.12), channel_id=1, source_target_pairs={{0,0},{16,16},{32,32},{48,48},{64,64},{80,80},{2,96},{18,112},{34,... | collective-permute-start | bytes 221192 | tf_op jit(solution)/shard_map/ppermute | solution.py:167
  10.1 0.0 collective-permute-done
  10.1 48.7 %all_gather.11.refs_1_ = bf16[384,1152]{1,0:T(8,128)(2,1)S(1)} all-gather(bf16[32,1152]{1,0:T(8,128)(2,1)S(1)} %collective-permute-done), channel_id=1, replica_groups=mesh['x'=4,'z'=12,'y'=8,'core'=2] {'z'}, dimensions={0}, use_global_device_ids=true | all-gather | bytes 958464 | tf_op jit(solution)/shard_map/all_gather | solution.py:168
  58.9 5.9 %collective-permute-start.1 = (bf16[384,1152]{1,0:T(8,128)(2,1)S(1)}, bf16[384,1152]{1,0:T(8,128)(2,1)S(1)}, u32[]{:S(2)}, u32[]{:S(2)}) collective-permute-start(bf16[384,1152]{1,0:T(8,128)(2,1)S(1)} %all_gather.11.refs_1_), channel_id=1, source_target_pairs={{0,192},{192,384},{384,576},{576,0},{1,193},{193,385},{385,577},{5... | collective-permute-start | bytes 2654216 | tf_op jit(solution)/shard_map/ppermute | solution.py:170
  64.8 3.8 %collective-permute-start.3 = (bf16[384,1152]{1,0:T(8,128)(2,1)S(1)}, bf16[384,1152]{1,0:T(8,128)(2,1)S(1)}, u32[]{:S(2)}, u32[]{:S(2)}) collective-permute-start(bf16[384,1152]{1,0:T(8,128)(2,1)S(1)} %all_gather.11.refs_1_), channel_id=1, source_target_pairs={{0,576},{192,0},{384,192},{576,384},{1,577},{193,1},{385,193},{577... | collective-permute-start | bytes 2654216 | tf_op jit(solution)/shard_map/ppermute | solution.py:169
  68.6 14.9 %collective-permute-done.1.refs_3_ = bf16[384,1152]{1,0:T(8,128)(2,1)S(1)} collective-permute-done((bf16[384,1152]{1,0:T(8,128)(2,1)S(1)}, bf16[384,1152]{1,0:T(8,128)(2,1)S(1)}, u32[]{:S(2)}, u32[]{:S(2)}) %collective-permute-start.1) | collective-permute-done | bytes 884768 | tf_op jit(solution)/shard_map/ppermute | solution.py:170
  83.5 0.9 slice.8
  84.4 2.9 %collective-permute-start.2 = (bf16[192,1152]{1,0:T(8,128)(2,1)}, bf16[192,1152]{1,0:T(8,128)(2,1)S(1)}, u32[]{:S(2)}, u32[]{:S(2)}) collective-permute-start(bf16[192,1152]{1,0:T(8,128)(2,1)} %slice.8), channel_id=1, source_target_pairs={{0,192},{192,384},{384,576},{576,0},{1,193},{193,385},{385,577},{5... | collective-permute-start | bytes 1327112 | tf_op jit(solution)/shard_map/ppermute | solution.py:171
  87.3 0.0 collective-permute-done.3.refs_2_
  87.3 0.8 slice.9
  88.1 3.6 %collective-permute-start.4 = (bf16[192,1152]{1,0:T(8,128)(2,1)}, bf16[192,1152]{1,0:T(8,128)(2,1)S(1)}, u32[]{:S(2)}, u32[]{:S(2)}) collective-permute-start(bf16[192,1152]{1,0:T(8,128)(2,1)} %slice.9), channel_id=1, source_target_pairs={{0,576},{192,0},{384,192},{576,384},{1,577},{193,1},{385,193},{577... | collective-permute-start | bytes 1327112 | tf_op jit(solution)/shard_map/ppermute | solution.py:172
  91.7 0.0 all-gather.3.cloned.1.call-done
  91.7 3.6 %shard_map.101 = (f32[4,96,256]{2,1,0:T(8,128)S(1)}, f32[4,96,256]{2,1,0:T(8,128)S(1)}) custom-call(bf16[8,256,1152]{2,1,0:T(8,128)(2,1)} %bitcast.1, bf16[384,1152]{1,0:T(8,128)(2,1)S(1)} %all_gather.11.refs_1_, bf16[384,1152]{1,0:T(8,128)(2,1)S(1)} %collective-permute-done.3.refs_2_, bf16[384,1152]{1,0:T(8,128)(2,1)S(1)} %collective-permute-done.1.refs_3_), custom_call_target="tpu_custom_call" | custom-call | flops 679477248 | bytes 6193152 | tf_op jit(solution)/shard_map/pallas_call | solution.py:105
  95.4 0.0 copy-start
  95.4 0.0 copy-start.1
  95.4 0.2 collective-permute-done.2.refs_1_
  95.6 3.0 %collective-permute-done.4.refs_2_ = bf16[192,1152]{1,0:T(8,128)(2,1)S(1)} collective-permute-done((bf16[192,1152]{1,0:T(8,128)(2,1)}, bf16[192,1152]{1,0:T(8,128)(2,1)S(1)}, u32[]{:S(2)}, u32[]{:S(2)}) %collective-permute-start.4) | collective-permute-done | bytes 442400 | tf_op jit(solution)/shard_map/ppermute | solution.py:172
  98.6 2.3 %shard_map.102 = (f32[4,96,256]{2,1,0:T(8,128)S(1)}, f32[4,96,256]{2,1,0:T(8,128)S(1)}) custom-call(bf16[8,256,1152]{2,1,0:T(8,128)(2,1)} %bitcast.2, bf16[192,1152]{1,0:T(8,128)(2,1)S(1)} %collective-permute-done.2.refs_1_, bf16[192,1152]{1,0:T(8,128)(2,1)S(1)} %collective-permute-done.4.refs_2_, f32[4,96,256]{2,1,0:T(8,128)S(1)} %get-tuple-element.13.refs_3_, ...), custom_call_target="tpu_custom_call" | custom-call | flops 226492416 | bytes 2064384 | tf_op jit(solution)/shard_map/pallas_call | solution.py:105
  100.9 6.9 %collective-permute-start.5 = (f32[4,96,256]{2,1,0:T(8,128)S(1)}, f32[4,96,256]{2,1,0:T(8,128)S(1)}, u32[]{:S(2)}, u32[]{:S(2)}) collective-permute-start(f32[4,96,256]{2,1,0:T(8,128)S(1)} %get-tuple-element.16), channel_id=1, source_target_pairs={{0,1},{1,0},{2,3},{3,2},{4,5},{5,4},{6,7},{7,6},{8,9},{9,8},{10,11... | collective-permute-start | bytes 1179656 | tf_op jit(solution)/shard_map/ppermute | solution.py:175
  107.8 1.3 %collective-permute-done.5.other = f32[4,96,256]{2,1,0:T(8,128)S(1)} collective-permute-done((f32[4,96,256]{2,1,0:T(8,128)S(1)}, f32[4,96,256]{2,1,0:T(8,128)S(1)}, u32[]{:S(2)}, u32[]{:S(2)}) %collective-permute-start.5) | collective-permute-done | bytes 393248 | tf_op jit(solution)/shard_map/ppermute | solution.py:175
  109.1 0.0 copy-done
  109.1 0.0 copy-done.1
  109.1 1.3 %shard_map.103 = f32[4,3]{1,0:T(4,128)} custom-call(s32[1,4]{1,0:T(1,128)S(1)} %copy-done, s32[48]{0:T(128)S(1)} %copy-done.1, f32[4,96,256]{2,1,0:T(8,128)S(1)} %get-tuple-element.15.mine, f32[4,96,256]{2,1,0:T(8,128)S(1)} %collective-permute-done.5.other), custom_call_target="tpu_custom_call" | custom-call | tf_op jit(solution)/shard_map/pallas_call | solution.py:155
Async XLA Ops:
  6.5 85.2 %all-gather.3.cloned.1.call-start = ((), (), s32[]{:S(2)}) async-start(), calls=%async_computation | async-start | bytes 5308416 | tf_op jit(solution)/shard_map/all_gather | solution.py:166
  8.6 1.5 %collective-permute-start = (bf16[32,1152]{1,0:T(8,128)(2,1)}, bf16[32,1152]{1,0:T(8,128)(2,1)S(1)}, u32[]{:S(2)}, u32[]{:S(2)}) collective-permute-start(bf16[32,1152]{1,0:T(8,128)(2,1)} %get-tuple-element.12), channel_id=1, source_target_pairs={{0,0},{16,16},{32,32},{48,48},{64,64},{80,80},{2,96},{18,112},{34,... | collective-permute-start | bytes 221192 | tf_op jit(solution)/shard_map/ppermute | solution.py:167
  58.9 24.7 %collective-permute-start.1 = (bf16[384,1152]{1,0:T(8,128)(2,1)S(1)}, bf16[384,1152]{1,0:T(8,128)(2,1)S(1)}, u32[]{:S(2)}, u32[]{:S(2)}) collective-permute-start(bf16[384,1152]{1,0:T(8,128)(2,1)S(1)} %all_gather.11.refs_1_), channel_id=1, source_target_pairs={{0,192},{192,384},{384,576},{576,0},{1,193},{193,385},{385,577},{5... | collective-permute-start | bytes 2654216 | tf_op jit(solution)/shard_map/ppermute | solution.py:170
  64.8 22.5 %collective-permute-start.3 = (bf16[384,1152]{1,0:T(8,128)(2,1)S(1)}, bf16[384,1152]{1,0:T(8,128)(2,1)S(1)}, u32[]{:S(2)}, u32[]{:S(2)}) collective-permute-start(bf16[384,1152]{1,0:T(8,128)(2,1)S(1)} %all_gather.11.refs_1_), channel_id=1, source_target_pairs={{0,576},{192,0},{384,192},{576,384},{1,577},{193,1},{385,193},{577... | collective-permute-start | bytes 2654216 | tf_op jit(solution)/shard_map/ppermute | solution.py:169
  84.4 11.2 %collective-permute-start.2 = (bf16[192,1152]{1,0:T(8,128)(2,1)}, bf16[192,1152]{1,0:T(8,128)(2,1)S(1)}, u32[]{:S(2)}, u32[]{:S(2)}) collective-permute-start(bf16[192,1152]{1,0:T(8,128)(2,1)} %slice.8), channel_id=1, source_target_pairs={{0,192},{192,384},{384,576},{576,0},{1,193},{193,385},{385,577},{5... | collective-permute-start | bytes 1327112 | tf_op jit(solution)/shard_map/ppermute | solution.py:171
  88.1 10.5 %collective-permute-start.4 = (bf16[192,1152]{1,0:T(8,128)(2,1)}, bf16[192,1152]{1,0:T(8,128)(2,1)S(1)}, u32[]{:S(2)}, u32[]{:S(2)}) collective-permute-start(bf16[192,1152]{1,0:T(8,128)(2,1)} %slice.9), channel_id=1, source_target_pairs={{0,576},{192,0},{384,192},{576,384},{1,577},{193,1},{385,193},{577... | collective-permute-start | bytes 1327112 | tf_op jit(solution)/shard_map/ppermute | solution.py:172
  95.4 13.7 %copy-start = (s32[1,4]{1,0:T(1,128)S(1)}, s32[1,4]{1,0:T(1,128)}, u32[]{:S(2)}) copy-start(s32[1,4]{1,0:T(1,128)} %tl.1) | copy-start | bytes 52
  95.4 13.7 %copy-start.1 = (s32[48]{0:T(128)S(1)}, s32[48]{0:T(128)}, u32[]{:S(2)}) copy-start(s32[48]{0:T(128)} %vl.1) | copy-start | bytes 580
  100.9 8.2 %collective-permute-start.5 = (f32[4,96,256]{2,1,0:T(8,128)S(1)}, f32[4,96,256]{2,1,0:T(8,128)S(1)}, u32[]{:S(2)}, u32[]{:S(2)}) collective-permute-start(f32[4,96,256]{2,1,0:T(8,128)S(1)} %get-tuple-element.16), channel_id=1, source_target_pairs={{0,1},{1,0},{2,3},{3,2},{4,5},{5,4},{6,7},{7,6},{8,9},{9,8},{10,11... | collective-permute-start | bytes 1179656 | tf_op jit(solution)/shard_map/ppermute | solution.py:175
Sparse Core Ops, SparseCore 0:
  9.7 72.3 all-gather.2

commit v6 on v5

v6 whole, which is shorter than its diff:
```python
import functools

import jax
import jax.numpy as jnp
from jax import lax
from jax.experimental import pallas as pl
from jax.experimental.pallas import tpu as pltpu
from jax.sharding import Mesh, PartitionSpec as P

score_scale = 0.015625

NX, NZ, NQ, NL, NC = 4, 12, 4, 2, 2
NY = NQ * NL
TOK, VLEN = 256, 32
WIDTH = 640
COLS = ((0, 256), (256, 640))
HALF = 3 * VLEN
GROUP = NZ // 2 * VLEN
MIB = 1024 * 1024

ANY = pl.BlockSpec(memory_space=pl.ANY)
VMEM = pl.BlockSpec(memory_space=pltpu.VMEM)
SMEM = pl.BlockSpec(memory_space=pltpu.SMEM)

CHIP = ("x", "z", "yh", "yl")


def swap(other):
    return [
        (
            ((x * NZ + z) * NQ + q) * NL + l,
            ((q * NZ + z) * NQ + x) * NL + (1 - l if other else l),
        )
        for x in range(NX)
        for z in range(NZ)
        for q in range(NQ)
        for l in range(NL)
    ]


def around(size, shift):
    return [(i, (i + shift) % size) for i in range(size)]


def join_kernel(tx, ta, tq, to, vx, va, vq, vo, parts, same, other, xq, ao, sems):
    xq[:, :256] = tx[...]
    xq[:, 256:] = tq[...]
    ao[:, :256] = ta[...]
    ao[:, 256:512] = to[...]
    ao[:, 512:] = jnp.zeros((TOK, 128), jnp.bfloat16)
    copies = [
        pltpu.make_async_copy(ao if y % 2 else xq, parts.at[y], sems.at[y])
        for y in range(NY)
    ]
    for c in copies:
        c.start()
    even = lax.axis_index("yl") == 0
    vxq = (vx[0], vq[0])
    vao = (va[0], jnp.concatenate((vo[0], jnp.zeros((VLEN, 128), jnp.bfloat16)), 1))
    for (lo, hi), p, q in zip(COLS, vxq, vao):
        same[:, lo:hi] = jnp.where(even, p, q)
        other[:, lo:hi] = jnp.where(even, q, p)
    for c in copies:
        c.wait()


def join(*arrays):
    block = jax.ShapeDtypeStruct((VLEN, WIDTH), jnp.bfloat16)
    whole = pltpu.VMEM((TOK, WIDTH), jnp.bfloat16)
    return pl.pallas_call(
        join_kernel,
        out_shape=(
            jax.ShapeDtypeStruct((NY, TOK, WIDTH), jnp.bfloat16),
            block,
            block,
        ),
        in_specs=[VMEM] * 8,
        out_specs=(ANY, VMEM, VMEM),
        scratch_shapes=[whole, whole, pltpu.SemaphoreType.DMA((NY,))],
        compiler_params=pltpu.CompilerParams(vmem_limit_bytes=58 * MIB),
    )(*arrays)


NEAR = ((0, 0, 12), (1, 0, 12), (3, 0, 12))
FAR = ((2, 0, 6), (2, 6, 12))


def gram_kernel(pieces, *refs):
    n = len(pieces)
    shifts = sorted({shift for shift, _, _ in pieces})
    train, vals, rest = refs[0], refs[1 : n + 1], refs[n + 1 :]
    before, (mine, send, tbuf, vbuf, tsem, vsem) = rest[:-6], rest[-6:]
    x, l = lax.axis_index("x"), lax.axis_index("yl")
    first = lax.axis_index("core") == 0
    tcopy = []
    for k, shift in enumerate(shifts):
        q = lax.rem(x + shift, NX)
        for e in range(2):
            y = 2 * q + (l if e == 0 else 1 - l)
            j = 2 * k + e
            tcopy.append(pltpu.make_async_copy(train.at[y], tbuf.at[j], tsem.at[j]))
    vcopy = [
        pltpu.make_async_copy(ref, vbuf.at[shifts.index(shift), lo:hi], vsem.at[i])
        for i, (ref, (shift, lo, hi)) in enumerate(zip(vals, pieces))
    ]
    for c in (*vcopy, *tcopy):
        c.start()
    for c in (*vcopy, *tcopy):
        c.wait()
    for g, (lo, hi) in enumerate(COLS):
        for m in range(2):
            acc = None
            for j in range(2 * len(shifts)):
                v = vbuf[j // 2, 6 * m : 6 * m + 6, j % 2, :, lo:hi]
                d = lax.dot_general(
                    v.reshape(GROUP, hi - lo),
                    tbuf[j, :, lo:hi],
                    (((1,), (1,)), ((), ())),
                    preferred_element_type=jnp.float32,
                )
                acc = d if acc is None else acc + d
            keep = jnp.where(first, acc[:HALF], acc[HALF:])
            give = jnp.where(first, acc[HALF:], acc[:HALF])
            if before:
                keep, give = keep + before[0][g, m], give + before[1][g, m]
            mine[g, m] = keep
            send[g, m] = give


def grams(pieces, train, vals, before=()):
    half = jax.ShapeDtypeStruct((2, 2, HALF, TOK), jnp.float32)
    count = len({shift for shift, _, _ in pieces})
    return pl.pallas_call(
        functools.partial(gram_kernel, pieces),
        out_shape=(half, half),
        in_specs=[ANY] * (1 + len(pieces)) + [VMEM] * len(before),
        out_specs=(VMEM, VMEM),
        scratch_shapes=[
            pltpu.VMEM((2 * count, TOK, WIDTH), jnp.bfloat16),
            pltpu.VMEM((count, NZ, 2, VLEN, WIDTH), jnp.bfloat16),
            pltpu.SemaphoreType.DMA((2 * count,)),
            pltpu.SemaphoreType.DMA((len(pieces),)),
        ],
        compiler_params=pltpu.CompilerParams(vmem_limit_bytes=GRAM_MIB * MIB),
        cost_estimate=pl.CostEstimate(
            flops=4 * count * NZ * VLEN * TOK * WIDTH,
            bytes_accessed=4 * count * (NZ * VLEN + TOK) * WIDTH,
            transcendentals=0,
        ),
    )(train, *vals, *before)


GRAM_MIB = 16


def score_kernel(tl, vl, mine, other, keep, give):
    core, l = lax.axis_index("core"), lax.axis_index("yl")
    g = mine[...] + other[...]
    contrib = g[0] * g[1]
    places = lax.broadcasted_iota(jnp.int32, (VLEN, TOK), 0)
    tokens = lax.broadcasted_iota(jnp.int32, (1, TOK), 1)
    rows = lax.broadcasted_iota(jnp.int32, (4, 3), 0)
    cols = lax.broadcasted_iota(jnp.int32, (4, 3), 1)
    results = []
    for m in range(2):
        first = NZ * lax.axis_index("yh") + 6 * m + 3 * core
        result = jnp.zeros((4, 3), jnp.float32)
        for s in range(3):
            block = contrib[m, s * VLEN : (s + 1) * VLEN]
            per_token = jnp.sum(
                jnp.where(places < vl[first + s], block, 0.0), axis=0, keepdims=True
            )
            start = jnp.int32(0)
            for k in range(4):
                end = start + tl[0, k]
                inside = (tokens >= start) & (tokens < end)
                total = jnp.sum(
                    jnp.where(inside, per_token, 0.0), axis=1, keepdims=True
                )
                result = jnp.where((rows == k) & (cols == s), total, result)
                start = end
        results.append(result * score_scale)
    keep[...] = jnp.where(l == 0, results[0], results[1])
    give[...] = jnp.where(l == 0, results[1], results[0])


def scores_of(tl, vl, mine, other):
    part = jax.ShapeDtypeStruct((4, 3), jnp.float32)
    return pl.pallas_call(
        score_kernel,
        out_shape=(part, part),
        in_specs=[SMEM, SMEM, VMEM, VMEM],
        out_specs=(VMEM, VMEM),
        compiler_params=pltpu.CompilerParams(vmem_limit_bytes=16 * MIB),
    )(tl, vl, mine, other)


def local(tx, ta, tq, to, tl, vx, va, vq, vo, vl):
    parts, same, other = join(tx, ta, tq, to, vx, va, vq, vo)
    train = lax.all_to_all(parts, ("yh", "yl"), 0, 0, tiled=True)
    val = jnp.stack(
        (
            lax.ppermute(same, CHIP, swap(False)),
            lax.ppermute(other, CHIP, swap(True)),
        )
    )
    own = lax.all_gather(val, "z", axis=0, tiled=False)
    right = lax.ppermute(own, "x", around(NX, -1))
    left = lax.ppermute(own, "x", around(NX, 1))
    far0 = lax.ppermute(left[:6], "x", around(NX, 1))
    far1 = lax.ppermute(right[6:], "x", around(NX, -1))
    near = grams(NEAR, train, (own, right, left))
    mine, send = grams(FAR, train, (far0, far1), near)
    theirs = lax.ppermute(send, "core", [(0, 1), (1, 0)])
    keep, give = scores_of(tl, vl, mine, theirs)
    return keep + lax.ppermute(give, "yl", [(0, 1), (1, 0)])


def solution(mesh):
    fine = Mesh(
        mesh.devices.reshape(NX, NZ, NQ, NL, NC), ("x", "z", "yh", "yl", "core")
    )
    dp, fsdp = ("x", "z"), ("yh", "yl", "core")
    in_specs = (
        (P(dp, fsdp),) * 4 + (P(dp, None),) + (P(dp, None, fsdp),) * 4 + (P(),)
    )
    return jax.shard_map(
        local, mesh=fine, in_specs=in_specs, out_specs=P(dp, fsdp), check_vma=False
    )
```

time: 119 us -> 166 us (1.39)
  waiting for transfers between devices: 19.5 us -> 61.4 us
  starting transfers between devices: 24.6 us -> 44.4 us
  between operations: 13.5 us -> 0.19 us
  blocking collectives: 48.7 us -> 43.5 us
  local copies, waits for them, and re-layouts: 1.66 us -> 6.3 us
    ppermute x4 -> x6, waiting for transfers between devices: 4.52 us -> 51.2 us  [the longest x1 46.1 us: local(): lax.ppermute(other, CHIP, swap(True))]
    ppermute x1, waiting for transfers between devices: 14.9 us -> 0.01 us  [local(): left = lax.ppermute(own, 'x', around(NX, 1))]
    ppermute x4 -> x6, starting transfers between devices: 14.9 us -> 28.6 us  [the longest x1 13.1 us: local(): theirs = lax.ppermute(send, 'core', [(0, 1), (1, 0)])]
    ppermute x1, waiting for transfers between devices: 0.01 us -> 10.2 us  [local(): right = lax.ppermute(own, 'x', around(NX, -1))]
    all_to_all x0 -> x1, starting transfers between devices: none -> 7.79 us  [local(): train = lax.all_to_all(parts, ('yh', 'yl'), 0, 0, tiled=True)]
    all_gather x1, blocking collectives: 48.7 us -> 43.5 us  [local(): own = lax.all_gather(val, 'z', axis=0, tiled=False)]
    unnamed x4 -> x20, local copies, waits for them, and re-layouts: 0.01 us -> 4.59 us
    ppermute x1, starting transfers between devices: 5.93 us -> 1.92 us  [local(): left = lax.ppermute(own, 'x', around(NX, 1))]
  transfers between devices with their start and end apart: 7 -> 9, of which waited for: 4 -> 5; matrix products, arithmetic and copies ran while one was open for 1% -> 1% of each run, Pallas kernels for 3% -> 2%
where the time goes in v6:
time: 166 us; the launch traced here: 165 us
  waiting for transfers between devices  61.4 us (37%)
  starting transfers between devices  44.4 us (27%)
  blocking collectives  43.5 us (26%)
  Pallas kernels  8.86 us (5%)
  local copies, waits for them, and re-layouts  6.3 us (4%)
    ppermute x1, waiting for transfers between devices, local(): lax.ppermute(other, CHIP, swap(True))  46.1 us
    all_gather x1, blocking collectives, local(): own = lax.all_gather(val, 'z', axis=0, tiled=False)  43.5 us
    ppermute x1, starting transfers between devices, local(): theirs = lax.ppermute(send, 'core', [(0, 1), (1, 0)])  13.1 us
    ppermute x1, waiting for transfers between devices, local(): right = lax.ppermute(own, 'x', around(NX, -1))  10.2 us
    all_to_all x1, starting transfers between devices, local(): train = lax.all_to_all(parts, ('yh', 'yl'), 0, 0, tiled=True)  7.79 us
    ppermute x1, starting transfers between devices, local(): far1 = lax.ppermute(right[6:], 'x', around(NX, -1))  6.51 us
    ppermute x1, starting transfers between devices, local(): right = lax.ppermute(own, 'x', around(NX, -1))  6.09 us
    pallas_call x2, Pallas kernels, grams(): pl.pallas_call(functools.partial(gram_kernel, pieces), out_shape=(half, h...  4.78 us
  transfers between devices with their start and end apart: 9, of which 5 were waited for; matrix products, arithmetic and copies ran while one was open for 1% of the time, Pallas kernels for 2%

profile of v6, /device:TPU:1, one launch (start us, length us, event | category | flops | bytes accessed | tf_op | source)
XLA Modules:
  0.0 165.3 jit_solution(15761550541989412635)
XLA Ops:
  0.0 3.4 %shard_map.100 = (bf16[8,256,640]{2,1,0:T(8,128)(2,1)}, bf16[32,640]{1,0:T(8,128)(2,1)}, bf16[32,640]{1,0:T(8,128)(2,1)}) custom-call(bf16[256,256]{1,0:T(8,128)(2,1)} %tx.1, bf16[256,256]{1,0:T(8,128)(2,1)} %ta.1, bf16[256,384]{1,0:T(8,128)(2,1)} %tq.1, bf16[256,256]{1,0:T(8,128)(2,1)} %to.1, bf16[1,32,256]{2,1,0:T(8,128)(2,1)} %vx.1, ...), custom_call_target="tpu_custom_call" | custom-call | tf_op jit(solution)/shard_map/pallas_call | solution.py:70
  3.4 0.0 copy-start.9
  3.4 0.0 copy-start.8
  3.4 7.8 %all-to-all-start = ((bf16[8,256,640]{2,1,0:T(8,128)(2,1)}), bf16[8,256,640]{2,1,0:T(8,128)(2,1)S(1)}, u32[]{:S(2)}, u32[]{:S(2)}) async-start(bf16[8,256,640]{2,1,0:T(8,128)(2,1)} %get-tuple-element.14), calls=%async_computation | async-start | bytes 5242880 | tf_op jit(solution)/shard_map/all_to_all | solution.py:200
  11.2 0.0 copy-done.9
  11.2 0.7 collective-permute-start
  11.9 0.0 copy-done.8
  11.9 3.4 %collective-permute-start.1 = (bf16[32,640]{1,0:T(8,128)(2,1)S(1)}, bf16[32,640]{1,0:T(8,128)(2,1)S(1)}, u32[]{:S(2)}, u32[]{:S(2)}) collective-permute-start(bf16[32,640]{1,0:T(8,128)(2,1)S(1)} %copy-done.8), channel_id=1, source_target_pairs={{0,2},{2,0},{4,194},{6,192},{8,386},{10,384},{12,578},{14,576},{16... | collective-permute-start | bytes 122888 | tf_op jit(solution)/shard_map/ppermute | solution.py:204
  15.2 0.0 collective-permute-done
  15.3 46.1 %collective-permute-done.1 = bf16[32,640]{1,0:T(8,128)(2,1)S(1)} collective-permute-done((bf16[32,640]{1,0:T(8,128)(2,1)S(1)}, bf16[32,640]{1,0:T(8,128)(2,1)S(1)}, u32[]{:S(2)}, u32[]{:S(2)}) %collective-permute-start.1) | collective-permute-done | bytes 40992 | tf_op jit(solution)/shard_map/ppermute | solution.py:204
  61.4 43.5 %all-gather = bf16[24,32,640]{2,1,0:T(8,128)(2,1)S(1)} all-gather(bf16[2,32,640]{2,1,0:T(8,128)(2,1)S(1)} %pad_maximum_fusion), channel_id=2, replica_groups=mesh['x'=4,'z'=12,'yh'=4,'yl'=2,'core'=2] {'z'}, dimensions={0}, use_global_device_ids=true | all-gather | bytes 1064960 | tf_op jit(solution)/shard_map/all_gather | solution.py:207
  104.9 0.0 copy-start
  104.9 6.1 %collective-permute-start.4 = (bf16[12,2,32,640]{3,2,1,0:T(8,128)(2,1)S(1)}, bf16[12,2,32,640]{3,2,1,0:T(8,128)(2,1)S(1)}, u32[]{:S(2)}, u32[]{:S(2)}) collective-permute-start(bf16[12,2,32,640]{3,2,1,0:T(8,128)(2,1)S(1)} %bitcast.3), channel_id=1, source_target_pairs={{0,576},{192,0},{384,192},{576,384},{1,577},{193,1},{385,193},{577... | collective-permute-start | bytes 2949128 | tf_op jit(solution)/shard_map/ppermute | solution.py:208
  111.0 1.9 %collective-permute-start.2 = (bf16[12,2,32,640]{3,2,1,0:T(8,128)(2,1)S(1)}, bf16[12,2,32,640]{3,2,1,0:T(8,128)(2,1)S(1)}, u32[]{:S(2)}, u32[]{:S(2)}) collective-permute-start(bf16[12,2,32,640]{3,2,1,0:T(8,128)(2,1)S(1)} %bitcast.4), channel_id=1, source_target_pairs={{0,192},{192,384},{384,576},{576,0},{1,193},{193,385},{385,577},{5... | collective-permute-start | bytes 2949128 | tf_op jit(solution)/shard_map/ppermute | solution.py:209
  113.0 10.2 %collective-permute-done.4.refs_2_ = bf16[12,2,32,640]{3,2,1,0:T(8,128)(2,1)S(1)} collective-permute-done((bf16[12,2,32,640]{3,2,1,0:T(8,128)(2,1)S(1)}, bf16[12,2,32,640]{3,2,1,0:T(8,128)(2,1)S(1)}, u32[]{:S(2)}, u32[]{:S(2)}) %collective-permute-start.4) | collective-permute-done | bytes 983072 | tf_op jit(solution)/shard_map/ppermute | solution.py:208
  123.2 0.0 copy-start.2
  123.2 0.9 slice.9
  124.1 6.5 %collective-permute-start.5 = (bf16[6,2,32,640]{3,2,1,0:T(8,128)(2,1)}, bf16[6,2,32,640]{3,2,1,0:T(8,128)(2,1)S(1)}, u32[]{:S(2)}, u32[]{:S(2)}) collective-permute-start(bf16[6,2,32,640]{3,2,1,0:T(8,128)(2,1)} %slice.9), channel_id=1, source_target_pairs={{0,576},{192,0},{384,192},{576,384},{1,577},{193,1},{385,193},{577... | collective-permute-start | bytes 1474568 | tf_op jit(solution)/shard_map/ppermute | solution.py:211
  130.6 0.0 collective-permute-done.2.refs_3_
  130.6 0.8 slice.8
  131.4 0.0 copy-done
  131.4 0.0 copy-done.2
  131.4 0.0 copy-start.4
  131.4 1.0 copy-done.4
  132.4 1.9 %collective-permute-start.3 = (bf16[6,2,32,640]{3,2,1,0:T(8,128)(2,1)}, bf16[6,2,32,640]{3,2,1,0:T(8,128)(2,1)}, u32[]{:S(2)}, u32[]{:S(2)}) collective-permute-start(bf16[6,2,32,640]{3,2,1,0:T(8,128)(2,1)} %slice.8), channel_id=1, source_target_pairs={{0,192},{192,384},{384,576},{576,0},{1,193},{193,385},{385,577},{5... | collective-permute-start | bytes 1474568 | tf_op jit(solution)/shard_map/ppermute | solution.py:210
  134.3 0.0 all-to-all-done.refs_0_
  134.3 0.0 copy-start.1
  134.3 1.2 copy-done.1
  135.5 0.0 copy-start.3
  135.5 1.2 copy-done.3
  136.7 0.0 copy-start.5
  136.7 1.2 copy-done.5
  137.9 3.1 %shard_map.101 = (f32[2,2,96,256]{3,2,1,0:T(8,128)S(1)}, f32[2,2,96,256]{3,2,1,0:T(8,128)S(1)}) custom-call(bf16[8,256,640]{2,1,0:T(8,128)(2,1)S(1)} %all-to-all-done.refs_0_, bf16[12,2,32,640]{3,2,1,0:T(8,128)(2,1)S(1)} %bitcast.5, bf16[12,2,32,640]{3,2,1,0:T(8,128)(2,1)S(1)} %copy-done.3, bf16[12,2,32,640]{3,2,1,0:T(8,128)(2,1)S(1)} %copy-done.5), custom_call_target="tpu_custom_call" | custom-call | flops 754974720 | bytes 4915200 | tf_op jit(solution)/shard_map/pallas_call | solution.py:133
  141.0 0.0 copy-start.6
  141.1 0.0 copy-start.7
  141.1 0.0 collective-permute-done.5.refs_2_
  141.1 2.4 %collective-permute-done.3.refs_1_ = bf16[6,2,32,640]{3,2,1,0:T(8,128)(2,1)} collective-permute-done((bf16[6,2,32,640]{3,2,1,0:T(8,128)(2,1)}, bf16[6,2,32,640]{3,2,1,0:T(8,128)(2,1)}, u32[]{:S(2)}, u32[]{:S(2)}) %collective-permute-start.3) | collective-permute-done | bytes 491552 | tf_op jit(solution)/shard_map/ppermute | solution.py:210
  143.5 1.7 %shard_map.102 = (f32[2,2,96,256]{3,2,1,0:T(8,128)S(1)}, f32[2,2,96,256]{3,2,1,0:T(8,128)S(1)}) custom-call(bf16[8,256,640]{2,1,0:T(8,128)(2,1)S(1)} %all-to-all-done.refs_0_, bf16[6,2,32,640]{3,2,1,0:T(8,128)(2,1)} %collective-permute-done.3.refs_1_, bf16[6,2,32,640]{3,2,1,0:T(8,128)(2,1)S(1)} %collective-permute-done.5.refs_2_, ...), custom_call_target="tpu_custom_call" | custom-call | flops 251658240 | bytes 1638400 | tf_op jit(solution)/shard_map/pallas_call | solution.py:133
  145.2 13.1 %collective-permute-start.6 = (f32[2,2,96,256]{3,2,1,0:T(8,128)S(1)}, f32[2,2,96,256]{3,2,1,0:T(8,128)S(1)}, u32[]{:S(2)}, u32[]{:S(2)}) collective-permute-start(f32[2,2,96,256]{3,2,1,0:T(8,128)S(1)} %get-tuple-element.20), channel_id=1, source_target_pairs={{0,1},{1,0},{2,3},{3,2},{4,5},{5,4},{6,7},{7,6},{8,9},{9,8},{10,11... | collective-permute-start | bytes 1179656 | tf_op jit(solution)/shard_map/ppermute | solution.py:214
  158.3 1.3 collective-permute-done.6.other
  159.6 0.0 copy-done.6
  159.7 0.0 copy-done.7
  159.7 0.7 shard_map.103
  160.4 3.0 %collective-permute-start.7 = (f32[4,3]{1,0:T(4,128)S(1)}, f32[4,3]{1,0:T(4,128)S(1)}, u32[]{:S(2)}, u32[]{:S(2)}) collective-permute-start(f32[4,3]{1,0:T(4,128)S(1)} %get-tuple-element.22), channel_id=1, source_target_pairs={{0,2},{2,0},{1,3},{3,1},{4,6},{6,4},{5,7},{7,5},{8,10},{10,8},{9,1... | collective-permute-start | bytes 152 | tf_op jit(solution)/shard_map/ppermute | solution.py:216
  163.3 1.3 collective-permute-done.7
  164.7 0.6 add.3
  (1 shorter events, 0.0 us)
Async XLA Ops:
  3.4 7.8 %copy-start.9 = (bf16[32,640]{1,0:T(8,128)(2,1)S(1)}, bf16[32,640]{1,0:T(8,128)(2,1)}, u32[]{:S(2)}) copy-start(bf16[32,640]{1,0:T(8,128)(2,1)} %get-tuple-element.15) | copy-start | bytes 122884
  3.4 8.5 %copy-start.8 = (bf16[32,640]{1,0:T(8,128)(2,1)S(1)}, bf16[32,640]{1,0:T(8,128)(2,1)}, u32[]{:S(2)}) copy-start(bf16[32,640]{1,0:T(8,128)(2,1)} %get-tuple-element.16) | copy-start | bytes 122884
  3.4 130.9 %all-to-all-start = ((bf16[8,256,640]{2,1,0:T(8,128)(2,1)}), bf16[8,256,640]{2,1,0:T(8,128)(2,1)S(1)}, u32[]{:S(2)}, u32[]{:S(2)}) async-start(bf16[8,256,640]{2,1,0:T(8,128)(2,1)} %get-tuple-element.14), calls=%async_computation | async-start | bytes 5242880 | tf_op jit(solution)/shard_map/all_to_all | solution.py:200
  11.2 4.0 %collective-permute-start = (bf16[32,640]{1,0:T(8,128)(2,1)S(1)}, bf16[32,640]{1,0:T(8,128)(2,1)S(1)}, u32[]{:S(2)}, u32[]{:S(2)}) collective-permute-start(bf16[32,640]{1,0:T(8,128)(2,1)S(1)} %copy-done.9), channel_id=1, source_target_pairs={{0,0},{2,2},{4,192},{6,194},{8,384},{10,386},{12,576},{14,578},{16... | collective-permute-start | bytes 122888 | tf_op jit(solution)/shard_map/ppermute | solution.py:203
  11.9 49.5 %collective-permute-start.1 = (bf16[32,640]{1,0:T(8,128)(2,1)S(1)}, bf16[32,640]{1,0:T(8,128)(2,1)S(1)}, u32[]{:S(2)}, u32[]{:S(2)}) collective-permute-start(bf16[32,640]{1,0:T(8,128)(2,1)S(1)} %copy-done.8), channel_id=1, source_target_pairs={{0,2},{2,0},{4,194},{6,192},{8,386},{10,384},{12,578},{14,576},{16... | collective-permute-start | bytes 122888 | tf_op jit(solution)/shard_map/ppermute | solution.py:204
  104.9 26.5 %copy-start = (bf16[24,32,640]{2,1,0:T(8,128)(2,1)}, bf16[24,32,640]{2,1,0:T(8,128)(2,1)S(1)}, u32[]{:S(2)}) copy-start(bf16[24,32,640]{2,1,0:T(8,128)(2,1)S(1)} %all-gather) | copy-start | bytes 2949124
  104.9 18.3 %collective-permute-start.4 = (bf16[12,2,32,640]{3,2,1,0:T(8,128)(2,1)S(1)}, bf16[12,2,32,640]{3,2,1,0:T(8,128)(2,1)S(1)}, u32[]{:S(2)}, u32[]{:S(2)}) collective-permute-start(bf16[12,2,32,640]{3,2,1,0:T(8,128)(2,1)S(1)} %bitcast.3), channel_id=1, source_target_pairs={{0,576},{192,0},{384,192},{576,384},{1,577},{193,1},{385,193},{577... | collective-permute-start | bytes 2949128 | tf_op jit(solution)/shard_map/ppermute | solution.py:208
  111.0 19.6 %collective-permute-start.2 = (bf16[12,2,32,640]{3,2,1,0:T(8,128)(2,1)S(1)}, bf16[12,2,32,640]{3,2,1,0:T(8,128)(2,1)S(1)}, u32[]{:S(2)}, u32[]{:S(2)}) collective-permute-start(bf16[12,2,32,640]{3,2,1,0:T(8,128)(2,1)S(1)} %bitcast.4), channel_id=1, source_target_pairs={{0,192},{192,384},{384,576},{576,0},{1,193},{193,385},{385,577},{5... | collective-permute-start | bytes 2949128 | tf_op jit(solution)/shard_map/ppermute | solution.py:209
  123.2 8.2 %copy-start.2 = (bf16[12,2,32,640]{3,2,1,0:T(8,128)(2,1)}, bf16[12,2,32,640]{3,2,1,0:T(8,128)(2,1)S(1)}, u32[]{:S(2)}) copy-start(bf16[12,2,32,640]{3,2,1,0:T(8,128)(2,1)S(1)} %collective-permute-done.4.refs_2_) | copy-start | bytes 2949124
  124.1 17.0 %collective-permute-start.5 = (bf16[6,2,32,640]{3,2,1,0:T(8,128)(2,1)}, bf16[6,2,32,640]{3,2,1,0:T(8,128)(2,1)S(1)}, u32[]{:S(2)}, u32[]{:S(2)}) collective-permute-start(bf16[6,2,32,640]{3,2,1,0:T(8,128)(2,1)} %slice.9), channel_id=1, source_target_pairs={{0,576},{192,0},{384,192},{576,384},{1,577},{193,1},{385,193},{577... | collective-permute-start | bytes 1474568 | tf_op jit(solution)/shard_map/ppermute | solution.py:211
  131.4 1.0 copy-start.4
  132.4 11.1 %collective-permute-start.3 = (bf16[6,2,32,640]{3,2,1,0:T(8,128)(2,1)}, bf16[6,2,32,640]{3,2,1,0:T(8,128)(2,1)}, u32[]{:S(2)}, u32[]{:S(2)}) collective-permute-start(bf16[6,2,32,640]{3,2,1,0:T(8,128)(2,1)} %slice.8), channel_id=1, source_target_pairs={{0,192},{192,384},{384,576},{576,0},{1,193},{193,385},{385,577},{5... | collective-permute-start | bytes 1474568 | tf_op jit(solution)/shard_map/ppermute | solution.py:210
  134.3 1.2 copy-start.1
  135.5 1.2 copy-start.3
  136.7 1.2 copy-start.5
  141.0 18.6 %copy-start.6 = (s32[1,4]{1,0:T(1,128)S(1)}, s32[1,4]{1,0:T(1,128)}, u32[]{:S(2)}) copy-start(s32[1,4]{1,0:T(1,128)} %tl.1) | copy-start | bytes 52
  141.1 18.6 %copy-start.7 = (s32[48]{0:T(128)S(1)}, s32[48]{0:T(128)}, u32[]{:S(2)}) copy-start(s32[48]{0:T(128)} %vl.1) | copy-start | bytes 580
  145.2 14.5 %collective-permute-start.6 = (f32[2,2,96,256]{3,2,1,0:T(8,128)S(1)}, f32[2,2,96,256]{3,2,1,0:T(8,128)S(1)}, u32[]{:S(2)}, u32[]{:S(2)}) collective-permute-start(f32[2,2,96,256]{3,2,1,0:T(8,128)S(1)} %get-tuple-element.20), channel_id=1, source_target_pairs={{0,1},{1,0},{2,3},{3,2},{4,5},{5,4},{6,7},{7,6},{8,9},{9,8},{10,11... | collective-permute-start | bytes 1179656 | tf_op jit(solution)/shard_map/ppermute | solution.py:214
  160.4 4.3 %collective-permute-start.7 = (f32[4,3]{1,0:T(4,128)S(1)}, f32[4,3]{1,0:T(4,128)S(1)}, u32[]{:S(2)}, u32[]{:S(2)}) collective-permute-start(f32[4,3]{1,0:T(4,128)S(1)} %get-tuple-element.22), channel_id=1, source_target_pairs={{0,2},{2,0},{1,3},{3,1},{4,6},{6,4},{5,7},{7,5},{8,10},{10,8},{9,1... | collective-permute-start | bytes 152 | tf_op jit(solution)/shard_map/ppermute | solution.py:216

commit v7 on v5

--- a/solution.py
+++ b/solution.py
@@ -54,27 +54,22 @@
     )(*arrays)
 
 
-NEAR = ((0, 2 * ROWS), (1, 2 * ROWS), (3, 2 * ROWS))
-FAR = ((2, ROWS), (2, ROWS))
-
-
-def gram_kernel(pieces, *refs):
-    n = len(pieces)
-    count = sum(rows for _, rows in pieces) // ROWS
-    train, vals, rest = refs[0], refs[1 : n + 1], refs[n + 1 :]
+def gram_kernel(shifts, *refs):
+    count = 2 * len(shifts)
+    train, vals, rest = refs[0], refs[1], refs[2:]
     before, (mine, send, tbuf, vbuf, tsem, vsem) = rest[:-6], rest[-6:]
     x = lax.axis_index("x")
     first = lax.axis_index("core") == 0
-    tcopy, vcopy, j = [], [], 0
-    for i, (ref, (shift, rows)) in enumerate(zip(vals, pieces)):
-        blocks = rows // ROWS
-        vcopy.append(
-            pltpu.make_async_copy(ref, vbuf.at[pl.ds(j * ROWS, rows)], vsem.at[i])
-        )
-        for h in range(blocks):
-            b = 2 * lax.rem(x + shift, NX) + (h if blocks == 2 else i)
-            tcopy.append(pltpu.make_async_copy(train.at[b], tbuf.at[j], tsem.at[j]))
-            j += 1
+    tcopy, vcopy = [], []
+    for i, shift in enumerate(shifts):
+        at = lax.rem(x + shift, NX)
+        source = vals.at[at] if before else vals
+        vcopy.append(pltpu.make_async_copy(source, vbuf.at[i], vsem.at[i]))
+        for h in range(2):
+            j = 2 * i + h
+            tcopy.append(
+                pltpu.make_async_copy(train.at[2 * at + h], tbuf.at[j], tsem.at[j])
+            )
     for c in (*vcopy, *tcopy):
         c.start()
     for c in vcopy:
@@ -85,7 +80,7 @@
             if g == 0:
                 tcopy[j].wait()
             d = lax.dot_general(
-                vbuf[j * ROWS : (j + 1) * ROWS, lo:hi],
+                vbuf[j // 2, (j % 2) * ROWS : (j % 2 + 1) * ROWS, lo:hi],
                 tbuf[j, :, lo:hi],
                 (((1,), (1,)), ((), ())),
                 preferred_element_type=jnp.float32,
@@ -99,30 +94,30 @@
         send[g] = give
 
 
-def grams(pieces, train, vals, before=()):
+def grams(shifts, train, vals, before=()):
     half = jax.ShapeDtypeStruct((4, HALF, TOK), jnp.float32)
-    count = sum(rows for _, rows in pieces) // ROWS
+    n = len(shifts)
     return pl.pallas_call(
-        functools.partial(gram_kernel, pieces),
+        functools.partial(gram_kernel, shifts),
         out_shape=(half, half),
-        in_specs=[ANY] * (1 + len(pieces)) + [VMEM] * len(before),
+        in_specs=[ANY] * 2 + [VMEM] * len(before),
         out_specs=(VMEM, VMEM),
         scratch_shapes=[
-            pltpu.VMEM((count, TOK, WIDTH), jnp.bfloat16),
-            pltpu.VMEM((count * ROWS, WIDTH), jnp.bfloat16),
-            pltpu.SemaphoreType.DMA((count,)),
-            pltpu.SemaphoreType.DMA((len(pieces),)),
+            pltpu.VMEM((2 * n, TOK, WIDTH), jnp.bfloat16),
+            pltpu.VMEM((n, 2 * ROWS, WIDTH), jnp.bfloat16),
+            pltpu.SemaphoreType.DMA((2 * n,)),
+            pltpu.SemaphoreType.DMA((n,)),
         ],
         compiler_params=pltpu.CompilerParams(vmem_limit_bytes=GRAM_MIB * MIB),
         cost_estimate=pl.CostEstimate(
-            flops=2 * count * ROWS * TOK * WIDTH,
-            bytes_accessed=2 * count * (ROWS + TOK) * WIDTH,
+            flops=4 * n * ROWS * TOK * WIDTH,
+            bytes_accessed=4 * n * (ROWS + TOK) * WIDTH,
             transcendentals=0,
         ),
-    )(train, *vals, *before)
+    )(train, vals, *before)
 
 
-GRAM_MIB = 48
+GRAM_MIB = 50
 
 
 def score_kernel(tl, vl, mine, other, out):
@@ -166,12 +161,10 @@
     full = lax.all_gather(train, "y", axis=0, tiled=False)
     val = lax.ppermute(val, ("x", "z", "y"), SWAP)
     own = lax.all_gather(val, "z", axis=0, tiled=True)
-    right = lax.ppermute(own, "x", around(NX, -1))
-    left = lax.ppermute(own, "x", around(NX, 1))
-    far0 = lax.ppermute(left[:ROWS], "x", around(NX, 1))
-    far1 = lax.ppermute(right[ROWS:], "x", around(NX, -1))
-    near = grams(NEAR, full, (own, right, left))
-    mine, send = grams(FAR, full, (far0, far1), near)
+    copies = jnp.broadcast_to(own[None], (NX, 2 * ROWS, WIDTH))
+    plane = lax.all_to_all(copies, "x", 0, 0, tiled=True)
+    near = grams((0,), full, own)
+    mine, send = grams((1, 3, 2), full, plane, near)
     other = lax.ppermute(send, "core", [(0, 1), (1, 0)])
     return scores_of(tl, vl, mine, other)
 

time: 119 us -> 130 us (1.092); the launches traced: 117 us -> 130 us
  waiting for transfers between devices: 19.5 us -> 38.8 us
  starting transfers between devices: 24.6 us -> 16.8 us
    all_to_all x0 -> x1, waiting for transfers between devices: none -> 25.9 us  [local(): plane = lax.all_to_all(copies, 'x', 0, 0, tiled=True)]
    ppermute x4 -> x0, waiting for transfers between devices: 18.1 us -> none  [the longest x1 14.9 us: local(): left = lax.ppermute(own, 'x', around(NX, 1))]
    ppermute x4 -> x0, starting transfers between devices: 16.2 us -> none  [the longest x1 5.93 us: local(): left = lax.ppermute(own, 'x', around(NX, 1))]
    all_gather x1, waiting for transfers between devices: 0.02 us -> 11.6 us  [local(): full = lax.all_gather(train, 'y', axis=0, tiled=False)]
    all_to_all x0 -> x1, starting transfers between devices: none -> 9.53 us  [local(): plane = lax.all_to_all(copies, 'x', 0, 0, tiled=True)]
    broadcast_in_dim x0 -> x1, local copies, waits for them, and re-layouts: none -> 2.07 us  [local(): copies = jnp.broadcast_to(own[None], (NX, 2 * ROWS, WIDTH))]
    slice x2 -> x0, local copies, waits for them, and re-layouts: 1.65 us -> none  [the longest x1 0.85 us: local(): far0 = lax.ppermute(left[:ROWS], 'x', around(NX, 1))]
  transfers between devices with their start and end apart: 7 -> 4, of which waited for: 4 -> 3; matrix products, arithmetic and copies ran while one was open for 1% -> 2% of each run, Pallas kernels for 3% -> 2%
where the time goes in v7:
time: 130 us
  blocking collectives  48.7 us (37%)
  waiting for transfers between devices  38.8 us (30%)
  starting transfers between devices  16.8 us (13%)
  between operations  13.4 us (10%)
  Pallas kernels  9.7 us (7%)
  local copies, waits for them, and re-layouts  2.07 us (2%)
    all_gather x1, blocking collectives, local(): own = lax.all_gather(val, 'z', axis=0, tiled=True)  48.7 us
    all_to_all x1, waiting for transfers between devices, local(): plane = lax.all_to_all(copies, 'x', 0, 0, tiled=True)  25.9 us
    all_gather x1, waiting for transfers between devices, local(): full = lax.all_gather(train, 'y', axis=0, tiled=False)  11.6 us
    all_to_all x1, starting transfers between devices, local(): plane = lax.all_to_all(copies, 'x', 0, 0, tiled=True)  9.53 us
    pallas_call x2, Pallas kernels, grams(): pl.pallas_call(functools.partial(gram_kernel, shifts), out_shape=(half, h...  6.39 us
    ppermute x1, starting transfers between devices, local(): other = lax.ppermute(send, 'core', [(0, 1), (1, 0)])  5.76 us
  transfers between devices with their start and end apart: 4, of which 3 were waited for; matrix products, arithmetic and copies ran while one was open for 2% of the time, Pallas kernels for 2%

profile of v7, /device:TPU:1, one launch (start us, length us, event | category | flops | bytes accessed | tf_op | source)
XLA Modules:
  0.0 129.6 jit_solution(13691429607009342094)
XLA Ops:
  6.5 0.0 all-gather.3.cloned.1.call-start
  6.5 2.1 %shard_map.100 = (bf16[256,1152]{1,0:T(8,128)(2,1)}, bf16[32,1152]{1,0:T(8,128)(2,1)}) custom-call(bf16[256,256]{1,0:T(8,128)(2,1)} %tx.1, bf16[256,256]{1,0:T(8,128)(2,1)} %ta.1, bf16[256,384]{1,0:T(8,128)(2,1)} %tq.1, bf16[256,256]{1,0:T(8,128)(2,1)} %to.1, bf16[1,32,256]{2,1,0:T(8,128)(2,1)} %vx.1, bf16[1,32,256]{2,1,0:T(8,128)(2,1)} %va.1, ...), custom_call_target="tpu_custom_call" | custom-call | tf_op jit(solution)/shard_map/pallas_call | solution.py:45
  8.6 0.0 all-gather.3.cloned.1.call-update
  8.6 1.5 %collective-permute-start = (bf16[32,1152]{1,0:T(8,128)(2,1)}, bf16[32,1152]{1,0:T(8,128)(2,1)S(1)}, u32[]{:S(2)}, u32[]{:S(2)}) collective-permute-start(bf16[32,1152]{1,0:T(8,128)(2,1)} %get-tuple-element.12), channel_id=1, source_target_pairs={{0,0},{16,16},{32,32},{48,48},{64,64},{80,80},{2,96},{18,112},{34,... | collective-permute-start | bytes 221192 | tf_op jit(solution)/shard_map/ppermute | solution.py:162
  10.2 0.0 collective-permute-done
  10.2 48.7 %all_gather.11.refs_1_ = bf16[384,1152]{1,0:T(8,128)(2,1)S(1)} all-gather(bf16[32,1152]{1,0:T(8,128)(2,1)S(1)} %collective-permute-done), channel_id=1, replica_groups=mesh['x'=4,'z'=12,'y'=8,'core'=2] {'z'}, dimensions={0}, use_global_device_ids=true | all-gather | bytes 958464 | tf_op jit(solution)/shard_map/all_gather | solution.py:163
  58.9 2.1 %broadcast_in_dim.2 = bf16[4,384,1152]{2,1,0:T(8,128)(2,1)} broadcast(bf16[384,1152]{1,0:T(8,128)(2,1)S(1)} %all_gather.11.refs_1_), dimensions={1,2} | broadcast | bytes 4423680 | tf_op jit(solution)/shard_map/broadcast_in_dim | solution.py:164
  61.0 9.5 %all-to-all-start = ((bf16[4,384,1152]{2,1,0:T(8,128)(2,1)}), bf16[4,384,1152]{2,1,0:T(8,128)(2,1)}, u32[]{:S(2)}, u32[]{:S(2)}) async-start(bf16[4,384,1152]{2,1,0:T(8,128)(2,1)} %broadcast_in_dim.2), calls=%async_computation | async-start | bytes 7077888 | tf_op jit(solution)/shard_map/all_to_all | solution.py:165
  70.5 11.6 %all-gather.3.cloned.1.call-done = bf16[2048,1152]{1,0:T(8,128)(2,1)} async-done(((bf16[256,1152]{1,0:T(8,128)(2,1)}), bf16[2048,1152]{1,0:T(8,128)(2,1)}) %all-gather.3.cloned.1.call-update) | async-done | bytes 4718608 | tf_op jit(solution)/shard_map/all_gather | solution.py:161
  82.1 2.0 %shard_map.101 = (f32[4,96,256]{2,1,0:T(8,128)S(1)}, f32[4,96,256]{2,1,0:T(8,128)S(1)}) custom-call(bf16[8,256,1152]{2,1,0:T(8,128)(2,1)} %bitcast.1, bf16[384,1152]{1,0:T(8,128)(2,1)S(1)} %all_gather.11.refs_1_), custom_call_target="tpu_custom_call" | custom-call | flops 226492416 | bytes 2064384 | tf_op jit(solution)/shard_map/pallas_call | solution.py:100
  84.1 25.9 %all-to-all-done.refs_1_ = bf16[4,384,1152]{2,1,0:T(8,128)(2,1)} async-done(((bf16[4,384,1152]{2,1,0:T(8,128)(2,1)}), bf16[4,384,1152]{2,1,0:T(8,128)(2,1)}, u32[]{:S(2)}, u32[]{:S(2)}) %all-to-all-start) | async-done | bytes 3538976 | tf_op jit(solution)/shard_map/all_to_all | solution.py:165
  109.9 0.0 copy-start
  110.0 0.0 copy-start.1
  110.0 4.4 %shard_map.102 = (f32[4,96,256]{2,1,0:T(8,128)S(1)}, f32[4,96,256]{2,1,0:T(8,128)S(1)}) custom-call(bf16[8,256,1152]{2,1,0:T(8,128)(2,1)} %bitcast.2, bf16[4,384,1152]{2,1,0:T(8,128)(2,1)} %all-to-all-done.refs_1_, f32[4,96,256]{2,1,0:T(8,128)S(1)} %get-tuple-element.13.refs_2_, f32[4,96,256]{2,1,0:T(8,128)S(1)} %get-tuple-element.14.refs_3_), custom_call_target="tpu_custom_call" | custom-call | flops 679477248 | bytes 6193152 | tf_op jit(solution)/shard_map/pallas_call | solution.py:100
  114.4 5.8 %collective-permute-start.1 = (f32[4,96,256]{2,1,0:T(8,128)S(1)}, f32[4,96,256]{2,1,0:T(8,128)S(1)}, u32[]{:S(2)}, u32[]{:S(2)}) collective-permute-start(f32[4,96,256]{2,1,0:T(8,128)S(1)} %get-tuple-element.16), channel_id=1, source_target_pairs={{0,1},{1,0},{2,3},{3,2},{4,5},{5,4},{6,7},{7,6},{8,9},{9,8},{10,11... | collective-permute-start | bytes 1179656 | tf_op jit(solution)/shard_map/ppermute | solution.py:168
  120.1 1.3 %collective-permute-done.1.other = f32[4,96,256]{2,1,0:T(8,128)S(1)} collective-permute-done((f32[4,96,256]{2,1,0:T(8,128)S(1)}, f32[4,96,256]{2,1,0:T(8,128)S(1)}, u32[]{:S(2)}, u32[]{:S(2)}) %collective-permute-start.1) | collective-permute-done | bytes 393248 | tf_op jit(solution)/shard_map/ppermute | solution.py:168
  121.5 0.0 copy-done
  121.5 0.0 copy-done.1
  121.5 1.3 shard_map.103
Async XLA Ops:
  6.5 75.6 %all-gather.3.cloned.1.call-start = ((), (), s32[]{:S(2)}) async-start(), calls=%async_computation.1 | async-start | bytes 5308416 | tf_op jit(solution)/shard_map/all_gather | solution.py:161
  8.6 1.5 %collective-permute-start = (bf16[32,1152]{1,0:T(8,128)(2,1)}, bf16[32,1152]{1,0:T(8,128)(2,1)S(1)}, u32[]{:S(2)}, u32[]{:S(2)}) collective-permute-start(bf16[32,1152]{1,0:T(8,128)(2,1)} %get-tuple-element.12), channel_id=1, source_target_pairs={{0,0},{16,16},{32,32},{48,48},{64,64},{80,80},{2,96},{18,112},{34,... | collective-permute-start | bytes 221192 | tf_op jit(solution)/shard_map/ppermute | solution.py:162
  61.0 49.0 %all-to-all-start = ((bf16[4,384,1152]{2,1,0:T(8,128)(2,1)}), bf16[4,384,1152]{2,1,0:T(8,128)(2,1)}, u32[]{:S(2)}, u32[]{:S(2)}) async-start(bf16[4,384,1152]{2,1,0:T(8,128)(2,1)} %broadcast_in_dim.2), calls=%async_computation | async-start | bytes 7077888 | tf_op jit(solution)/shard_map/all_to_all | solution.py:165
  109.9 11.5 %copy-start = (s32[1,4]{1,0:T(1,128)S(1)}, s32[1,4]{1,0:T(1,128)}, u32[]{:S(2)}) copy-start(s32[1,4]{1,0:T(1,128)} %tl.1) | copy-start | bytes 52
  110.0 11.5 %copy-start.1 = (s32[48]{0:T(128)S(1)}, s32[48]{0:T(128)}, u32[]{:S(2)}) copy-start(s32[48]{0:T(128)} %vl.1) | copy-start | bytes 580
  114.4 7.1 %collective-permute-start.1 = (f32[4,96,256]{2,1,0:T(8,128)S(1)}, f32[4,96,256]{2,1,0:T(8,128)S(1)}, u32[]{:S(2)}, u32[]{:S(2)}) collective-permute-start(f32[4,96,256]{2,1,0:T(8,128)S(1)} %get-tuple-element.16), channel_id=1, source_target_pairs={{0,1},{1,0},{2,3},{3,2},{4,5},{5,4},{6,7},{7,6},{8,9},{9,8},{10,11... | collective-permute-start | bytes 1179656 | tf_op jit(solution)/shard_map/ppermute | solution.py:168
Sparse Core Ops, SparseCore 0:
  9.7 72.3 all-gather.2

commit v8 on v5

--- a/solution.py
+++ b/solution.py
@@ -35,6 +35,13 @@
     return [(i, (i + shift) % size) for i in range(size)]
 
 
+APART = [
+    (x * NC + c, (x + (-1 if c else 1)) % NX * NC + c)
+    for x in range(NX)
+    for c in range(NC)
+]
+
+
 def join_kernel(tx, ta, tq, to, vx, va, vq, vo, train, val):
     for t, v, (lo, hi) in zip((tx, ta, tq, to), (vx, va, vq, vo), COLS):
         train[:, lo:hi] = t[...]
@@ -55,7 +62,7 @@
 
 
 NEAR = ((0, 2 * ROWS), (1, 2 * ROWS), (3, 2 * ROWS))
-FAR = ((2, ROWS), (2, ROWS))
+FAR = ((2, 2 * ROWS),)
 
 
 def gram_kernel(pieces, *refs):
@@ -168,10 +175,10 @@
     own = lax.all_gather(val, "z", axis=0, tiled=True)
     right = lax.ppermute(own, "x", around(NX, -1))
     left = lax.ppermute(own, "x", around(NX, 1))
-    far0 = lax.ppermute(left[:ROWS], "x", around(NX, 1))
-    far1 = lax.ppermute(right[ROWS:], "x", around(NX, -1))
+    onward = lax.select(lax.axis_index("core") == 0, left, right)
+    far = lax.ppermute(onward, ("x", "core"), APART)
     near = grams(NEAR, full, (own, right, left))
-    mine, send = grams(FAR, full, (far0, far1), near)
+    mine, send = grams(FAR, full, (far,), near)
     other = lax.ppermute(send, "core", [(0, 1), (1, 0)])
     return scores_of(tl, vl, mine, other)
 

time: 119 us -> 122 us (1.025); the launches traced: 117 us -> 122 us
  waiting for transfers between devices: 19.5 us -> 28 us
  starting transfers between devices: 24.6 us -> 21.8 us
  local copies, waits for them, and re-layouts: 1.66 us -> 0.01 us
    ppermute x2 -> x1, waiting for transfers between devices: 3.19 us -> 8.02 us  [local(): far = lax.ppermute(onward, ('x', 'core'), APART)]
    ppermute x2 -> x1, starting transfers between devices: 6.47 us -> 2.55 us  [local(): far = lax.ppermute(onward, ('x', 'core'), APART)]
    ppermute x1, waiting for transfers between devices: 0.01 us -> 3.66 us  [local(): right = lax.ppermute(own, 'x', around(NX, -1))]
    slice x2 -> x0, local copies, waits for them, and re-layouts: 1.65 us -> none  [the longest x1 0.85 us: local(): far0 = lax.ppermute(left[:ROWS], 'x', around(NX, 1))]
  transfers between devices with their start and end apart: 7 -> 6, of which waited for: 4 -> 4; matrix products, arithmetic and copies ran while one was open for 1% -> 1% of each run, Pallas kernels for 3% -> 3%
where the time goes in v8:
time: 122 us
  blocking collectives  48.7 us (40%)
  waiting for transfers between devices  28 us (23%)
  starting transfers between devices  21.8 us (18%)
  between operations  13.5 us (11%)
  Pallas kernels  8.92 us (7%)
    all_gather x1, blocking collectives, local(): own = lax.all_gather(val, 'z', axis=0, tiled=True)  48.7 us
    ppermute x1, waiting for transfers between devices, local(): left = lax.ppermute(own, 'x', around(NX, 1))  14.9 us
    ppermute x1, waiting for transfers between devices, local(): far = lax.ppermute(onward, ('x', 'core'), APART)  8.02 us
    ppermute x1, starting transfers between devices, local(): other = lax.ppermute(send, 'core', [(0, 1), (1, 0)])  7.99 us
    ppermute x1, starting transfers between devices, local(): left = lax.ppermute(own, 'x', around(NX, 1))  5.93 us
    pallas_call x2, Pallas kernels, grams(): pl.pallas_call(functools.partial(gram_kernel, pieces), out_shape=(half, h...  5.63 us
    ppermute x1, starting transfers between devices, local(): right = lax.ppermute(own, 'x', around(NX, -1))  3.8 us
    ppermute x1, waiting for transfers between devices, local(): right = lax.ppermute(own, 'x', around(NX, -1))  3.66 us
  transfers between devices with their start and end apart: 6, of which 4 were waited for; matrix products, arithmetic and copies ran while one was open for 1% of the time, Pallas kernels for 3%

profile of v8, /device:TPU:1, one launch (start us, length us, event | category | flops | bytes accessed | tf_op | source)
XLA Modules:
  0.0 122.0 jit_solution(12481035218728407300)
XLA Ops:
  6.5 0.0 all-gather.3.cloned.1.call-start
  6.5 2.0 %shard_map.100 = (bf16[256,1152]{1,0:T(8,128)(2,1)}, bf16[32,1152]{1,0:T(8,128)(2,1)}) custom-call(bf16[256,256]{1,0:T(8,128)(2,1)} %tx.1, bf16[256,256]{1,0:T(8,128)(2,1)} %ta.1, bf16[256,384]{1,0:T(8,128)(2,1)} %tq.1, bf16[256,256]{1,0:T(8,128)(2,1)} %to.1, bf16[1,32,256]{2,1,0:T(8,128)(2,1)} %vx.1, bf16[1,32,256]{2,1,0:T(8,128)(2,1)} %va.1, ...), custom_call_target="tpu_custom_call" | custom-call | tf_op jit(solution)/shard_map/pallas_call | solution.py:52
  8.6 0.0 all-gather.3.cloned.1.call-update
  8.6 1.5 %collective-permute-start = (bf16[32,1152]{1,0:T(8,128)(2,1)}, bf16[32,1152]{1,0:T(8,128)(2,1)S(1)}, u32[]{:S(2)}, u32[]{:S(2)}) collective-permute-start(bf16[32,1152]{1,0:T(8,128)(2,1)} %get-tuple-element.12), channel_id=1, source_target_pairs={{0,0},{16,16},{32,32},{48,48},{64,64},{80,80},{2,96},{18,112},{34,... | collective-permute-start | bytes 221192 | tf_op jit(solution)/shard_map/ppermute | solution.py:174
  10.1 0.0 collective-permute-done
  10.1 48.7 %all_gather.11.refs_1_ = bf16[384,1152]{1,0:T(8,128)(2,1)S(1)} all-gather(bf16[32,1152]{1,0:T(8,128)(2,1)S(1)} %collective-permute-done), channel_id=1, replica_groups=mesh['x'=4,'z'=12,'y'=8,'core'=2] {'z'}, dimensions={0}, use_global_device_ids=true | all-gather | bytes 958464 | tf_op jit(solution)/shard_map/all_gather | solution.py:175
  58.9 5.9 %collective-permute-start.1 = (bf16[384,1152]{1,0:T(8,128)(2,1)S(1)}, bf16[384,1152]{1,0:T(8,128)(2,1)S(1)}, u32[]{:S(2)}, u32[]{:S(2)}) collective-permute-start(bf16[384,1152]{1,0:T(8,128)(2,1)S(1)} %all_gather.11.refs_1_), channel_id=1, source_target_pairs={{0,192},{192,384},{384,576},{576,0},{1,193},{193,385},{385,577},{5... | collective-permute-start | bytes 2654216 | tf_op jit(solution)/shard_map/ppermute | solution.py:177
  64.8 3.8 %collective-permute-start.2 = (bf16[384,1152]{1,0:T(8,128)(2,1)S(1)}, bf16[384,1152]{1,0:T(8,128)(2,1)S(1)}, u32[]{:S(2)}, u32[]{:S(2)}) collective-permute-start(bf16[384,1152]{1,0:T(8,128)(2,1)S(1)} %all_gather.11.refs_1_), channel_id=1, source_target_pairs={{0,576},{192,0},{384,192},{576,384},{1,577},{193,1},{385,193},{577... | collective-permute-start | bytes 2654216 | tf_op jit(solution)/shard_map/ppermute | solution.py:176
  68.6 14.9 %collective-permute-done.1.refs_3_ = bf16[384,1152]{1,0:T(8,128)(2,1)S(1)} collective-permute-done((bf16[384,1152]{1,0:T(8,128)(2,1)S(1)}, bf16[384,1152]{1,0:T(8,128)(2,1)S(1)}, u32[]{:S(2)}, u32[]{:S(2)}) %collective-permute-start.1) | collective-permute-done | bytes 884768 | tf_op jit(solution)/shard_map/ppermute | solution.py:177
  83.6 3.7 %collective-permute-done.2.refs_2_ = bf16[384,1152]{1,0:T(8,128)(2,1)S(1)} collective-permute-done((bf16[384,1152]{1,0:T(8,128)(2,1)S(1)}, bf16[384,1152]{1,0:T(8,128)(2,1)S(1)}, u32[]{:S(2)}, u32[]{:S(2)}) %collective-permute-start.2) | collective-permute-done | bytes 884768 | tf_op jit(solution)/shard_map/ppermute | solution.py:176
  87.2 1.1 broadcast_select_fusion
  88.3 2.5 %collective-permute-start.3 = (bf16[384,1152]{1,0:T(8,128)(2,1)}, bf16[384,1152]{1,0:T(8,128)(2,1)S(1)}, u32[]{:S(2)}, u32[]{:S(2)}) collective-permute-start(bf16[384,1152]{1,0:T(8,128)(2,1)} %broadcast_select_fusion), channel_id=1, source_target_pairs={{0,192},{1,577},{192,384},{193,1},{384,576},{385,193},{576,0},{577... | collective-permute-start | bytes 2654216 | tf_op jit(solution)/shard_map/ppermute | solution.py:179
  90.8 0.0 all-gather.3.cloned.1.call-done
  90.9 3.6 %shard_map.101 = (f32[4,96,256]{2,1,0:T(8,128)S(1)}, f32[4,96,256]{2,1,0:T(8,128)S(1)}) custom-call(bf16[8,256,1152]{2,1,0:T(8,128)(2,1)} %bitcast.1, bf16[384,1152]{1,0:T(8,128)(2,1)S(1)} %all_gather.11.refs_1_, bf16[384,1152]{1,0:T(8,128)(2,1)S(1)} %collective-permute-done.2.refs_2_, bf16[384,1152]{1,0:T(8,128)(2,1)S(1)} %collective-permute-done.1.refs_3_), custom_call_target="tpu_custom_call" | custom-call | flops 679477248 | bytes 6193152 | tf_op jit(solution)/shard_map/pallas_call | solution.py:112
  94.5 0.0 copy-start
  94.5 0.0 copy-start.1
  94.5 8.0 %collective-permute-done.3.refs_1_ = bf16[384,1152]{1,0:T(8,128)(2,1)S(1)} collective-permute-done((bf16[384,1152]{1,0:T(8,128)(2,1)}, bf16[384,1152]{1,0:T(8,128)(2,1)S(1)}, u32[]{:S(2)}, u32[]{:S(2)}) %collective-permute-start.3) | collective-permute-done | bytes 884768 | tf_op jit(solution)/shard_map/ppermute | solution.py:179
  102.6 2.0 %shard_map.102 = (f32[4,96,256]{2,1,0:T(8,128)S(1)}, f32[4,96,256]{2,1,0:T(8,128)S(1)}) custom-call(bf16[8,256,1152]{2,1,0:T(8,128)(2,1)} %bitcast.2, bf16[384,1152]{1,0:T(8,128)(2,1)S(1)} %collective-permute-done.3.refs_1_, f32[4,96,256]{2,1,0:T(8,128)S(1)} %get-tuple-element.13.refs_2_, f32[4,96,256]{2,1,0:T(8,128)S(1)} %get-tuple-element.14.refs_3_), custom_call_target="tpu_custom_call" | custom-call | flops 226492416 | bytes 2064384 | tf_op jit(solution)/shard_map/pallas_call | solution.py:112
  104.6 8.0 %collective-permute-start.4 = (f32[4,96,256]{2,1,0:T(8,128)S(1)}, f32[4,96,256]{2,1,0:T(8,128)S(1)}, u32[]{:S(2)}, u32[]{:S(2)}) collective-permute-start(f32[4,96,256]{2,1,0:T(8,128)S(1)} %get-tuple-element.16), channel_id=1, source_target_pairs={{0,1},{1,0},{2,3},{3,2},{4,5},{5,4},{6,7},{7,6},{8,9},{9,8},{10,11... | collective-permute-start | bytes 1179656 | tf_op jit(solution)/shard_map/ppermute | solution.py:182
  112.6 1.3 %collective-permute-done.4.other = f32[4,96,256]{2,1,0:T(8,128)S(1)} collective-permute-done((f32[4,96,256]{2,1,0:T(8,128)S(1)}, f32[4,96,256]{2,1,0:T(8,128)S(1)}, u32[]{:S(2)}, u32[]{:S(2)}) %collective-permute-start.4) | collective-permute-done | bytes 393248 | tf_op jit(solution)/shard_map/ppermute | solution.py:182
  113.9 0.0 copy-done
  113.9 0.0 copy-done.1
  113.9 1.3 %shard_map.103 = f32[4,3]{1,0:T(4,128)} custom-call(s32[1,4]{1,0:T(1,128)S(1)} %copy-done, s32[48]{0:T(128)S(1)} %copy-done.1, f32[4,96,256]{2,1,0:T(8,128)S(1)} %get-tuple-element.15.mine, f32[4,96,256]{2,1,0:T(8,128)S(1)} %collective-permute-done.4.other), custom_call_target="tpu_custom_call" | custom-call | tf_op jit(solution)/shard_map/pallas_call | solution.py:162
Async XLA Ops:
  6.5 84.3 %all-gather.3.cloned.1.call-start = ((), (), s32[]{:S(2)}) async-start(), calls=%async_computation | async-start | bytes 5308416 | tf_op jit(solution)/shard_map/all_gather | solution.py:173
  8.6 1.5 %collective-permute-start = (bf16[32,1152]{1,0:T(8,128)(2,1)}, bf16[32,1152]{1,0:T(8,128)(2,1)S(1)}, u32[]{:S(2)}, u32[]{:S(2)}) collective-permute-start(bf16[32,1152]{1,0:T(8,128)(2,1)} %get-tuple-element.12), channel_id=1, source_target_pairs={{0,0},{16,16},{32,32},{48,48},{64,64},{80,80},{2,96},{18,112},{34,... | collective-permute-start | bytes 221192 | tf_op jit(solution)/shard_map/ppermute | solution.py:174
  58.9 24.7 %collective-permute-start.1 = (bf16[384,1152]{1,0:T(8,128)(2,1)S(1)}, bf16[384,1152]{1,0:T(8,128)(2,1)S(1)}, u32[]{:S(2)}, u32[]{:S(2)}) collective-permute-start(bf16[384,1152]{1,0:T(8,128)(2,1)S(1)} %all_gather.11.refs_1_), channel_id=1, source_target_pairs={{0,192},{192,384},{384,576},{576,0},{1,193},{193,385},{385,577},{5... | collective-permute-start | bytes 2654216 | tf_op jit(solution)/shard_map/ppermute | solution.py:177
  64.8 22.4 %collective-permute-start.2 = (bf16[384,1152]{1,0:T(8,128)(2,1)S(1)}, bf16[384,1152]{1,0:T(8,128)(2,1)S(1)}, u32[]{:S(2)}, u32[]{:S(2)}) collective-permute-start(bf16[384,1152]{1,0:T(8,128)(2,1)S(1)} %all_gather.11.refs_1_), channel_id=1, source_target_pairs={{0,576},{192,0},{384,192},{576,384},{1,577},{193,1},{385,193},{577... | collective-permute-start | bytes 2654216 | tf_op jit(solution)/shard_map/ppermute | solution.py:176
  88.3 14.3 %collective-permute-start.3 = (bf16[384,1152]{1,0:T(8,128)(2,1)}, bf16[384,1152]{1,0:T(8,128)(2,1)S(1)}, u32[]{:S(2)}, u32[]{:S(2)}) collective-permute-start(bf16[384,1152]{1,0:T(8,128)(2,1)} %broadcast_select_fusion), channel_id=1, source_target_pairs={{0,192},{1,577},{192,384},{193,1},{384,576},{385,193},{576,0},{577... | collective-permute-start | bytes 2654216 | tf_op jit(solution)/shard_map/ppermute | solution.py:179
  94.5 19.4 %copy-start = (s32[1,4]{1,0:T(1,128)S(1)}, s32[1,4]{1,0:T(1,128)}, u32[]{:S(2)}) copy-start(s32[1,4]{1,0:T(1,128)} %tl.1) | copy-start | bytes 52
  94.5 19.4 %copy-start.1 = (s32[48]{0:T(128)S(1)}, s32[48]{0:T(128)}, u32[]{:S(2)}) copy-start(s32[48]{0:T(128)} %vl.1) | copy-start | bytes 580
  104.6 9.3 %collective-permute-start.4 = (f32[4,96,256]{2,1,0:T(8,128)S(1)}, f32[4,96,256]{2,1,0:T(8,128)S(1)}, u32[]{:S(2)}, u32[]{:S(2)}) collective-permute-start(f32[4,96,256]{2,1,0:T(8,128)S(1)} %get-tuple-element.16), channel_id=1, source_target_pairs={{0,1},{1,0},{2,3},{3,2},{4,5},{5,4},{6,7},{7,6},{8,9},{9,8},{10,11... | collective-permute-start | bytes 1179656 | tf_op jit(solution)/shard_map/ppermute | solution.py:182
Sparse Core Ops, SparseCore 0:
  9.7 72.3 all-gather.2

commit v9 on v5

--- a/solution.py
+++ b/solution.py
@@ -35,21 +35,18 @@
     return [(i, (i + shift) % size) for i in range(size)]
 
 
-def join_kernel(tx, ta, tq, to, vx, va, vq, vo, train, val):
-    for t, v, (lo, hi) in zip((tx, ta, tq, to), (vx, va, vq, vo), COLS):
-        train[:, lo:hi] = t[...]
-        val[:, lo:hi] = v[0]
+def join_kernel(*refs):
+    *parts, out = refs
+    for part, (lo, hi) in zip(parts, COLS):
+        out[:, lo:hi] = part[...].reshape(out.shape[0], hi - lo)
 
 
-def join(*arrays):
+def join(rows, *arrays):
     return pl.pallas_call(
         join_kernel,
-        out_shape=(
-            jax.ShapeDtypeStruct((TOK, WIDTH), jnp.bfloat16),
-            jax.ShapeDtypeStruct((VLEN, WIDTH), jnp.bfloat16),
-        ),
-        in_specs=[VMEM] * 8,
-        out_specs=(VMEM, VMEM),
+        out_shape=jax.ShapeDtypeStruct((rows, WIDTH), jnp.bfloat16),
+        in_specs=[VMEM] * 4,
+        out_specs=VMEM,
         compiler_params=pltpu.CompilerParams(vmem_limit_bytes=60 * MIB),
     )(*arrays)
 
@@ -162,9 +159,11 @@
 
 
 def local(tx, ta, tq, to, tl, vx, va, vq, vo, vl):
-    train, val = join(tx, ta, tq, to, vx, va, vq, vo)
+    val = join(VLEN, vx, va, vq, vo)
+    val = lax.ppermute(val, ("x", "z", "y"), SWAP)
+    tx, ta, tq, to, val = lax.optimization_barrier((tx, ta, tq, to, val))
+    train = join(TOK, tx, ta, tq, to)
     full = lax.all_gather(train, "y", axis=0, tiled=False)
-    val = lax.ppermute(val, ("x", "z", "y"), SWAP)
     own = lax.all_gather(val, "z", axis=0, tiled=True)
     right = lax.ppermute(own, "x", around(NX, -1))
     left = lax.ppermute(own, "x", around(NX, 1))

time: 119 us -> 120 us (level); the launches traced: 117 us -> 120 us
  waiting for transfers between devices: 19.5 us -> 26.1 us
  starting transfers between devices: 24.6 us -> 20.8 us
  blocking collectives: 48.7 us -> 47.2 us
  Pallas kernels: 9.25 us -> 10.6 us
    all_gather x1, waiting for transfers between devices: 0.02 us -> 10.8 us  [local(): full = lax.all_gather(train, 'y', axis=0, tiled=False)]
    ppermute x1, starting transfers between devices: 6.85 us -> 2.59 us  [local(): other = lax.ppermute(send, 'core', [(0, 1), (1, 0)])]
    ppermute x1, waiting for transfers between devices: 2.96 us -> 0.01 us  [local(): far1 = lax.ppermute(right[ROWS:], 'x', around(NX, -1))]
    all_gather x1, blocking collectives: 48.7 us -> 47.2 us  [local(): own = lax.all_gather(val, 'z', axis=0, tiled=True)]
    pallas_call x1 -> x2, Pallas kernels: 2.04 us -> 3.4 us  [join(): pl.pallas_call(join_kernel, out_shape=jax.ShapeDtypeStruct((rows, WIDTH),...]
  transfers between devices with their start and end apart: 7 -> 7, of which waited for: 4 -> 3; matrix products, arithmetic and copies ran while one was open for 1% -> 1% of each run, Pallas kernels for 3% -> 3%
where the time goes in v9:
time: 120 us
  blocking collectives  47.2 us (39%)
  waiting for transfers between devices  26.1 us (22%)
  starting transfers between devices  20.8 us (17%)
  between operations  13.5 us (11%)
  Pallas kernels  10.6 us (9%)
  local copies, waits for them, and re-layouts  1.66 us (1%)
    all_gather x1, blocking collectives, local(): own = lax.all_gather(val, 'z', axis=0, tiled=True)  47.2 us
    ppermute x1, waiting for transfers between devices, local(): left = lax.ppermute(own, 'x', around(NX, 1))  13.9 us
    all_gather x1, waiting for transfers between devices, local(): full = lax.all_gather(train, 'y', axis=0, tiled=False)  10.8 us
    pallas_call x2, Pallas kernels, grams(): pl.pallas_call(functools.partial(gram_kernel, pieces), out_shape=(half, h...  5.97 us
    ppermute x1, starting transfers between devices, local(): left = lax.ppermute(own, 'x', around(NX, 1))  5.92 us
    ppermute x1, starting transfers between devices, local(): right = lax.ppermute(own, 'x', around(NX, -1))  3.77 us
    ppermute x1, starting transfers between devices, local(): far1 = lax.ppermute(right[ROWS:], 'x', around(NX, -1))  3.64 us
    pallas_call x2, Pallas kernels, join(): pl.pallas_call(join_kernel, out_shape=jax.ShapeDtypeStruct((rows, WIDTH),...  3.4 us
  transfers between devices with their start and end apart: 7, of which 3 were waited for; matrix products, arithmetic and copies ran while one was open for 1% of the time, Pallas kernels for 3%

profile of v9, /device:TPU:1, one launch (start us, length us, event | category | flops | bytes accessed | tf_op | source)
XLA Modules:
  0.0 119.9 jit_solution(3974006710774744390)
XLA Ops:
  6.5 0.0 all-gather.3.cloned.1.call-start
  6.5 1.4 %shard_map.100 = bf16[32,1152]{1,0:T(8,128)(2,1)} custom-call(bf16[1,32,256]{2,1,0:T(8,128)(2,1)} %refs_0_.1, bf16[1,32,256]{2,1,0:T(8,128)(2,1)} %refs_1_.1, bf16[1,32,384]{2,1,0:T(8,128)(2,1)} %refs_2_.1, bf16[1,32,256]{2,1,0:T(8,128)(2,1)} %refs_3_.1), custom_call_target="tpu_custom_call" | custom-call | tf_op jit(solution)/shard_map/pallas_call | solution.py:45
  7.9 1.5 %collective-permute-start = (bf16[32,1152]{1,0:T(8,128)(2,1)}, bf16[32,1152]{1,0:T(8,128)(2,1)S(1)}, u32[]{:S(2)}, u32[]{:S(2)}) collective-permute-start(bf16[32,1152]{1,0:T(8,128)(2,1)} %shard_map.100), channel_id=1, source_target_pairs={{0,0},{16,16},{32,32},{48,48},{64,64},{80,80},{2,96},{18,112},{34,... | collective-permute-start | bytes 221192 | tf_op jit(solution)/shard_map/ppermute | solution.py:163
  9.5 0.0 collective-permute-done
  9.5 2.0 %shard_map.101 = bf16[256,1152]{1,0:T(8,128)(2,1)} custom-call(bf16[256,256]{1,0:T(8,128)(2,1)} %refs_0_.2, bf16[256,256]{1,0:T(8,128)(2,1)} %refs_1_.2, bf16[256,384]{1,0:T(8,128)(2,1)} %refs_2_.2, bf16[256,256]{1,0:T(8,128)(2,1)} %refs_3_.2), custom_call_target="tpu_custom_call" | custom-call | tf_op jit(solution)/shard_map/pallas_call | solution.py:45
  11.5 0.0 all-gather.3.cloned.1.call-update
  11.5 47.2 %all_gather.11.refs_1_ = bf16[384,1152]{1,0:T(8,128)(2,1)S(1)} all-gather(bf16[32,1152]{1,0:T(8,128)(2,1)S(1)} %collective-permute-done), channel_id=1, replica_groups=mesh['x'=4,'z'=12,'y'=8,'core'=2] {'z'}, dimensions={0}, use_global_device_ids=true | all-gather | bytes 958464 | tf_op jit(solution)/shard_map/all_gather | solution.py:167
  58.7 5.9 %collective-permute-start.1 = (bf16[384,1152]{1,0:T(8,128)(2,1)S(1)}, bf16[384,1152]{1,0:T(8,128)(2,1)S(1)}, u32[]{:S(2)}, u32[]{:S(2)}) collective-permute-start(bf16[384,1152]{1,0:T(8,128)(2,1)S(1)} %all_gather.11.refs_1_), channel_id=1, source_target_pairs={{0,192},{192,384},{384,576},{576,0},{1,193},{193,385},{385,577},{5... | collective-permute-start | bytes 2654216 | tf_op jit(solution)/shard_map/ppermute | solution.py:169
  64.6 3.8 %collective-permute-start.3 = (bf16[384,1152]{1,0:T(8,128)(2,1)S(1)}, bf16[384,1152]{1,0:T(8,128)(2,1)S(1)}, u32[]{:S(2)}, u32[]{:S(2)}) collective-permute-start(bf16[384,1152]{1,0:T(8,128)(2,1)S(1)} %all_gather.11.refs_1_), channel_id=1, source_target_pairs={{0,576},{192,0},{384,192},{576,384},{1,577},{193,1},{385,193},{577... | collective-permute-start | bytes 2654216 | tf_op jit(solution)/shard_map/ppermute | solution.py:168
  68.4 13.9 %collective-permute-done.1.refs_3_ = bf16[384,1152]{1,0:T(8,128)(2,1)S(1)} collective-permute-done((bf16[384,1152]{1,0:T(8,128)(2,1)S(1)}, bf16[384,1152]{1,0:T(8,128)(2,1)S(1)}, u32[]{:S(2)}, u32[]{:S(2)}) %collective-permute-start.1) | collective-permute-done | bytes 884768 | tf_op jit(solution)/shard_map/ppermute | solution.py:169
  82.3 0.8 slice.8
  83.1 3.3 %collective-permute-start.2 = (bf16[192,1152]{1,0:T(8,128)(2,1)}, bf16[192,1152]{1,0:T(8,128)(2,1)S(1)}, u32[]{:S(2)}, u32[]{:S(2)}) collective-permute-start(bf16[192,1152]{1,0:T(8,128)(2,1)} %slice.8), channel_id=1, source_target_pairs={{0,192},{192,384},{384,576},{576,0},{1,193},{193,385},{385,577},{5... | collective-permute-start | bytes 1327112 | tf_op jit(solution)/shard_map/ppermute | solution.py:170
  86.5 0.0 collective-permute-done.3.refs_2_
  86.5 0.8 slice.9
  87.3 3.6 %collective-permute-start.4 = (bf16[192,1152]{1,0:T(8,128)(2,1)}, bf16[192,1152]{1,0:T(8,128)(2,1)S(1)}, u32[]{:S(2)}, u32[]{:S(2)}) collective-permute-start(bf16[192,1152]{1,0:T(8,128)(2,1)} %slice.9), channel_id=1, source_target_pairs={{0,576},{192,0},{384,192},{576,384},{1,577},{193,1},{385,193},{577... | collective-permute-start | bytes 1327112 | tf_op jit(solution)/shard_map/ppermute | solution.py:171
  90.9 10.8 %all-gather.3.cloned.1.call-done = bf16[2048,1152]{1,0:T(8,128)(2,1)} async-done(((bf16[256,1152]{1,0:T(8,128)(2,1)}), bf16[2048,1152]{1,0:T(8,128)(2,1)}) %all-gather.3.cloned.1.call-update) | async-done | bytes 4718608 | tf_op jit(solution)/shard_map/all_gather | solution.py:166
  101.8 3.6 %shard_map.102 = (f32[4,96,256]{2,1,0:T(8,128)S(1)}, f32[4,96,256]{2,1,0:T(8,128)S(1)}) custom-call(bf16[8,256,1152]{2,1,0:T(8,128)(2,1)} %bitcast.1, bf16[384,1152]{1,0:T(8,128)(2,1)S(1)} %all_gather.11.refs_1_, bf16[384,1152]{1,0:T(8,128)(2,1)S(1)} %collective-permute-done.3.refs_2_, bf16[384,1152]{1,0:T(8,128)(2,1)S(1)} %collective-permute-done.1.refs_3_), custom_call_target="tpu_custom_call" | custom-call | flops 679477248 | bytes 6193152 | tf_op jit(solution)/shard_map/pallas_call | solution.py:102
  105.4 0.0 copy-start
  105.4 0.0 copy-start.1
  105.4 0.0 collective-permute-done.2.refs_1_
  105.4 0.0 collective-permute-done.4.refs_2_
  105.4 2.3 %shard_map.103 = (f32[4,96,256]{2,1,0:T(8,128)S(1)}, f32[4,96,256]{2,1,0:T(8,128)S(1)}) custom-call(bf16[8,256,1152]{2,1,0:T(8,128)(2,1)} %bitcast.2, bf16[192,1152]{1,0:T(8,128)(2,1)S(1)} %collective-permute-done.2.refs_1_, bf16[192,1152]{1,0:T(8,128)(2,1)S(1)} %collective-permute-done.4.refs_2_, f32[4,96,256]{2,1,0:T(8,128)S(1)} %get-tuple-element.19.refs_3_, ...), custom_call_target="tpu_custom_call" | custom-call | flops 226492416 | bytes 2064384 | tf_op jit(solution)/shard_map/pallas_call | solution.py:102
  107.8 2.6 %collective-permute-start.5 = (f32[4,96,256]{2,1,0:T(8,128)S(1)}, f32[4,96,256]{2,1,0:T(8,128)S(1)}, u32[]{:S(2)}, u32[]{:S(2)}) collective-permute-start(f32[4,96,256]{2,1,0:T(8,128)S(1)} %get-tuple-element.22), channel_id=1, source_target_pairs={{0,1},{1,0},{2,3},{3,2},{4,5},{5,4},{6,7},{7,6},{8,9},{9,8},{10,11... | collective-permute-start | bytes 1179656 | tf_op jit(solution)/shard_map/ppermute | solution.py:174
  110.4 1.3 %collective-permute-done.5.other = f32[4,96,256]{2,1,0:T(8,128)S(1)} collective-permute-done((f32[4,96,256]{2,1,0:T(8,128)S(1)}, f32[4,96,256]{2,1,0:T(8,128)S(1)}, u32[]{:S(2)}, u32[]{:S(2)}) %collective-permute-start.5) | collective-permute-done | bytes 393248 | tf_op jit(solution)/shard_map/ppermute | solution.py:174
  111.7 0.0 copy-done
  111.7 0.0 copy-done.1
  111.7 1.3 %shard_map.104 = f32[4,3]{1,0:T(4,128)} custom-call(s32[1,4]{1,0:T(1,128)S(1)} %copy-done, s32[48]{0:T(128)S(1)} %copy-done.1, f32[4,96,256]{2,1,0:T(8,128)S(1)} %get-tuple-element.21.mine, f32[4,96,256]{2,1,0:T(8,128)S(1)} %collective-permute-done.5.other), custom_call_target="tpu_custom_call" | custom-call | tf_op jit(solution)/shard_map/pallas_call | solution.py:152
Async XLA Ops:
  6.5 95.2 %all-gather.3.cloned.1.call-start = ((), (), s32[]{:S(2)}) async-start(), calls=%async_computation | async-start | bytes 5308416 | tf_op jit(solution)/shard_map/all_gather | solution.py:166
  7.9 1.5 %collective-permute-start = (bf16[32,1152]{1,0:T(8,128)(2,1)}, bf16[32,1152]{1,0:T(8,128)(2,1)S(1)}, u32[]{:S(2)}, u32[]{:S(2)}) collective-permute-start(bf16[32,1152]{1,0:T(8,128)(2,1)} %shard_map.100), channel_id=1, source_target_pairs={{0,0},{16,16},{32,32},{48,48},{64,64},{80,80},{2,96},{18,112},{34,... | collective-permute-start | bytes 221192 | tf_op jit(solution)/shard_map/ppermute | solution.py:163
  58.7 23.6 %collective-permute-start.1 = (bf16[384,1152]{1,0:T(8,128)(2,1)S(1)}, bf16[384,1152]{1,0:T(8,128)(2,1)S(1)}, u32[]{:S(2)}, u32[]{:S(2)}) collective-permute-start(bf16[384,1152]{1,0:T(8,128)(2,1)S(1)} %all_gather.11.refs_1_), channel_id=1, source_target_pairs={{0,192},{192,384},{384,576},{576,0},{1,193},{193,385},{385,577},{5... | collective-permute-start | bytes 2654216 | tf_op jit(solution)/shard_map/ppermute | solution.py:169
  64.6 21.9 %collective-permute-start.3 = (bf16[384,1152]{1,0:T(8,128)(2,1)S(1)}, bf16[384,1152]{1,0:T(8,128)(2,1)S(1)}, u32[]{:S(2)}, u32[]{:S(2)}) collective-permute-start(bf16[384,1152]{1,0:T(8,128)(2,1)S(1)} %all_gather.11.refs_1_), channel_id=1, source_target_pairs={{0,576},{192,0},{384,192},{576,384},{1,577},{193,1},{385,193},{577... | collective-permute-start | bytes 2654216 | tf_op jit(solution)/shard_map/ppermute | solution.py:168
  83.1 22.3 %collective-permute-start.2 = (bf16[192,1152]{1,0:T(8,128)(2,1)}, bf16[192,1152]{1,0:T(8,128)(2,1)S(1)}, u32[]{:S(2)}, u32[]{:S(2)}) collective-permute-start(bf16[192,1152]{1,0:T(8,128)(2,1)} %slice.8), channel_id=1, source_target_pairs={{0,192},{192,384},{384,576},{576,0},{1,193},{193,385},{385,577},{5... | collective-permute-start | bytes 1327112 | tf_op jit(solution)/shard_map/ppermute | solution.py:170
  87.3 18.1 %collective-permute-start.4 = (bf16[192,1152]{1,0:T(8,128)(2,1)}, bf16[192,1152]{1,0:T(8,128)(2,1)S(1)}, u32[]{:S(2)}, u32[]{:S(2)}) collective-permute-start(bf16[192,1152]{1,0:T(8,128)(2,1)} %slice.9), channel_id=1, source_target_pairs={{0,576},{192,0},{384,192},{576,384},{1,577},{193,1},{385,193},{577... | collective-permute-start | bytes 1327112 | tf_op jit(solution)/shard_map/ppermute | solution.py:171
  105.4 6.3 %copy-start = (s32[1,4]{1,0:T(1,128)S(1)}, s32[1,4]{1,0:T(1,128)}, u32[]{:S(2)}) copy-start(s32[1,4]{1,0:T(1,128)} %tl.1) | copy-start | bytes 52
  105.4 6.3 %copy-start.1 = (s32[48]{0:T(128)S(1)}, s32[48]{0:T(128)}, u32[]{:S(2)}) copy-start(s32[48]{0:T(128)} %vl.1) | copy-start | bytes 580
  107.8 3.9 %collective-permute-start.5 = (f32[4,96,256]{2,1,0:T(8,128)S(1)}, f32[4,96,256]{2,1,0:T(8,128)S(1)}, u32[]{:S(2)}, u32[]{:S(2)}) collective-permute-start(f32[4,96,256]{2,1,0:T(8,128)S(1)} %get-tuple-element.22), channel_id=1, source_target_pairs={{0,1},{1,0},{2,3},{3,2},{4,5},{5,4},{6,7},{7,6},{8,9},{9,8},{10,11... | collective-permute-start | bytes 1179656 | tf_op jit(solution)/shard_map/ppermute | solution.py:174
Sparse Core Ops, SparseCore 0:
  11.6 90.1 all-gather.2

commit v10 on v4

--- a/solution.py
+++ b/solution.py
@@ -52,62 +52,90 @@
     )(*arrays)
 
 
-def gram_kernel(train, own, right, left, far0, far1, mine, send, tbuf, vbuf, tsem, vsem):
+NEAR = (0, 1, 3)
+PARAMS = dict(vmem_limit_bytes=48 * MIB)
+PART = jax.ShapeDtypeStruct((4, HALF, TOK), jnp.float32)
+
+
+def products(blocks, trains, waits=None):
+    for g, (lo, hi) in enumerate(COLS):
+        acc = None
+        for j, (block, t) in enumerate(zip(blocks, trains)):
+            if g == 0 and waits:
+                waits[j].wait()
+            d = lax.dot_general(
+                block[:, lo:hi],
+                t[:, lo:hi],
+                (((1,), (1,)), ((), ())),
+                preferred_element_type=jnp.float32,
+            )
+            acc = d if acc is None else acc + d
+        yield g, acc[:HALF], acc[HALF:]
+
+
+def near_kernel(train, *refs):
+    vals, (mine, send, tfar, tbuf, vbuf, tsem, vsem) = refs[:3], refs[3:]
     x = lax.axis_index("x")
     first = lax.axis_index("core") == 0
-    opposite = lax.rem(x + 2, NX)
     vcopy = [
-        pltpu.make_async_copy(src, dst, vsem.at[i])
-        for i, (src, dst) in enumerate(
-            (
-                (own, vbuf.at[x]),
-                (right, vbuf.at[lax.rem(x + 1, NX)]),
-                (left, vbuf.at[lax.rem(x + 3, NX)]),
-                (far0, vbuf.at[opposite, 0:ROWS]),
-                (far1, vbuf.at[opposite, ROWS : 2 * ROWS]),
-            )
-        )
+        pltpu.make_async_copy(v, vbuf.at[i], vsem.at[i]) for i, v in enumerate(vals)
     ]
-    tcopy = [
-        pltpu.make_async_copy(train.at[:, :, lo:hi], tbuf.at[:, :, lo:hi], tsem.at[g])
-        for g, (lo, hi) in enumerate(COLS)
-    ]
-    for c in (*tcopy, *vcopy):
+    tcopy = []
+    for j in range(NY):
+        shift = (*NEAR, 2)[j // 2]
+        b = 2 * lax.rem(x + shift, NX) + j % 2
+        target = tbuf.at[j] if j < 6 else tfar.at[j - 6]
+        tcopy.append(pltpu.make_async_copy(train.at[b], target, tsem.at[j]))
+    for c in (*vcopy, *tcopy):
         c.start()
     for c in vcopy:
         c.wait()
-    for g, (lo, hi) in enumerate(COLS):
-        tcopy[g].wait()
-        acc = jnp.zeros((ROWS, TOK), jnp.float32)
-        for b in range(NY):
-            acc += lax.dot_general(
-                vbuf[b // 2, (b % 2) * ROWS : (b % 2 + 1) * ROWS, lo:hi],
-                tbuf[b, :, lo:hi],
-                (((1,), (1,)), ((), ())),
-                preferred_element_type=jnp.float32,
-            )
-        send[g] = jnp.where(first, acc[HALF:], acc[:HALF])
-        mine[g] = jnp.where(first, acc[:HALF], acc[HALF:])
-
-
-def grams(*arrays):
-    half = jax.ShapeDtypeStruct((4, HALF, TOK), jnp.float32)
-    return pl.pallas_call(
-        gram_kernel,
-        out_shape=(half, half),
-        in_specs=[ANY] * 6,
+    blocks = [
+        vbuf.at[j // 2, (j % 2) * ROWS : (j % 2 + 1) * ROWS] for j in range(6)
+    ]
+    for g, zero, one in products(blocks, [tbuf.at[j] for j in range(6)], tcopy):
+        mine[g] = jnp.where(first, zero, one)
+        send[g] = jnp.where(first, one, zero)
+    for c in tcopy[6:]:
+        c.wait()
+
+
+def near_grams(train, *vals):
+    return pl.pallas_call(
+        near_kernel,
+        out_shape=(PART, PART, jax.ShapeDtypeStruct((2, TOK, WIDTH), jnp.bfloat16)),
+        in_specs=[ANY] * 4,
+        out_specs=(VMEM,) * 3,
+        scratch_shapes=[
+            pltpu.VMEM((6, TOK, WIDTH), jnp.bfloat16),
+            pltpu.VMEM((3, 2 * ROWS, WIDTH), jnp.bfloat16),
+            pltpu.SemaphoreType.DMA((NY,)),
+            pltpu.SemaphoreType.DMA((3,)),
+        ],
+        compiler_params=pltpu.CompilerParams(**PARAMS),
+        cost_estimate=pl.CostEstimate(
+            flops=12 * ROWS * TOK * WIDTH,
+            bytes_accessed=12 * (ROWS + TOK) * WIDTH,
+            transcendentals=0,
+        ),
+    )(train, *vals)
+
+
+def far_kernel(tfar, far0, far1, mine0, send0, mine, send):
+    first = lax.axis_index("core") == 0
+    for g, zero, one in products([far0, far1], [tfar.at[0], tfar.at[1]]):
+        mine[g] = mine0[g] + jnp.where(first, zero, one)
+        send[g] = send0[g] + jnp.where(first, one, zero)
+
+
+def far_grams(*arrays):
+    return pl.pallas_call(
+        far_kernel,
+        out_shape=(PART, PART),
+        in_specs=[VMEM] * 5,
         out_specs=(VMEM, VMEM),
-        scratch_shapes=[
-            pltpu.VMEM((NY, TOK, WIDTH), jnp.bfloat16),
-            pltpu.VMEM((NX, 2 * ROWS, WIDTH), jnp.bfloat16),
-            pltpu.SemaphoreType.DMA((4,)),
-            pltpu.SemaphoreType.DMA((5,)),
-        ],
-        compiler_params=pltpu.CompilerParams(vmem_limit_bytes=GRAM_MIB * MIB),
+        compiler_params=pltpu.CompilerParams(**PARAMS),
     )(*arrays)
-
-
-GRAM_MIB = 50
 
 
 def score_kernel(tl, vl, mine, other, out):
@@ -155,7 +183,8 @@
     left = lax.ppermute(own, "x", around(NX, 1))
     far0 = lax.ppermute(left[:ROWS], "x", around(NX, 1))
     far1 = lax.ppermute(right[ROWS:], "x", around(NX, -1))
-    mine, send = grams(full, own, right, left, far0, far1)
+    mine, send, tfar = near_grams(full, own, right, left)
+    mine, send = far_grams(tfar, far0, far1, mine, send)
     other = lax.ppermute(send, "core", [(0, 1), (1, 0)])
     return scores_of(tl, vl, mine, other)
 

time: 121 us -> 117 us (0.967)
  waiting for transfers between devices: 23.5 us -> 19.5 us
  Pallas kernels: 9.22 us -> 7.5 us
  local copies, waits for them, and re-layouts: 0.09 us -> 1.66 us
    ppermute x1, waiting for transfers between devices: 4.47 us -> 0.22 us  [local(): far0 = lax.ppermute(left[:ROWS], 'x', around(NX, 1))]
    pallas_call x1 -> x2, Pallas kernels: 5.93 us -> 4.2 us  [the longest x1 3.67 us: near_grams(): pl.pallas_call(near_kernel, out_shape=(PART, PART, jax.ShapeDtypeStruct((...]
  transfers between devices with their start and end apart: 7 -> 7, of which waited for: 5 -> 4; matrix products, arithmetic and copies ran while one was open for 0% -> 1% of each run, Pallas kernels for 0% -> 3%
where the time goes in v10:
time: 117 us; the launch traced here: 115 us
  blocking collectives  48.7 us (42%)
  starting transfers between devices  24.6 us (21%)
  waiting for transfers between devices  19.5 us (17%)
  between operations  13.5 us (12%)
  Pallas kernels  7.5 us (6%)
  local copies, waits for them, and re-layouts  1.66 us (1%)
    all_gather x1, blocking collectives, local(): own = lax.all_gather(val, 'z', axis=0, tiled=True)  48.7 us
    ppermute x1, waiting for transfers between devices, local(): left = lax.ppermute(own, 'x', around(NX, 1))  14.9 us
    ppermute x1, starting transfers between devices, local(): other = lax.ppermute(send, 'core', [(0, 1), (1, 0)])  6.85 us
    ppermute x1, starting transfers between devices, local(): left = lax.ppermute(own, 'x', around(NX, 1))  5.93 us
    ppermute x1, starting transfers between devices, local(): right = lax.ppermute(own, 'x', around(NX, -1))  3.8 us
    pallas_call x1, Pallas kernels, near_grams(): pl.pallas_call(near_kernel, out_shape=(PART, PART, jax.ShapeDtypeStruct((...  3.67 us
    ppermute x1, starting transfers between devices, local(): far1 = lax.ppermute(right[ROWS:], 'x', around(NX, -1))  3.57 us
    ppermute x1, waiting for transfers between devices, local(): far1 = lax.ppermute(right[ROWS:], 'x', around(NX, -1))  2.96 us
  transfers between devices with their start and end apart: 7, of which 4 were waited for; matrix products, arithmetic and copies ran while one was open for 1% of the time, Pallas kernels for 3%

profile of v10, /device:TPU:1, one launch (start us, length us, event | category | flops | bytes accessed | tf_op | source)
XLA Modules:
  0.0 115.4 jit_solution(12524167694820601276)
XLA Ops:
  6.5 0.0 all-gather.3.cloned.1.call-start
  6.5 2.0 %shard_map.100 = (bf16[256,1152]{1,0:T(8,128)(2,1)}, bf16[32,1152]{1,0:T(8,128)(2,1)}) custom-call(bf16[256,256]{1,0:T(8,128)(2,1)} %tx.1, bf16[256,256]{1,0:T(8,128)(2,1)} %ta.1, bf16[256,384]{1,0:T(8,128)(2,1)} %tq.1, bf16[256,256]{1,0:T(8,128)(2,1)} %to.1, bf16[1,32,256]{2,1,0:T(8,128)(2,1)} %vx.1, bf16[1,32,256]{2,1,0:T(8,128)(2,1)} %va.1, ...), custom_call_target="tpu_custom_call" | custom-call | tf_op jit(solution)/shard_map/pallas_call | solution.py:43
  8.6 0.0 all-gather.3.cloned.1.call-update
  8.6 1.5 %collective-permute-start = (bf16[32,1152]{1,0:T(8,128)(2,1)}, bf16[32,1152]{1,0:T(8,128)(2,1)S(1)}, u32[]{:S(2)}, u32[]{:S(2)}) collective-permute-start(bf16[32,1152]{1,0:T(8,128)(2,1)} %get-tuple-element.13), channel_id=1, source_target_pairs={{0,0},{16,16},{32,32},{48,48},{64,64},{80,80},{2,96},{18,112},{34,... | collective-permute-start | bytes 221192 | tf_op jit(solution)/shard_map/ppermute | solution.py:180
  10.1 0.0 collective-permute-done
  10.1 48.7 %all_gather.11.refs_0_ = bf16[384,1152]{1,0:T(8,128)(2,1)S(1)} all-gather(bf16[32,1152]{1,0:T(8,128)(2,1)S(1)} %collective-permute-done), channel_id=1, replica_groups=mesh['x'=4,'z'=12,'y'=8,'core'=2] {'z'}, dimensions={0}, use_global_device_ids=true | all-gather | bytes 958464 | tf_op jit(solution)/shard_map/all_gather | solution.py:181
  58.9 5.9 %collective-permute-start.2 = (bf16[384,1152]{1,0:T(8,128)(2,1)S(1)}, bf16[384,1152]{1,0:T(8,128)(2,1)S(1)}, u32[]{:S(2)}, u32[]{:S(2)}) collective-permute-start(bf16[384,1152]{1,0:T(8,128)(2,1)S(1)} %all_gather.11.refs_0_), channel_id=1, source_target_pairs={{0,192},{192,384},{384,576},{576,0},{1,193},{193,385},{385,577},{5... | collective-permute-start | bytes 2654216 | tf_op jit(solution)/shard_map/ppermute | solution.py:183
  64.8 3.8 %collective-permute-start.1 = (bf16[384,1152]{1,0:T(8,128)(2,1)S(1)}, bf16[384,1152]{1,0:T(8,128)(2,1)S(1)}, u32[]{:S(2)}, u32[]{:S(2)}) collective-permute-start(bf16[384,1152]{1,0:T(8,128)(2,1)S(1)} %all_gather.11.refs_0_), channel_id=1, source_target_pairs={{0,576},{192,0},{384,192},{576,384},{1,577},{193,1},{385,193},{577... | collective-permute-start | bytes 2654216 | tf_op jit(solution)/shard_map/ppermute | solution.py:182
  68.6 14.9 %collective-permute-done.2.refs_2_ = bf16[384,1152]{1,0:T(8,128)(2,1)S(1)} collective-permute-done((bf16[384,1152]{1,0:T(8,128)(2,1)S(1)}, bf16[384,1152]{1,0:T(8,128)(2,1)S(1)}, u32[]{:S(2)}, u32[]{:S(2)}) %collective-permute-start.2) | collective-permute-done | bytes 884768 | tf_op jit(solution)/shard_map/ppermute | solution.py:183
  83.5 0.9 slice.8
  84.4 2.9 %collective-permute-start.3 = (bf16[192,1152]{1,0:T(8,128)(2,1)}, bf16[192,1152]{1,0:T(8,128)(2,1)S(1)}, u32[]{:S(2)}, u32[]{:S(2)}) collective-permute-start(bf16[192,1152]{1,0:T(8,128)(2,1)} %slice.8), channel_id=1, source_target_pairs={{0,192},{192,384},{384,576},{576,0},{1,193},{193,385},{385,577},{5... | collective-permute-start | bytes 1327112 | tf_op jit(solution)/shard_map/ppermute | solution.py:184
  87.3 0.0 collective-permute-done.1.refs_1_
  87.3 0.8 slice.9
  88.1 3.6 %collective-permute-start.4 = (bf16[192,1152]{1,0:T(8,128)(2,1)}, bf16[192,1152]{1,0:T(8,128)(2,1)S(1)}, u32[]{:S(2)}, u32[]{:S(2)}) collective-permute-start(bf16[192,1152]{1,0:T(8,128)(2,1)} %slice.9), channel_id=1, source_target_pairs={{0,576},{192,0},{384,192},{576,384},{1,577},{193,1},{385,193},{577... | collective-permute-start | bytes 1327112 | tf_op jit(solution)/shard_map/ppermute | solution.py:185
  91.7 0.0 all-gather.3.cloned.1.call-done
  91.7 0.0 copy-start
  91.7 0.0 copy-start.1
  91.7 3.7 %shard_map.101 = (f32[4,96,256]{2,1,0:T(8,128)S(1)}, f32[4,96,256]{2,1,0:T(8,128)S(1)}, bf16[2,256,1152]{2,1,0:T(8,128)(2,1)S(1)}) custom-call(bf16[8,256,1152]{2,1,0:T(8,128)(2,1)} %bitcast.1, bf16[384,1152]{1,0:T(8,128)(2,1)S(1)} %all_gather.11.refs_0_, bf16[384,1152]{1,0:T(8,128)(2,1)S(1)} %collective-permute-done.1.refs_1_, ...), custom_call_target="tpu_custom_call" | custom-call | flops 679477248 | bytes 6193152 | tf_op jit(solution)/shard_map/pallas_call | solution.py:104
  95.4 0.2 collective-permute-done.3.far0
  95.6 3.0 %collective-permute-done.4.far1 = bf16[192,1152]{1,0:T(8,128)(2,1)S(1)} collective-permute-done((bf16[192,1152]{1,0:T(8,128)(2,1)}, bf16[192,1152]{1,0:T(8,128)(2,1)S(1)}, u32[]{:S(2)}, u32[]{:S(2)}) %collective-permute-start.4) | collective-permute-done | bytes 442400 | tf_op jit(solution)/shard_map/ppermute | solution.py:185
  98.6 0.5 shard_map.102
  99.1 6.9 %collective-permute-start.5 = (f32[4,96,256]{2,1,0:T(8,128)S(1)}, f32[4,96,256]{2,1,0:T(8,128)S(1)}, u32[]{:S(2)}, u32[]{:S(2)}) collective-permute-start(f32[4,96,256]{2,1,0:T(8,128)S(1)} %get-tuple-element.18), channel_id=1, source_target_pairs={{0,1},{1,0},{2,3},{3,2},{4,5},{5,4},{6,7},{7,6},{8,9},{9,8},{10,11... | collective-permute-start | bytes 1179656 | tf_op jit(solution)/shard_map/ppermute | solution.py:188
  106.0 1.3 %collective-permute-done.5.other = f32[4,96,256]{2,1,0:T(8,128)S(1)} collective-permute-done((f32[4,96,256]{2,1,0:T(8,128)S(1)}, f32[4,96,256]{2,1,0:T(8,128)S(1)}, u32[]{:S(2)}, u32[]{:S(2)}) %collective-permute-start.5) | collective-permute-done | bytes 393248 | tf_op jit(solution)/shard_map/ppermute | solution.py:188
  107.3 0.0 copy-done
  107.3 0.0 copy-done.1
  107.3 1.3 %shard_map.103 = f32[4,3]{1,0:T(4,128)} custom-call(s32[1,4]{1,0:T(1,128)S(1)} %copy-done, s32[48]{0:T(128)S(1)} %copy-done.1, f32[4,96,256]{2,1,0:T(8,128)S(1)} %get-tuple-element.17.mine, f32[4,96,256]{2,1,0:T(8,128)S(1)} %collective-permute-done.5.other), custom_call_target="tpu_custom_call" | custom-call | tf_op jit(solution)/shard_map/pallas_call | solution.py:168
Async XLA Ops:
  6.5 85.2 %all-gather.3.cloned.1.call-start = ((), (), s32[]{:S(2)}) async-start(), calls=%async_computation | async-start | bytes 5308416 | tf_op jit(solution)/shard_map/all_gather | solution.py:179
  8.6 1.5 %collective-permute-start = (bf16[32,1152]{1,0:T(8,128)(2,1)}, bf16[32,1152]{1,0:T(8,128)(2,1)S(1)}, u32[]{:S(2)}, u32[]{:S(2)}) collective-permute-start(bf16[32,1152]{1,0:T(8,128)(2,1)} %get-tuple-element.13), channel_id=1, source_target_pairs={{0,0},{16,16},{32,32},{48,48},{64,64},{80,80},{2,96},{18,112},{34,... | collective-permute-start | bytes 221192 | tf_op jit(solution)/shard_map/ppermute | solution.py:180
  58.9 24.7 %collective-permute-start.2 = (bf16[384,1152]{1,0:T(8,128)(2,1)S(1)}, bf16[384,1152]{1,0:T(8,128)(2,1)S(1)}, u32[]{:S(2)}, u32[]{:S(2)}) collective-permute-start(bf16[384,1152]{1,0:T(8,128)(2,1)S(1)} %all_gather.11.refs_0_), channel_id=1, source_target_pairs={{0,192},{192,384},{384,576},{576,0},{1,193},{193,385},{385,577},{5... | collective-permute-start | bytes 2654216 | tf_op jit(solution)/shard_map/ppermute | solution.py:183
  64.8 22.5 %collective-permute-start.1 = (bf16[384,1152]{1,0:T(8,128)(2,1)S(1)}, bf16[384,1152]{1,0:T(8,128)(2,1)S(1)}, u32[]{:S(2)}, u32[]{:S(2)}) collective-permute-start(bf16[384,1152]{1,0:T(8,128)(2,1)S(1)} %all_gather.11.refs_0_), channel_id=1, source_target_pairs={{0,576},{192,0},{384,192},{576,384},{1,577},{193,1},{385,193},{577... | collective-permute-start | bytes 2654216 | tf_op jit(solution)/shard_map/ppermute | solution.py:182
  84.4 11.2 %collective-permute-start.3 = (bf16[192,1152]{1,0:T(8,128)(2,1)}, bf16[192,1152]{1,0:T(8,128)(2,1)S(1)}, u32[]{:S(2)}, u32[]{:S(2)}) collective-permute-start(bf16[192,1152]{1,0:T(8,128)(2,1)} %slice.8), channel_id=1, source_target_pairs={{0,192},{192,384},{384,576},{576,0},{1,193},{193,385},{385,577},{5... | collective-permute-start | bytes 1327112 | tf_op jit(solution)/shard_map/ppermute | solution.py:184
  88.1 10.5 %collective-permute-start.4 = (bf16[192,1152]{1,0:T(8,128)(2,1)}, bf16[192,1152]{1,0:T(8,128)(2,1)S(1)}, u32[]{:S(2)}, u32[]{:S(2)}) collective-permute-start(bf16[192,1152]{1,0:T(8,128)(2,1)} %slice.9), channel_id=1, source_target_pairs={{0,576},{192,0},{384,192},{576,384},{1,577},{193,1},{385,193},{577... | collective-permute-start | bytes 1327112 | tf_op jit(solution)/shard_map/ppermute | solution.py:185
  91.7 15.6 %copy-start = (s32[1,4]{1,0:T(1,128)S(1)}, s32[1,4]{1,0:T(1,128)}, u32[]{:S(2)}) copy-start(s32[1,4]{1,0:T(1,128)} %tl.1) | copy-start | bytes 52
  91.7 15.6 %copy-start.1 = (s32[48]{0:T(128)S(1)}, s32[48]{0:T(128)}, u32[]{:S(2)}) copy-start(s32[48]{0:T(128)} %vl.1) | copy-start | bytes 580
  99.1 8.2 %collective-permute-start.5 = (f32[4,96,256]{2,1,0:T(8,128)S(1)}, f32[4,96,256]{2,1,0:T(8,128)S(1)}, u32[]{:S(2)}, u32[]{:S(2)}) collective-permute-start(f32[4,96,256]{2,1,0:T(8,128)S(1)} %get-tuple-element.18), channel_id=1, source_target_pairs={{0,1},{1,0},{2,3},{3,2},{4,5},{5,4},{6,7},{7,6},{8,9},{9,8},{10,11... | collective-permute-start | bytes 1179656 | tf_op jit(solution)/shard_map/ppermute | solution.py:188
Sparse Core Ops, SparseCore 0:
  9.7 72.3 all-gather.2

commit v11 on v10

--- a/solution.py
+++ b/solution.py
@@ -33,10 +33,15 @@
     return [(i, (i + shift) % size) for i in range(size)]
 
 
-def join_kernel(tx, ta, tq, to, vx, va, vq, vo, train, val):
-    for t, v, (lo, hi) in zip((tx, ta, tq, to), (vx, va, vq, vo), COLS):
-        train[:, lo:hi] = t[...]
-        val[:, lo:hi] = v[0]
+def join_kernel(tx, ta, tq, to, vx, va, vq, vo, train, val, sems):
+    copies = []
+    for i, (t, v, (lo, hi)) in enumerate(zip((tx, ta, tq, to), (vx, va, vq, vo), COLS)):
+        copies.append(pltpu.make_async_copy(t, train.at[:, lo:hi], sems.at[2 * i]))
+        copies.append(pltpu.make_async_copy(v.at[0], val.at[:, lo:hi], sems.at[2 * i + 1]))
+    for c in copies:
+        c.start()
+    for c in copies:
+        c.wait()
 
 
 def join(*arrays):
@@ -46,8 +51,9 @@
             jax.ShapeDtypeStruct((TOK, WIDTH), jnp.bfloat16),
             jax.ShapeDtypeStruct((VLEN, WIDTH), jnp.bfloat16),
         ),
-        in_specs=[VMEM] * 8,
+        in_specs=[ANY] * 8,
         out_specs=(VMEM, VMEM),
+        scratch_shapes=[pltpu.SemaphoreType.DMA((8,))],
         compiler_params=pltpu.CompilerParams(vmem_limit_bytes=60 * MIB),
     )(*arrays)
 

time: 117 us -> 117 us (level)
  no operation moved by 1% of the time
where the time goes in v11:
time: 117 us; the launch traced here: 115 us
  blocking collectives  48.7 us (42%)
  starting transfers between devices  24.6 us (21%)
  waiting for transfers between devices  19.5 us (17%)
  between operations  13.5 us (12%)
  Pallas kernels  7.56 us (6%)
  local copies, waits for them, and re-layouts  1.66 us (1%)
    all_gather x1, blocking collectives, local(): own = lax.all_gather(val, 'z', axis=0, tiled=True)  48.7 us
    ppermute x1, waiting for transfers between devices, local(): left = lax.ppermute(own, 'x', around(NX, 1))  14.9 us
    ppermute x1, starting transfers between devices, local(): other = lax.ppermute(send, 'core', [(0, 1), (1, 0)])  6.85 us
    ppermute x1, starting transfers between devices, local(): left = lax.ppermute(own, 'x', around(NX, 1))  5.93 us
    ppermute x1, starting transfers between devices, local(): right = lax.ppermute(own, 'x', around(NX, -1))  3.8 us
    pallas_call x1, Pallas kernels, near_grams(): pl.pallas_call(near_kernel, out_shape=(PART, PART, jax.ShapeDtypeStruct((...  3.67 us
    ppermute x1, starting transfers between devices, local(): far1 = lax.ppermute(right[ROWS:], 'x', around(NX, -1))  3.57 us
    ppermute x1, waiting for transfers between devices, local(): far1 = lax.ppermute(right[ROWS:], 'x', around(NX, -1))  2.96 us
  transfers between devices with their start and end apart: 7, of which 4 were waited for; matrix products, arithmetic and copies ran while one was open for 1% of the time, Pallas kernels for 3%

profile of v11, /device:TPU:1, one launch (start us, length us, event | category | flops | bytes accessed | tf_op | source)
XLA Modules:
  0.0 115.5 jit_solution(10386411476611023757)
XLA Ops:
  6.5 0.0 all-gather.3.cloned.1.call-start
  6.5 2.1 %shard_map.100 = (bf16[256,1152]{1,0:T(8,128)(2,1)}, bf16[32,1152]{1,0:T(8,128)(2,1)}) custom-call(bf16[256,256]{1,0:T(8,128)(2,1)} %tx.1, bf16[256,256]{1,0:T(8,128)(2,1)} %ta.1, bf16[256,384]{1,0:T(8,128)(2,1)} %tq.1, bf16[256,256]{1,0:T(8,128)(2,1)} %to.1, bf16[1,32,256]{2,1,0:T(8,128)(2,1)} %vx.1, bf16[1,32,256]{2,1,0:T(8,128)(2,1)} %va.1, ...), custom_call_target="tpu_custom_call" | custom-call | tf_op jit(solution)/shard_map/pallas_call | solution.py:48
  8.6 0.0 all-gather.3.cloned.1.call-update
  8.7 1.5 %collective-permute-start = (bf16[32,1152]{1,0:T(8,128)(2,1)}, bf16[32,1152]{1,0:T(8,128)(2,1)S(1)}, u32[]{:S(2)}, u32[]{:S(2)}) collective-permute-start(bf16[32,1152]{1,0:T(8,128)(2,1)} %get-tuple-element.13), channel_id=1, source_target_pairs={{0,0},{16,16},{32,32},{48,48},{64,64},{80,80},{2,96},{18,112},{34,... | collective-permute-start | bytes 221192 | tf_op jit(solution)/shard_map/ppermute | solution.py:186
  10.2 0.0 collective-permute-done
  10.2 48.7 %all_gather.11.refs_0_ = bf16[384,1152]{1,0:T(8,128)(2,1)S(1)} all-gather(bf16[32,1152]{1,0:T(8,128)(2,1)S(1)} %collective-permute-done), channel_id=1, replica_groups=mesh['x'=4,'z'=12,'y'=8,'core'=2] {'z'}, dimensions={0}, use_global_device_ids=true | all-gather | bytes 958464 | tf_op jit(solution)/shard_map/all_gather | solution.py:187
  58.9 5.9 %collective-permute-start.2 = (bf16[384,1152]{1,0:T(8,128)(2,1)S(1)}, bf16[384,1152]{1,0:T(8,128)(2,1)S(1)}, u32[]{:S(2)}, u32[]{:S(2)}) collective-permute-start(bf16[384,1152]{1,0:T(8,128)(2,1)S(1)} %all_gather.11.refs_0_), channel_id=1, source_target_pairs={{0,192},{192,384},{384,576},{576,0},{1,193},{193,385},{385,577},{5... | collective-permute-start | bytes 2654216 | tf_op jit(solution)/shard_map/ppermute | solution.py:189
  64.9 3.8 %collective-permute-start.1 = (bf16[384,1152]{1,0:T(8,128)(2,1)S(1)}, bf16[384,1152]{1,0:T(8,128)(2,1)S(1)}, u32[]{:S(2)}, u32[]{:S(2)}) collective-permute-start(bf16[384,1152]{1,0:T(8,128)(2,1)S(1)} %all_gather.11.refs_0_), channel_id=1, source_target_pairs={{0,576},{192,0},{384,192},{576,384},{1,577},{193,1},{385,193},{577... | collective-permute-start | bytes 2654216 | tf_op jit(solution)/shard_map/ppermute | solution.py:188
  68.7 14.9 %collective-permute-done.2.refs_2_ = bf16[384,1152]{1,0:T(8,128)(2,1)S(1)} collective-permute-done((bf16[384,1152]{1,0:T(8,128)(2,1)S(1)}, bf16[384,1152]{1,0:T(8,128)(2,1)S(1)}, u32[]{:S(2)}, u32[]{:S(2)}) %collective-permute-start.2) | collective-permute-done | bytes 884768 | tf_op jit(solution)/shard_map/ppermute | solution.py:189
  83.6 0.9 slice.8
  84.5 2.9 %collective-permute-start.3 = (bf16[192,1152]{1,0:T(8,128)(2,1)}, bf16[192,1152]{1,0:T(8,128)(2,1)S(1)}, u32[]{:S(2)}, u32[]{:S(2)}) collective-permute-start(bf16[192,1152]{1,0:T(8,128)(2,1)} %slice.8), channel_id=1, source_target_pairs={{0,192},{192,384},{384,576},{576,0},{1,193},{193,385},{385,577},{5... | collective-permute-start | bytes 1327112 | tf_op jit(solution)/shard_map/ppermute | solution.py:190
  87.4 0.0 collective-permute-done.1.refs_1_
  87.4 0.8 slice.9
  88.2 3.6 %collective-permute-start.4 = (bf16[192,1152]{1,0:T(8,128)(2,1)}, bf16[192,1152]{1,0:T(8,128)(2,1)S(1)}, u32[]{:S(2)}, u32[]{:S(2)}) collective-permute-start(bf16[192,1152]{1,0:T(8,128)(2,1)} %slice.9), channel_id=1, source_target_pairs={{0,576},{192,0},{384,192},{576,384},{1,577},{193,1},{385,193},{577... | collective-permute-start | bytes 1327112 | tf_op jit(solution)/shard_map/ppermute | solution.py:191
  91.8 0.0 all-gather.3.cloned.1.call-done
  91.8 0.0 copy-start
  91.8 0.0 copy-start.1
  91.8 3.7 %shard_map.101 = (f32[4,96,256]{2,1,0:T(8,128)S(1)}, f32[4,96,256]{2,1,0:T(8,128)S(1)}, bf16[2,256,1152]{2,1,0:T(8,128)(2,1)S(1)}) custom-call(bf16[8,256,1152]{2,1,0:T(8,128)(2,1)} %bitcast.1, bf16[384,1152]{1,0:T(8,128)(2,1)S(1)} %all_gather.11.refs_0_, bf16[384,1152]{1,0:T(8,128)(2,1)S(1)} %collective-permute-done.1.refs_1_, ...), custom_call_target="tpu_custom_call" | custom-call | flops 679477248 | bytes 6193152 | tf_op jit(solution)/shard_map/pallas_call | solution.py:110
  95.5 0.2 collective-permute-done.3.far0
  95.7 3.0 %collective-permute-done.4.far1 = bf16[192,1152]{1,0:T(8,128)(2,1)S(1)} collective-permute-done((bf16[192,1152]{1,0:T(8,128)(2,1)}, bf16[192,1152]{1,0:T(8,128)(2,1)S(1)}, u32[]{:S(2)}, u32[]{:S(2)}) %collective-permute-start.4) | collective-permute-done | bytes 442400 | tf_op jit(solution)/shard_map/ppermute | solution.py:191
  98.7 0.5 shard_map.102
  99.2 6.9 %collective-permute-start.5 = (f32[4,96,256]{2,1,0:T(8,128)S(1)}, f32[4,96,256]{2,1,0:T(8,128)S(1)}, u32[]{:S(2)}, u32[]{:S(2)}) collective-permute-start(f32[4,96,256]{2,1,0:T(8,128)S(1)} %get-tuple-element.18), channel_id=1, source_target_pairs={{0,1},{1,0},{2,3},{3,2},{4,5},{5,4},{6,7},{7,6},{8,9},{9,8},{10,11... | collective-permute-start | bytes 1179656 | tf_op jit(solution)/shard_map/ppermute | solution.py:194
  106.1 1.3 %collective-permute-done.5.other = f32[4,96,256]{2,1,0:T(8,128)S(1)} collective-permute-done((f32[4,96,256]{2,1,0:T(8,128)S(1)}, f32[4,96,256]{2,1,0:T(8,128)S(1)}, u32[]{:S(2)}, u32[]{:S(2)}) %collective-permute-start.5) | collective-permute-done | bytes 393248 | tf_op jit(solution)/shard_map/ppermute | solution.py:194
  107.4 0.0 copy-done
  107.4 0.0 copy-done.1
  107.4 1.3 %shard_map.103 = f32[4,3]{1,0:T(4,128)} custom-call(s32[1,4]{1,0:T(1,128)S(1)} %copy-done, s32[48]{0:T(128)S(1)} %copy-done.1, f32[4,96,256]{2,1,0:T(8,128)S(1)} %get-tuple-element.17.mine, f32[4,96,256]{2,1,0:T(8,128)S(1)} %collective-permute-done.5.other), custom_call_target="tpu_custom_call" | custom-call | tf_op jit(solution)/shard_map/pallas_call | solution.py:174
Async XLA Ops:
  6.5 85.2 %all-gather.3.cloned.1.call-start = ((), (), s32[]{:S(2)}) async-start(), calls=%async_computation | async-start | bytes 5308416 | tf_op jit(solution)/shard_map/all_gather | solution.py:185
  8.7 1.5 %collective-permute-start = (bf16[32,1152]{1,0:T(8,128)(2,1)}, bf16[32,1152]{1,0:T(8,128)(2,1)S(1)}, u32[]{:S(2)}, u32[]{:S(2)}) collective-permute-start(bf16[32,1152]{1,0:T(8,128)(2,1)} %get-tuple-element.13), channel_id=1, source_target_pairs={{0,0},{16,16},{32,32},{48,48},{64,64},{80,80},{2,96},{18,112},{34,... | collective-permute-start | bytes 221192 | tf_op jit(solution)/shard_map/ppermute | solution.py:186
  58.9 24.7 %collective-permute-start.2 = (bf16[384,1152]{1,0:T(8,128)(2,1)S(1)}, bf16[384,1152]{1,0:T(8,128)(2,1)S(1)}, u32[]{:S(2)}, u32[]{:S(2)}) collective-permute-start(bf16[384,1152]{1,0:T(8,128)(2,1)S(1)} %all_gather.11.refs_0_), channel_id=1, source_target_pairs={{0,192},{192,384},{384,576},{576,0},{1,193},{193,385},{385,577},{5... | collective-permute-start | bytes 2654216 | tf_op jit(solution)/shard_map/ppermute | solution.py:189
  64.9 22.5 %collective-permute-start.1 = (bf16[384,1152]{1,0:T(8,128)(2,1)S(1)}, bf16[384,1152]{1,0:T(8,128)(2,1)S(1)}, u32[]{:S(2)}, u32[]{:S(2)}) collective-permute-start(bf16[384,1152]{1,0:T(8,128)(2,1)S(1)} %all_gather.11.refs_0_), channel_id=1, source_target_pairs={{0,576},{192,0},{384,192},{576,384},{1,577},{193,1},{385,193},{577... | collective-permute-start | bytes 2654216 | tf_op jit(solution)/shard_map/ppermute | solution.py:188
  84.5 11.2 %collective-permute-start.3 = (bf16[192,1152]{1,0:T(8,128)(2,1)}, bf16[192,1152]{1,0:T(8,128)(2,1)S(1)}, u32[]{:S(2)}, u32[]{:S(2)}) collective-permute-start(bf16[192,1152]{1,0:T(8,128)(2,1)} %slice.8), channel_id=1, source_target_pairs={{0,192},{192,384},{384,576},{576,0},{1,193},{193,385},{385,577},{5... | collective-permute-start | bytes 1327112 | tf_op jit(solution)/shard_map/ppermute | solution.py:190
  88.2 10.5 %collective-permute-start.4 = (bf16[192,1152]{1,0:T(8,128)(2,1)}, bf16[192,1152]{1,0:T(8,128)(2,1)S(1)}, u32[]{:S(2)}, u32[]{:S(2)}) collective-permute-start(bf16[192,1152]{1,0:T(8,128)(2,1)} %slice.9), channel_id=1, source_target_pairs={{0,576},{192,0},{384,192},{576,384},{1,577},{193,1},{385,193},{577... | collective-permute-start | bytes 1327112 | tf_op jit(solution)/shard_map/ppermute | solution.py:191
  91.8 15.6 %copy-start = (s32[1,4]{1,0:T(1,128)S(1)}, s32[1,4]{1,0:T(1,128)}, u32[]{:S(2)}) copy-start(s32[1,4]{1,0:T(1,128)} %tl.1) | copy-start | bytes 52
  91.8 15.6 %copy-start.1 = (s32[48]{0:T(128)S(1)}, s32[48]{0:T(128)}, u32[]{:S(2)}) copy-start(s32[48]{0:T(128)} %vl.1) | copy-start | bytes 580
  99.2 8.2 %collective-permute-start.5 = (f32[4,96,256]{2,1,0:T(8,128)S(1)}, f32[4,96,256]{2,1,0:T(8,128)S(1)}, u32[]{:S(2)}, u32[]{:S(2)}) collective-permute-start(f32[4,96,256]{2,1,0:T(8,128)S(1)} %get-tuple-element.18), channel_id=1, source_target_pairs={{0,1},{1,0},{2,3},{3,2},{4,5},{5,4},{6,7},{7,6},{8,9},{9,8},{10,11... | collective-permute-start | bytes 1179656 | tf_op jit(solution)/shard_map/ppermute | solution.py:194
Sparse Core Ops, SparseCore 0:
  9.7 72.3 all-gather.2
